TPU v7x, 32 devices: a whole 2x2x4 slice. The times are simulated.
32 devices in a mesh: blk: 16 (over z, y, core), rep: 2 (over x).
Axes of the slice: x: 2, y: 2, z: 4, core: 2. Of those that a mesh axis runs over, the one named last changes fastest.
Arguments:
- query_ids: int32 [2, 32, 128], P('rep', 'blk'), may hold values from 0 to 30591
- passage_ids: int32 [2, 32, 512], P('rep', 'blk'), may hold values from 0 to 30591
- query_lengths: int32 [2, 32], P('rep', 'blk'), may hold values from 32 to 128, as said below
- passage_lengths: int32 [2, 32], P('rep', 'blk'), may hold values from 64 to 512, as said below
- positive: int32 [2, 32], P('rep', 'blk'), may hold values from -1 to 31, as said below
- prefix_lengths: int32 [6], replicated, may hold values from 8 to 256, as said below
- prefix_weights: float32 [6], replicated, may hold values from 0.5 to 2
- owners: int32 [269], replicated, may hold values from 0 to 271, as said below
- weights: float32 [272, 128, 256], P('blk'), may hold values from -0.375 to 0.375
- first_moments: float32 [272, 128, 256], P('blk'), may hold values from -5.722046e-06 to 5.722046e-06
- second_moments: float32 [272, 128, 256], P('blk'), may hold values from 1.1344825e-14 to 4.53793e-14
- vectors: float32 [16, 256], replicated, may hold values from -0.5 to 1.5
- vector_first: float32 [16, 256], replicated, may hold values from -1.9073486e-05 to 1.9073486e-05
- vector_second: float32 [16, 256], replicated, may hold values from 1.4935193e-12 to 4.7792617e-11
Outputs:
- new_weights: float32 [272, 128, 256], P('blk')
- new_first: float32 [272, 128, 256], P('blk')
- new_second: float32 [272, 128, 256], P('blk')
- new_vectors: float32 [16, 256], replicated
- new_vector_first: float32 [16, 256], replicated
- new_vector_second: float32 [16, 256], replicated
- loss_sum: float32 [], replicated
- valid_count: float32 [], replicated
- clip_norm: float32 [], replicated
Inputs may be any that keep to these rules, and one draw needn't show every extreme that they name: `query_lengths`: at least 32; each rep group has a query of length 128. `passage_lengths`: at least 64; each rep group has a passage of length 512. `positive`: indices within a rep group are distinct; the last query of each group counts. `prefix_lengths`: rising multiples of 8, the last equal to 256. `owners`: distinct slots; slot s lies on index s // 17 of blk; some index of blk holds 17 blocks.
All inputs are finite; a program needn't handle non-finite values.
Results may differ from a plain program's by a relative error of at most 0.029.
Values may be sent and summed in bfloat16 or wider, within the bound.
No kernel may reach another device: no remote copies, remote signals or barrier semaphores. Data moves between devices by JAX's collectives and lax.ppermute only.
A program may use at most 320 MiB of HBM per device.

v0:
```python
from functools import partial

import jax
import jax.numpy as jnp
from jax import lax
from jax.sharding import PartitionSpec as P

D = 256
HEADS = 4
FF = 1024
VOCAB = 30592
LAYERS = 1
PLEN = 512
STEP = 7


TEMPER = 8.0
CLIP_AT = 0.01
RATE = 0.06
VECTOR_RATE = 0.8
BETA_ONE = 0.9
BETA_TWO = 0.999
DECAY = 0.01
EPSILON = 1e-08
NORM_EPS = 1e-06
HUGE = 1000000000.0
HIGHEST = lax.Precision.HIGHEST


def mult(left_op, right_op):
    return jnp.dot(left_op, right_op, preferred_element_type=jnp.float32)


def mult_tn(left_op, right_op):
    return lax.dot_general(
        left_op, right_op, (((0,), (0,)), ((), ())), preferred_element_type=jnp.float32
    )


def mult_nt(left_op, right_op):
    return lax.dot_general(
        left_op, right_op, (((1,), (1,)), ((), ())), preferred_element_type=jnp.float32
    )


def norm_rows(values_in, gain_row, shift_row):
    centred = values_in - jnp.mean(values_in, -1, keepdims=True)
    inv_scale = lax.rsqrt(jnp.mean(centred * centred, -1, keepdims=True) + NORM_EPS)
    normed = centred * inv_scale
    return (normed * gain_row + shift_row, normed, inv_scale)


def norm_back(incoming, normed, inv_scale, gain_row):
    dnormed = incoming * gain_row
    inner_part = (
        dnormed
        - jnp.mean(dnormed, -1, keepdims=True)
        - normed * jnp.mean(dnormed * normed, -1, keepdims=True)
    )
    return (inner_part * inv_scale, jnp.sum(incoming * normed, 0), jnp.sum(incoming, 0))


def layer_parts(flat_rows, vectors, layer_index):
    offset = VOCAB + PLEN + D + layer_index * (4 * D + 2 * FF)
    w_qkv = jnp.concatenate(
        [
            flat_rows[offset : offset + D],
            flat_rows[offset + D : offset + 2 * D],
            flat_rows[offset + 2 * D : offset + 3 * D],
        ],
        1,
    )
    w_out = flat_rows[offset + 3 * D : offset + 4 * D]
    w_up = flat_rows[offset + 4 * D : offset + 4 * D + FF]
    w_down = flat_rows[offset + 4 * D + FF : offset + 4 * D + 2 * FF]
    row_base = 4 + layer_index * (8 + FF // D)
    return ((w_qkv, w_out, w_up, w_down), vectors[row_base : row_base + 8 + FF // D])


def divide_into_heads(packed_buffer, column):
    return packed_buffer[:, column * D : (column + 1) * D].reshape(
        packed_buffer.shape[0], HEADS, D // HEADS
    )


def attend_probs(packed_buffer, key_keep):
    scores = jnp.einsum(
        "cnp,fnp->ncf",
        divide_into_heads(packed_buffer, 0),
        divide_into_heads(packed_buffer, 1),
        preferred_element_type=jnp.float32,
    ) * (D // HEADS) ** (-0.5)
    scores = jnp.where(key_keep[None, None, :], scores, -HUGE)
    return jax.nn.softmax(scores, -1)


def attend(pieces):
    packed_buffer, key_keep = pieces
    attn_probs = attend_probs(packed_buffer, key_keep)
    blended = jnp.einsum(
        "nbi,ins->bns",
        attn_probs.astype(jnp.bfloat16),
        divide_into_heads(packed_buffer, 2),
        preferred_element_type=jnp.float32,
    )
    return blended.reshape(packed_buffer.shape[0], D)


def attend_back(pieces):
    packed_buffer, key_keep, grad_out = pieces
    seq_len = packed_buffer.shape[0]
    head_scale = (D // HEADS) ** (-0.5)
    attn_probs = attend_probs(packed_buffer, key_keep)
    gradient_row_block = grad_out.reshape(seq_len, HEADS, D // HEADS)
    grad_values = jnp.einsum(
        "fxn,xfa->nfa",
        attn_probs.astype(jnp.bfloat16),
        gradient_row_block,
        preferred_element_type=jnp.float32,
    )
    grad_probs = jnp.einsum(
        "cnp,fnp->ncf",
        gradient_row_block,
        divide_into_heads(packed_buffer, 2),
        preferred_element_type=jnp.float32,
    )
    grad_scores = attn_probs * (grad_probs - jnp.sum(grad_probs * attn_probs, -1, keepdims=True))
    score_lowered = grad_scores.astype(jnp.bfloat16)
    grad_queries = (
        jnp.einsum(
            "nbi,ins->bns",
            score_lowered,
            divide_into_heads(packed_buffer, 1),
            preferred_element_type=jnp.float32,
        )
        * head_scale
    )
    grad_keys = (
        jnp.einsum(
            "fxn,xfa->nfa",
            score_lowered,
            divide_into_heads(packed_buffer, 0),
            preferred_element_type=jnp.float32,
        )
        * head_scale
    )
    return jnp.concatenate(
        [
            grad_queries.reshape(seq_len, D),
            grad_keys.reshape(seq_len, D),
            grad_values.reshape(seq_len, D),
        ],
        1,
    ).astype(jnp.bfloat16)


def layer_forward(hidden_in, weights_set, vec_rows, key_keep):
    w_qkv, w_out, w_up, w_down = weights_set
    groups, seq_len = key_keep.shape
    in_low = hidden_in.astype(jnp.bfloat16)
    bias_qkv = jnp.concatenate([vec_rows[0], jnp.zeros_like(vec_rows[0]), vec_rows[1]])
    packed_buffer = (mult(in_low, w_qkv) + bias_qkv).astype(jnp.bfloat16)
    blended = lax.map(attend, (packed_buffer.reshape(groups, seq_len, 3 * D), key_keep))
    blend_low = blended.reshape(groups * seq_len, D).astype(jnp.bfloat16)
    summed = hidden_in + mult(blend_low, w_out) + vec_rows[2]
    normal_one, normed_one, scale_one = norm_rows(summed, vec_rows[4], vec_rows[5])
    normal_low = normal_one.astype(jnp.bfloat16)
    up_in = mult_nt(normal_low, w_up) + vec_rows[8:].reshape(FF)
    acted = jax.nn.gelu(up_in, approximate=False).astype(jnp.bfloat16)
    second = normal_one + mult(acted, w_down) + vec_rows[3]
    result, normed_two, scale_two = norm_rows(second, vec_rows[6], vec_rows[7])
    return (
        result,
        (
            in_low,
            packed_buffer,
            blend_low,
            normed_one,
            scale_one,
            normal_low,
            up_in,
            acted,
            normed_two,
            scale_two,
        ),
    )


def layer_backward(grad_out, weights_set, vec_rows, key_keep, saved):
    w_qkv, w_out, w_up, w_down = weights_set
    (
        in_low,
        packed_buffer,
        blend_low,
        normed_one,
        scale_one,
        normal_low,
        up_in,
        acted,
        normed_two,
        scale_two,
    ) = saved
    groups, seq_len = key_keep.shape
    grad_second, grad_gain_two, grad_shift_two = norm_back(
        grad_out, normed_two, scale_two, vec_rows[6]
    )
    down_low = grad_second.astype(jnp.bfloat16)
    grad_down = mult_tn(acted, down_low)
    grad_acted = mult_nt(down_low, w_down)
    gelu_pull = jax.vjp(partial(jax.nn.gelu, approximate=False), up_in)[1]
    up_low = gelu_pull(grad_acted)[0].astype(jnp.bfloat16)
    grad_up = mult_tn(up_low, normal_low)
    grad_normal = grad_second + mult(up_low, w_up)
    grad_summed, gradient_first_gain, grad_shift_one = norm_back(
        grad_normal, normed_one, scale_one, vec_rows[4]
    )
    branch_low = grad_summed.astype(jnp.bfloat16)
    grad_wout = mult_tn(blend_low, branch_low)
    blend_grad = mult_nt(branch_low, w_out).astype(jnp.bfloat16)
    grad_packed = lax.map(
        attend_back,
        (
            packed_buffer.reshape(groups, seq_len, 3 * D),
            key_keep,
            blend_grad.reshape(groups, seq_len, D),
        ),
    ).reshape(groups * seq_len, 3 * D)
    grad_wqkv = mult_tn(in_low, grad_packed)
    grad_in = grad_summed + mult_nt(grad_packed, w_qkv)
    packed_sum = jnp.sum(grad_packed.astype(jnp.float32), 0)
    matrix_grads = jnp.concatenate(
        [
            grad_wqkv[:, :D],
            grad_wqkv[:, D : 2 * D],
            grad_wqkv[:, 2 * D :],
            grad_wout,
            grad_up,
            grad_down,
        ],
        0,
    )
    vector_grads = jnp.concatenate(
        [
            jnp.stack(
                [
                    packed_sum[:D],
                    packed_sum[2 * D :],
                    jnp.sum(branch_low.astype(jnp.float32), 0),
                    jnp.sum(down_low.astype(jnp.float32), 0),
                    gradient_first_gain,
                    grad_shift_one,
                    grad_gain_two,
                    grad_shift_two,
                ]
            ),
            jnp.sum(up_low.astype(jnp.float32), 0).reshape(FF // D, D),
        ],
        0,
    )
    return (grad_in, matrix_grads, vector_grads)


def embed_sequences(flat_rows, vectors, token_ids, lengths):
    groups, seq_len = token_ids.shape
    key_keep = jnp.arange(seq_len)[None, :] < lengths[:, None]
    table_rows = jnp.take(flat_rows, token_ids.reshape(-1), axis=0).astype(jnp.float32)
    places = flat_rows[VOCAB : VOCAB + seq_len].astype(jnp.float32)
    embedded = (table_rows.reshape(groups, seq_len, D) + places[None] + vectors[0]).reshape(
        groups * seq_len, D
    )
    hidden_now, normed_emb, scaled_embedding = norm_rows(embedded, vectors[1], vectors[2])
    weights_set, vec_rows = layer_parts(flat_rows, vectors, 0)
    hidden_now, saved = layer_forward(hidden_now, weights_set, vec_rows, key_keep)
    layer_saves = [saved]
    first_rows = hidden_now.reshape(groups, seq_len, D)[:, 0].astype(jnp.bfloat16)
    pooled = jnp.tanh(mult(first_rows, flat_rows[VOCAB + PLEN : VOCAB + PLEN + D]) + vectors[3])
    return (pooled, (normed_emb, scaled_embedding, layer_saves, first_rows))


def encode_back(grad_pooled, pooled, flat_rows, vectors, token_ids, lengths, encoder_kept):
    normed_emb, scaled_embedding, layer_saves, first_rows = encoder_kept
    groups, seq_len = token_ids.shape
    key_keep = jnp.arange(seq_len)[None, :] < lengths[:, None]
    w_pool = flat_rows[VOCAB + PLEN : VOCAB + PLEN + D].astype(jnp.float32)
    grad_pre = grad_pooled * (1.0 - pooled * pooled)
    grad_pool = jnp.dot(first_rows.astype(jnp.float32).T, grad_pre, precision=HIGHEST)
    grad_first = jnp.dot(grad_pre, w_pool.T, precision=HIGHEST)
    grad_hidden = (
        jnp.zeros((groups, seq_len, D), jnp.float32)
        .at[:, 0]
        .set(grad_first)
        .reshape(groups * seq_len, D)
    )
    matrices = []
    vector_parts = []
    for layer_index in reversed(range(LAYERS)):
        weights_set, vec_rows = layer_parts(flat_rows, vectors, layer_index)
        grad_hidden, matrix_grads, vector_grads = layer_backward(
            grad_hidden, weights_set, vec_rows, key_keep, layer_saves[layer_index]
        )
        matrices.insert(0, matrix_grads)
        vector_parts.insert(0, vector_grads)
    grad_embed, grad_gain, grad_shift = norm_back(
        grad_hidden, normed_emb, scaled_embedding, vectors[1]
    )
    grad_table = jnp.zeros((VOCAB, D), jnp.float32).at[token_ids.reshape(-1)].add(grad_embed)
    grad_places = (
        jnp.zeros((PLEN, D), jnp.float32)
        .at[:seq_len]
        .set(jnp.sum(grad_embed.reshape(groups, seq_len, D), 0))
    )
    flat_grad = jnp.concatenate([grad_table, grad_places, grad_pool] + matrices, 0)
    head_rows = jnp.stack([jnp.sum(grad_embed, 0), grad_gain, grad_shift, jnp.sum(grad_pre, 0)])
    return (flat_grad, jnp.concatenate([head_rows] + vector_parts, 0))


def adam_step(weight, moment_one, moment_two, gradient, step_rate, decay_rate):
    moment_one = BETA_ONE * moment_one + (1.0 - BETA_ONE) * gradient
    moment_two = BETA_TWO * moment_two + (1.0 - BETA_TWO) * gradient * gradient
    update = (
        moment_one
        / (1.0 - BETA_ONE**STEP)
        / (jnp.sqrt(moment_two / (1.0 - BETA_TWO**STEP)) + EPSILON)
    )
    return (weight - step_rate * (update + decay_rate * weight), moment_one, moment_two)


def local(
    query_ids,
    passage_ids,
    query_lengths,
    passage_lengths,
    positive,
    prefix_lengths,
    prefix_weights,
    owners,
    weights,
    first_moments,
    second_moments,
    vectors,
    vector_first,
    vector_second,
):
    slot_count, unit_rows = (weights.shape[0], weights.shape[1])
    gathered = lax.all_gather(weights.astype(jnp.bfloat16), "blk", axis=0, tiled=True)
    flat_rows = jnp.take(gathered, owners, axis=0).reshape(-1, D)
    query_pooled, query_kept = embed_sequences(flat_rows, vectors, query_ids[0], query_lengths[0])
    passage_pooled, passage_kept = embed_sequences(
        flat_rows, vectors, passage_ids[0], passage_lengths[0]
    )
    all_passages = lax.all_gather(passage_pooled.astype(jnp.bfloat16), "blk", axis=0, tiled=True)
    prefix_masks = (jnp.arange(D)[None, :] < prefix_lengths[:, None]).astype(jnp.float32)
    prefix_scale = TEMPER * lax.rsqrt(prefix_lengths.astype(jnp.float32))
    queries = query_pooled.astype(jnp.bfloat16).astype(jnp.float32)
    passages = all_passages.astype(jnp.float32)
    masked = queries[None] * prefix_masks[:, None, :]
    logits = (
        jnp.einsum("mpd,jd->mpj", masked, passages, precision=HIGHEST) * prefix_scale[:, None, None]
    )
    counted = positive[0] >= 0
    target = (jnp.arange(passages.shape[0])[None, :] == positive[0][:, None]).astype(jnp.float32)
    running_totals = jax.nn.logsumexp(logits, -1) - jnp.sum(logits * target[None], -1)
    per_query = jnp.sum(prefix_weights[:, None] * running_totals, 0)
    loss_part = jnp.sum(jnp.where(counted, per_query, 0.0))
    count_part = jnp.sum(counted.astype(jnp.float32))
    count_total, loss_total = lax.psum((count_part, loss_part), ("blk", "rep"))
    row_factor = (prefix_weights * prefix_scale / count_total)[:, None, None] * counted.astype(
        jnp.float32
    )[None, :, None]
    grad_logits = (jax.nn.softmax(logits, -1) - target[None]) * row_factor
    grad_query = jnp.sum(
        jnp.einsum("mpj,jd->mpd", grad_logits, passages, precision=HIGHEST)
        * prefix_masks[:, None, :],
        0,
    )
    grad_passage = lax.psum_scatter(
        jnp.einsum("mpj,mpd->jd", grad_logits, masked, precision=HIGHEST),
        "blk",
        scatter_dimension=0,
        tiled=True,
    )
    flat_query, vec_query = encode_back(
        grad_query, query_pooled, flat_rows, vectors, query_ids[0], query_lengths[0], query_kept
    )
    flat_pass, vec_pass = encode_back(
        grad_passage,
        passage_pooled,
        flat_rows,
        vectors,
        passage_ids[0],
        passage_lengths[0],
        passage_kept,
    )
    vec_total = lax.psum(vec_query + vec_pass, ("blk", "rep"))
    buffer = (
        jnp.zeros((lax.axis_size("blk") * slot_count, unit_rows, D), jnp.float32)
        .at[owners]
        .set((flat_query + flat_pass).reshape(-1, unit_rows, D))
    )
    vec_square = jnp.sum(vec_total * vec_total)
    reduced = lax.psum_scatter(buffer, "blk", scatter_dimension=0, tiled=True)
    reduced = lax.psum(reduced, "rep")
    square_sum = lax.psum(jnp.sum(reduced * reduced), "blk")
    old_weight, old_first, old_second = (weights, first_moments, second_moments)
    slot_ids = lax.axis_index("blk") * slot_count + jnp.arange(slot_count)
    owned_mask = jnp.any(slot_ids[:, None] == owners[None, :], 1)[:, None, None]
    grad_norm = jnp.sqrt(square_sum + vec_square)
    factor = CLIP_AT / jnp.maximum(grad_norm, CLIP_AT)
    new_weight, new_first, new_second = adam_step(
        old_weight, old_first, old_second, reduced * factor, RATE, DECAY
    )
    new_weight = jnp.where(owned_mask, new_weight, old_weight)
    new_first = jnp.where(owned_mask, new_first, old_first)
    new_second = jnp.where(owned_mask, new_second, old_second)
    new_vec, new_vec_first, new_vec_second = adam_step(
        vectors, vector_first, vector_second, vec_total * factor, VECTOR_RATE, 0.0
    )
    return (
        new_weight,
        new_first,
        new_second,
        new_vec,
        new_vec_first,
        new_vec_second,
        loss_total,
        count_total,
        grad_norm,
    )


def solution(mesh):
    in_specs = (
        P("rep", "blk", None),
        P("rep", "blk", None),
        P("rep", "blk"),
        P("rep", "blk"),
        P("rep", "blk"),
        P(),
        P(),
        P(),
        P("blk", None, None),
        P("blk", None, None),
        P("blk", None, None),
        P(),
        P(),
        P(),
    )
    out_specs = (
        P("blk", None, None),
        P("blk", None, None),
        P("blk", None, None),
        P(),
        P(),
        P(),
        P(),
        P(),
        P(),
    )
    return jax.shard_map(local, mesh=mesh, in_specs=in_specs, out_specs=out_specs, check_vma=False)
```

profile of v0, /device:TPU:0, one launch (start us, length us, event | category | flops | bytes accessed | tf_op | source)
XLA Modules:
  0.0 1120.6 jit_solution(5132912848576741451)
XLA Ops:
  16.7 90.4 %all-gather.3.cloned.1.call-done = bf16[272,128,256]{2,1,0:T(8,128)(2,1)} async-done(((bf16[17,128,256]{2,1,0:T(8,128)(2,1)}), bf16[272,128,256]{2,1,0:T(8,128)(2,1)}) %all-gather.3.cloned.1.call-update) | async-done | bytes 17825808 | tf_op jit(solution)/shard_map/all_gather | solution.py:345
  107.0 16.4 %gather_fusion = bf16[269,128,256]{2,1,0:T(8,128)(2,1)} fusion(bf16[272,128,256]{2,1,0:T(8,128)(2,1)} %all-gather.3.cloned.1.call-done, s32[1024]{0:T(1024)S(1)} %get-tuple-element.442), kind=kCustom, calls=%fused_computation | custom fusion | bytes 35259444 | tf_op jit(solution)/shard_map/jit(_take)/gather | solution.py:346
  123.5 10.5 broadcast_select_fusion
  134.9 18.7 %bitcast_select_fusion = bf16[34432,256]{1,0:T(8,128)(2,1)} fusion(bf16[269,128,256]{2,1,0:T(8,128)(2,1)S(1)} %copy-done, pred[34432]{0:T(1024)(128)(4,1)S(1)} %broadcast_bitcast_fusion), kind=kLoop, calls=%fused_computation.79 | loop fusion | flops 8814592 | bytes 35292800 | tf_op jit(solution)/shard_map/jit(_take)/select_n | solution.py:346
  153.6 9.2 gather_fusion.1
  167.7 3.7 multiply_convert_fusion.3
  172.8 12.1 %gather_fusion.2 = bf16[1024,256]{1,0:T(8,128)(2,1)S(1)} fusion(bf16[34432,256]{1,0:T(8,128)(2,1)} %bitcast_select_fusion, s32[1024]{0:T(1024)S(1)} %broadcast_clamp_fusion), kind=kCustom, calls=%fused_computation.2 | custom fusion | bytes 1052672 | tf_op jit(solution)/shard_map/jit(_take)/gather | solution.py:266
  190.0 18.0 %while.46 = (s32[]{:T(128)}, bf16[2,512,256]{2,1,0:T(8,128)(2,1)}, bf16[2,512,768]{1,2,0:T(8,128)(2,1)S(1)}, pred[2,512]{1,0:T(4,128)(4,1)S(1)}, s32[]{:T(128)}) while((s32[]{:T(128)}, bf16[2,512,256]{2,1,0:T(8,128)(2,1)}, bf16[2,512,768]{1,2,0:T(8,128)(2,1)S(1)}, pred[2,512]{1,0:T(4,128)(4,1)S(1)}, s32[]{:T(128)}) %tuple.207), condition=%wide.region_16.17_spmd, body=%wide.region_13.16_spmd.sunk | while | flops 274727424 | bytes 13649989 | solution.py:163
  190.6 4.8 fusion.299
  199.6 4.8 fusion.299
  210.0 12.4 %multiply_convert_fusion.2 = (bf16[1024,1024]{1,0:T(8,128)(2,1)S(1)}, f32[1024,1024]{1,0:T(8,128)}, f32[1024,1024]{1,0:T(8,128)}) fusion(f32[1024]{0:T(1024)} %bitcast.593, bf16[1024,256]{1,0:T(8,128)(2,1)} %bitcast.492, f32[1024,256]{1,0:T(8,128)S(1)} %get-tuple-element.420, f32[256]{0:T(256)} %bitcast.560, f32[256]{0:T(256)S(1)} %bitcast.539, ...), kind=kOutput, calls=%fused_computation.89 | convolution fusion | flops 607387648 | bytes 12072960 | tf_op jit(solution)/shard_map/dot_general | solution.py:41
  224.7 20.4 %all-gather = bf16[16,2,256]{2,1,0:T(2,128)(2,1)S(1)} all-gather(bf16[1,2,256]{2,1,0:T(2,128)(2,1)S(1)} %convert_bitcast_fusion), channel_id=1, replica_groups=mesh['blk'=16,'rep'=2] {'blk'}, dimensions={0}, use_global_device_ids=true | all-gather | bytes 17408 | tf_op jit(solution)/shard_map/all_gather | solution.py:351
  246.3 37.1 %psum.35 = f32[]{:T(128)} all-reduce(f32[]{:T(128)} %get-tuple-element.303), channel_id=1, replica_groups=mesh['blk'=16,'rep'=2] {'blk','rep'}, use_global_device_ids=true, to_apply=%region_24.25 | all-reduce | flops 1 | bytes 8 | tf_op jit(solution)/shard_map/psum | solution.py:366
  285.0 60.9 %all-reduce.3 = f32[32,256]{1,0:T(8,128)S(1)} all-reduce(f32[32,256]{1,0:T(8,128)S(1)} %convolution_bitcast_fusion.2), channel_id=2, replica_groups=mesh['blk'=16,'rep'=2] {'blk'}, use_global_device_ids=true, to_apply=%region_39.40.clone | all-reduce | flops 8192 | bytes 65536
  358.1 5.8 convert_reduce_fusion
  368.0 27.9 %while.48 = (s32[]{:T(128)}, bf16[2,512,768]{1,2,0:T(8,128)(2,1)}, bf16[2,512,768]{1,2,0:T(8,128)(2,1)S(1)}, pred[2,512]{1,0:T(4,128)(4,1)S(1)}, bf16[2,512,256]{2,1,0:T(8,128)(2,1)}, /*index=5*/s32[]{:T(128)}) while((s32[]{:T(128)}, bf16[2,512,768]{1,2,0:T(8,128)(2,1)}, bf16[2,512,768]{1,2,0:T(8,128)(2,1)S(1)}, ...), condition=%wide.region_48.49_spmd, body=%wide.region_44.48_spmd.sunk | while | flops 687733248 | bytes 57723016 | solution.py:220
  368.9 3.5 fusion.328
  382.8 3.5 fusion.328
  397.9 3.8 multiply_reduce_fusion.4
  412.4 16.8 %while.47 = (s32[]{:T(128)}, bf16[2,128,768]{1,2,0:T(8,128)(2,1)S(1)}, bf16[2,128,768]{1,2,0:T(8,128)(2,1)S(1)}, pred[2,128]{1,0:T(4,128)(4,1)}, bf16[2,128,256]{2,1,0:T(8,128)(2,1)}, /*index=5*/s32[]{:T(128)}) while((s32[]{:T(128)}, bf16[2,128,768]{1,2,0:T(8,128)(2,1)S(1)}, bf16[2,128,768]{1,2,0:T(8,128)(2,1)S(1)}, ...), condition=%wide.region_34.35_spmd, body=%wide.region_30.34_spmd.sunk | while | flops 52134144 | bytes 3945045 | solution.py:220
  437.2 18.6 %scatter_custom_fusion.1 = f32[30592,256]{1,0:T(8,128)} fusion(s32[1024]{0:T(1024)} %bitcast.587, f32[1024,256]{1,0:T(8,128)S(1)} %get-tuple-element.352, f32[]{:T(128)} %constant.373.clone.1), kind=kCustom, calls=%fused_computation.81 | custom fusion | flops 262144 | bytes 31326720 | tf_op jit(solution)/shard_map/scatter-add | solution.py:306
  455.8 21.5 %constant_dynamic-update-slice_fusion.4 = f32[34432,256]{1,0:T(8,128)} fusion(f32[30592,256]{1,0:T(8,128)} %scatter_custom_fusion.1), kind=kLoop, calls=%fused_computation.274 | loop fusion | bytes 62652416
  491.6 14.6 %scatter_custom_fusion = f32[30592,256]{1,0:T(8,128)} fusion(s32[256]{0:T(256)} %bitcast.603, f32[256,256]{1,0:T(8,128)S(1)} %get-tuple-element.358, f32[]{:T(128)} %constant.373.clone.1), kind=kCustom, calls=%fused_computation.83 | custom fusion | flops 65536 | bytes 31326720 | tf_op jit(solution)/shard_map/scatter-add | solution.py:306
  506.3 21.6 %constant_dynamic-update-slice_fusion.2 = f32[34432,256]{1,0:T(8,128)} fusion(f32[30592,256]{1,0:T(8,128)} %scatter_custom_fusion), kind=kLoop, calls=%fused_computation.272 | loop fusion | bytes 62652416
  536.1 34.9 %add.621 = f32[34432,256]{1,0:T(8,128)} add(f32[34432,256]{1,0:T(8,128)} %convolution_dynamic-update-slice_fusion, f32[34432,256]{1,0:T(8,128)} %convolution_dynamic-update-slice_fusion.2) | non-fusion elementwise | flops 8814592 | bytes 105775104 | tf_op jit(solution)/shard_map/add | solution.py:398
  570.9 11.9 %broadcast_in_dim.211 = f32[272,128,256]{2,1,0:T(8,128)} broadcast(f32[]{:T(128)} %constant.373.clone.1), dimensions={} | broadcast | bytes 35651588 | tf_op jit(solution)/shard_map/broadcast_in_dim | solution.py:396
  582.8 66.7 %scatter_fusion = f32[272,128,256]{2,1,0:T(8,128)} fusion(f32[272,128,256]{2,1,0:T(8,128)} %broadcast_in_dim.211, s32[269]{0:T(512)S(1)} %copy-done.87, f32[269,128,256]{2,1,0:T(8,128)} %bitcast.430), kind=kCustom, calls=%fused_computation.5 | custom fusion | bytes 105776176 | tf_op jit(solution)/shard_map/scatter | solution.py:398
  649.8 347.3 %reduce-scatter.2.cloned.1.call-done = f32[17,128,256]{2,1,0:T(8,128)} async-done(((f32[272,128,256]{2,1,0:T(8,128)}), f32[17,128,256]{2,1,0:T(8,128)}) %reduce-scatter.2.cloned.1.call-update) | async-done | bytes 2228240 | tf_op jit(solution)/shard_map/reduce_scatter | solution.py:401
  999.6 40.0 %all-reduce.4 = (f32[16,256]{1,0:T(8,128)S(1)}, f32[]{:T(128)}) all-reduce(f32[16,256]{1,0:T(8,128)S(1)} %add.623, f32[]{:T(128)} %get-tuple-element.302), channel_id=1, replica_groups=mesh['blk'=16,'rep'=2] {'blk','rep'}, use_global_device_ids=true, to_apply=%region_82.83 | all-reduce | flops 4097 | bytes 32776 | tf_op jit(solution)/shard_map/psum | solution.py:394
  1039.6 25.3 %all-reduce.7.cloned.1.call-done = f32[17,128,256]{2,1,0:T(8,128)} async-done(((f32[17,128,256]{2,1,0:T(8,128)}), f32[17,128,256]{2,1,0:T(8,128)}) %all-reduce.7.cloned.1.call-update) | async-done | bytes 2228240 | tf_op jit(solution)/shard_map/psum | solution.py:402
  1068.3 33.8 %psum.37 = f32[]{:T(128)} all-reduce(f32[]{:T(128)} %multiply_reduce_fusion.2), channel_id=1, replica_groups=mesh['blk'=16,'rep'=2] {'blk'}, use_global_device_ids=true, to_apply=%region_57.58 | all-reduce | flops 1 | bytes 8 | tf_op jit(solution)/shard_map/psum | solution.py:403
  1104.1 8.3 fusion.56
  (578 shorter events, 139.9 us)
Async XLA Ops:
  7.3 99.8 %all-gather.3.cloned.1.call-start = ((), (), s32[]{:S(2)}) async-start(), calls=%async_computation.1 | async-start | bytes 18939904 | tf_op jit(solution)/shard_map/all_gather | solution.py:345
  10.1 987.0 %reduce-scatter.2.cloned.1.call-start = ((), (), s32[]{:S(2)}) async-start(), calls=%async_computation.2 | async-start | bytes 37879808 | tf_op jit(solution)/shard_map/reduce_scatter | solution.py:401
  12.2 173.7 %copy-start.51 = (f32[1,256]{1,0:T(1,128)}, f32[1,256]{1,0:T(1,128)S(1)}, u32[]{:S(2)}) copy-start(f32[1,256]{1,0:T(1,128)S(1)} %get-tuple-element.405) | copy-start | bytes 3076
  12.2 173.7 %copy-start.60 = (f32[1,256]{1,0:T(1,128)}, f32[1,256]{1,0:T(1,128)S(1)}, u32[]{:S(2)}) copy-start(f32[1,256]{1,0:T(1,128)S(1)} %get-tuple-element.404) | copy-start | bytes 3076
  12.2 173.7 %copy-start.90 = (f32[1,256]{1,0:T(1,128)}, f32[1,256]{1,0:T(1,128)S(1)}, u32[]{:S(2)}) copy-start(f32[1,256]{1,0:T(1,128)S(1)} %get-tuple-element.403) | copy-start | bytes 3076
  649.5 347.6 %copy-start.89 = (s32[269]{0:T(512)S(1)}, s32[269]{0:T(512)}, u32[]{:S(2)}) copy-start(s32[269]{0:T(512)} %param.39) | copy-start | bytes 3232
  649.5 347.8 %copy-start.136 = (f32[1024]{0:T(1024)S(1)}, f32[1024]{0:T(1024)}, u32[]{:S(2)}) copy-start(f32[1024]{0:T(1024)} %get-tuple-element.439) | copy-start | bytes 12292
  649.5 347.8 %copy-start.139 = (f32[1024]{0:T(1024)S(1)}, f32[1024]{0:T(1024)}, u32[]{:S(2)}) copy-start(f32[1024]{0:T(1024)} %get-tuple-element.437) | copy-start | bytes 12292
  649.5 349.5 %copy-start.116 = (f32[256]{0:T(256)S(1)}, f32[256]{0:T(256)}, u32[]{:S(2)}) copy-start(f32[256]{0:T(256)} %get-tuple-element.277) | copy-start | bytes 3076
  649.5 349.6 %copy-start.120 = (f32[256]{0:T(256)S(1)}, f32[256]{0:T(256)}, u32[]{:S(2)}) copy-start(f32[256]{0:T(256)} %get-tuple-element.298) | copy-start | bytes 3076
  649.5 349.6 %copy-start.121 = (f32[256]{0:T(256)S(1)}, f32[256]{0:T(256)}, u32[]{:S(2)}) copy-start(f32[256]{0:T(256)} %get-tuple-element.345) | copy-start | bytes 3076
  649.6 349.6 %copy-start.122 = (f32[256]{0:T(256)S(1)}, f32[256]{0:T(256)}, u32[]{:S(2)}) copy-start(f32[256]{0:T(256)} %get-tuple-element.347) | copy-start | bytes 3076
  649.6 349.6 %copy-start.125 = (f32[256]{0:T(256)S(1)}, f32[256]{0:T(256)}, u32[]{:S(2)}) copy-start(f32[256]{0:T(256)} %get-tuple-element.275) | copy-start | bytes 3076
  649.6 349.6 %copy-start.126 = (f32[256]{0:T(256)S(1)}, f32[256]{0:T(256)}, u32[]{:S(2)}) copy-start(f32[256]{0:T(256)} %get-tuple-element.284) | copy-start | bytes 3076
  649.6 349.6 %copy-start.132 = (f32[256]{0:T(256)S(1)}, f32[256]{0:T(256)}, u32[]{:S(2)}) copy-start(f32[256]{0:T(256)} %get-tuple-element.351) | copy-start | bytes 3076
  649.6 349.6 %copy-start.135 = (f32[256]{0:T(256)S(1)}, f32[256]{0:T(256)}, u32[]{:S(2)}) copy-start(f32[256]{0:T(256)} %get-tuple-element.349) | copy-start | bytes 3076
  649.6 349.6 %copy-start.148 = (f32[256]{0:T(256)S(1)}, f32[256]{0:T(256)}, u32[]{:S(2)}) copy-start(f32[256]{0:T(256)} %get-tuple-element.279) | copy-start | bytes 3076
  649.6 349.6 %copy-start.149 = (f32[256]{0:T(256)S(1)}, f32[256]{0:T(256)}, u32[]{:S(2)}) copy-start(f32[256]{0:T(256)} %get-tuple-element.283) | copy-start | bytes 3076
  649.7 349.6 %copy-start.25 = (bf16[2,128,768]{1,2,0:T(8,128)(2,1)S(1)}, bf16[2,128,768]{1,2,0:T(8,128)(2,1)}, u32[]{:S(2)}) copy-start(bf16[2,128,768]{1,2,0:T(8,128)(2,1)} %copy-done.24) | copy-start | bytes 1179652
  649.7 349.8 %copy-start.119 = (f32[256]{0:T(256)S(1)}, f32[256]{0:T(256)}, u32[]{:S(2)}) copy-start(f32[256]{0:T(256)} %get-tuple-element.300) | copy-start | bytes 3076
  649.7 349.8 %copy-start.123 = (f32[256]{0:T(256)S(1)}, f32[256]{0:T(256)}, u32[]{:S(2)}) copy-start(f32[256]{0:T(256)} %get-tuple-element.287) | copy-start | bytes 3076
  649.7 349.8 %copy-start.124 = (f32[256]{0:T(256)S(1)}, f32[256]{0:T(256)}, u32[]{:S(2)}) copy-start(f32[256]{0:T(256)} %get-tuple-element.353) | copy-start | bytes 3076
  649.7 349.8 %copy-start.127 = (f32[256]{0:T(256)S(1)}, f32[256]{0:T(256)}, u32[]{:S(2)}) copy-start(f32[256]{0:T(256)} %get-tuple-element.289) | copy-start | bytes 3076
  649.7 349.8 %copy-start.128 = (f32[256]{0:T(256)S(1)}, f32[256]{0:T(256)}, u32[]{:S(2)}) copy-start(f32[256]{0:T(256)} %get-tuple-element.293) | copy-start | bytes 3076
  649.7 349.8 %copy-start.129 = (f32[256]{0:T(256)S(1)}, f32[256]{0:T(256)}, u32[]{:S(2)}) copy-start(f32[256]{0:T(256)} %get-tuple-element.355) | copy-start | bytes 3076
  649.7 349.8 %copy-start.140 = (f32[256]{0:T(256)S(1)}, f32[256]{0:T(256)}, u32[]{:S(2)}) copy-start(f32[256]{0:T(256)} %get-tuple-element.285) | copy-start | bytes 3076
  649.7 349.8 %copy-start.141 = (f32[256]{0:T(256)S(1)}, f32[256]{0:T(256)}, u32[]{:S(2)}) copy-start(f32[256]{0:T(256)} %get-tuple-element.294) | copy-start | bytes 3076
  649.7 453.7 %copy-start.59 = (f32[16,256]{1,0:T(8,128)S(1)}, f32[16,256]{1,0:T(8,128)}, u32[]{:S(2)}) copy-start(f32[16,256]{1,0:T(8,128)} %param.43) | copy-start | bytes 49156
  649.8 453.7 %copy-start.97 = (f32[16,256]{1,0:T(8,128)S(1)}, f32[16,256]{1,0:T(8,128)}, u32[]{:S(2)}) copy-start(f32[16,256]{1,0:T(8,128)} %param.44) | copy-start | bytes 49156
  649.8 453.7 %copy-start.98 = (f32[16,256]{1,0:T(8,128)S(1)}, f32[16,256]{1,0:T(8,128)}, u32[]{:S(2)}) copy-start(f32[16,256]{1,0:T(8,128)} %param.45) | copy-start | bytes 49156
  649.8 454.3 %copy-start.16 = (f32[17,128,256]{2,1,0:T(8,128)S(1)}, f32[17,128,256]{2,1,0:T(8,128)}, u32[]{:S(2)}) copy-start(f32[17,128,256]{2,1,0:T(8,128)} %param.40) | copy-start | bytes 6684676
  649.8 415.1 %all-reduce.7.cloned.1.call-start = ((), (), s32[]{:S(2)}) async-start(), calls=%async_computation.3 | async-start | bytes 4456448 | tf_op jit(solution)/shard_map/psum | solution.py:402
  (137 other events, 3815.6 us)
Sparse Core Ops, SparseCore 0:
  10.3 96.7 all-gather.2
  649.8 347.2 reduce-scatter.1
  999.5 65.3 all-reduce.6
where the time goes:
time: 1130 us; the launch traced here: 1120 us
  waiting for transfers between devices  463 us (41%)
  local copies, waits for them, and re-layouts  196 us (17%)
  blocking collectives  192 us (17%)
  other arithmetic  149 us (13%)
  matrix products  101 us (9%)
  between operations  19.6 us (2%)
    reduce_scatter x1, waiting for transfers between devices, local(): reduced = lax.psum_scatter(buffer, 'blk', scatter_dimension=0, tiled=True)  347 us
    all_gather x1, waiting for transfers between devices, local(): lax.all_gather(weights.astype(jnp.bfloat16), 'blk', axis=0, tiled=True)  90.4 us
    scatter x1, local copies, waits for them, and re-layouts, local(): buffer = jnp.zeros((lax.axis_size('blk') * slot_count, unit_rows, D), jnp...  66.7 us
    unnamed x1, blocking collectives  60.9 us
    unnamed x345, local copies, waits for them, and re-layouts  53 us
    psum x1, blocking collectives, local(): vec_total = lax.psum(vec_query + vec_pass, ('blk', 'rep'))  40 us
    psum x1, blocking collectives, local(): count_total, loss_total = lax.psum((count_part, loss_part), ('blk', 'rep'))  37.1 us
    add x1, other arithmetic, local(): flat_query + flat_pass  34.9 us
  transfers between devices with their start and end apart: 3, of which 3 were waited for; matrix products, arithmetic and copies ran while one was open for 1% of the time, Pallas kernels for 0%

commit v1 on v0

--- a/solution.py
+++ b/solution.py
@@ -3,6 +3,8 @@
 import jax
 import jax.numpy as jnp
 from jax import lax
+from jax.experimental import pallas as pl
+from jax.experimental.pallas import tpu as pltpu
 from jax.sharding import PartitionSpec as P
 
 D = 256
@@ -428,6 +430,971 @@
     )
 
 
+F32 = jnp.float32
+BF16 = jnp.bfloat16
+I32 = jnp.int32
+UNIT = 128
+TABLE_BLOCKS = VOCAB // UNIT
+PLACE_BLOCKS = PLEN // UNIT
+DENSE = PLACE_BLOCKS + (D + 4 * D + 2 * FF) // UNIT
+HALF = 64
+QROWS = 128
+TOKENS = 2 * QROWS + 2 * PLEN
+STARTS = (0, QROWS, 2 * QROWS, 2 * QROWS + PLEN)
+UNITS_L = 12
+L_ROWS = 4 * UNITS_L
+NEVER = -1e30
+PARAMS = pltpu.CompilerParams(vmem_limit_bytes=56 << 20)
+
+AT_POOL = PLEN
+AT_Q = AT_POOL + D
+AT_K = AT_Q + D
+AT_V = AT_K + D
+AT_O = AT_V + D
+AT_UP = AT_O + D
+AT_DOWN = AT_UP + FF
+
+TAB_PLACE, TAB_OWNER, TAB_UNIT, TAB_SLOT, TAB_KIND, TAB_FLAG = 0, 32, 64, 96, 128, 160
+TAB_SIZE = 256
+
+KIND_TABLE, KIND_PLACE, KIND_DENSE = 1, 2, 8
+
+vmem = pl.BlockSpec(memory_space=pltpu.VMEM)
+smem = pl.BlockSpec(memory_space=pltpu.SMEM)
+hbm = pl.BlockSpec(memory_space=pl.ANY)
+
+
+def iota(shape, axis):
+    return lax.broadcasted_iota(I32, shape, axis)
+
+
+def dot_nn(a, b):
+    return lax.dot_general(a, b, (((1,), (0,)), ((), ())), preferred_element_type=F32)
+
+
+def dot_nt(a, b):
+    return lax.dot_general(a, b, (((1,), (1,)), ((), ())), preferred_element_type=F32)
+
+
+def dot_tn(a, b):
+    return lax.dot_general(a, b, (((0,), (0,)), ((), ())), preferred_element_type=F32)
+
+
+def split(a):
+    high = a.astype(BF16)
+    return high, (a - high.astype(F32)).astype(BF16)
+
+
+def fine(dot, a, b):
+    high, low = split(a)
+    rows = a.shape[0]
+    both = dot(jnp.concatenate([high, low], 0), b)
+    return both[:rows] + both[rows:]
+
+
+def to_column(row):
+    return jnp.broadcast_to(row, (128, 128)).T[:, :1]
+
+
+def token_facts(query_lengths, passage_lengths):
+    lane = iota((1, TOKENS), 1)
+    sequence = (
+        (lane >= STARTS[1]).astype(I32)
+        + (lane >= STARTS[2]).astype(I32)
+        + (lane >= STARTS[3]).astype(I32)
+    )
+    ends = [
+        STARTS[0] + query_lengths[0, 0],
+        STARTS[1] + query_lengths[0, 1],
+        STARTS[2] + passage_lengths[0, 0],
+        STARTS[3] + passage_lengths[0, 1],
+    ]
+    end = jnp.where(
+        sequence == 0,
+        ends[0],
+        jnp.where(sequence == 1, ends[1], jnp.where(sequence == 2, ends[2], ends[3])),
+    )
+    return sequence, lane < end
+
+
+def prepare_kernel(slots, cap, owners, me, weights, dense_out, tab, counts, units, block, sems):
+    n_units = owners.shape[0]
+    n_blk = counts.shape[0]
+
+    def clear(i, c):
+        counts[i] = 0
+        units[i] = 0
+        return c
+
+    lax.fori_loop(0, n_blk, clear, 0)
+
+    def wipe(i, c):
+        tab[i] = 0
+        return c
+
+    lax.fori_loop(0, TAB_SIZE, wipe, 0)
+    mine = me[0]
+    base = n_units - DENSE
+
+    def place(b, c):
+        slot = owners[base + b]
+        owner = slot // slots
+        inside = slot - owner * slots
+        rank = counts[owner]
+        counts[owner] = rank + 1
+        tab[TAB_PLACE + b] = owner * cap + jnp.minimum(rank, cap - 1)
+        tab[TAB_OWNER + b] = owner
+        tab[TAB_SLOT + b] = inside
+        tab[TAB_FLAG] = jnp.maximum(tab[TAB_FLAG], (rank >= cap).astype(I32))
+
+        @pl.when((owner == mine) & (rank < cap))
+        def _():
+            pltpu.make_async_copy(weights.at[inside], block.at[rank], sems.at[rank]).start()
+
+        return c
+
+    lax.fori_loop(0, DENSE, place, 0)
+    have = counts[mine]
+    for c in range(cap):
+
+        @pl.when(c < have)
+        def _():
+            pltpu.make_async_copy(weights.at[0], block.at[c], sems.at[c]).wait()
+            dense_out[c] = block[c].astype(BF16)
+
+        @pl.when(c >= have)
+        def _():
+            dense_out[c] = jnp.zeros((UNIT, D), BF16)
+
+
+def prepare(owners, me, weights, n_blk, cap):
+    slots = weights.shape[0]
+    return pl.pallas_call(
+        partial(prepare_kernel, slots, cap),
+        out_shape=(
+            jax.ShapeDtypeStruct((cap, UNIT, D), BF16),
+            jax.ShapeDtypeStruct((TAB_SIZE,), I32),
+        ),
+        in_specs=[smem, smem, hbm],
+        out_specs=(vmem, smem),
+        scratch_shapes=[
+            pltpu.SMEM((n_blk,), I32),
+            pltpu.SMEM((n_blk,), I32),
+            pltpu.VMEM((cap, UNIT, D), F32),
+            pltpu.SemaphoreType.DMA((cap,)),
+        ],
+        compiler_params=PARAMS,
+        name="prepare",
+    )(owners, me, weights)
+
+
+def request_kernel(
+    slots, n_blk, cap, owners, tab_in, me, positive, query_lengths, passage_lengths, owner_row,
+    query_ids, passage_ids, message, where_row, tab, ids, units,
+):
+    n_rep = 2
+    n_dest = n_blk * n_rep
+    mine = me[0]
+    n_units = owners.shape[0]
+
+    def copy(i, c):
+        tab[i] = tab_in[i]
+        return c
+
+    lax.fori_loop(0, TAB_SIZE, copy, 0)
+
+    def clear(i, c):
+        units[i] = 0
+        return c
+
+    lax.fori_loop(0, n_blk, clear, 0)
+
+    def kind(b, c):
+        inside = owners[b] - mine * slots
+
+        @pl.when((inside >= 0) & (inside < slots))
+        def _():
+            tab[TAB_KIND + inside] = jnp.where(
+                b < TABLE_BLOCKS,
+                KIND_TABLE,
+                jnp.where(
+                    b < TABLE_BLOCKS + PLACE_BLOCKS, KIND_PLACE + b - TABLE_BLOCKS, KIND_DENSE
+                ),
+            )
+
+        return c
+
+    lax.fori_loop(0, n_units, kind, 0)
+    for b in range(PLACE_BLOCKS, DENSE):
+        owner = tab_in[TAB_OWNER + b]
+        used = units[owner]
+        need = 2 if AT_K <= b * UNIT < AT_O else 1
+        units[owner] = used + need
+        tab[TAB_UNIT + b] = jnp.minimum(used, UNITS_L - need)
+        tab[TAB_FLAG] = jnp.maximum(tab[TAB_FLAG], (used + need > UNITS_L).astype(I32))
+
+    ids[:, 0:QROWS] = query_ids[0:1]
+    ids[:, QROWS : 2 * QROWS] = query_ids[1:2]
+    ids[:, STARTS[2] : STARTS[3]] = passage_ids[0:1]
+    ids[:, STARTS[3] :] = passage_ids[1:2]
+    token = ids[...]
+    _, live = token_facts(query_lengths, passage_lengths)
+    lane = iota((1, TOKENS), 1)
+    block = token // UNIT
+    slot = jnp.zeros((1, TOKENS), I32)
+    table_rows = -(-TABLE_BLOCKS // 128) * 128
+    for at in range(0, table_rows, 128):
+        column = to_column(owner_row[:, at : at + 128])
+        hit = (iota((128, TOKENS), 0) + at) == block
+        slot = slot + jnp.sum(jnp.where(hit, column, 0), 0, keepdims=True)
+    owner = jnp.zeros((1, TOKENS), I32)
+    for k in range(1, n_blk):
+        owner = owner + (slot >= k * slots).astype(I32)
+    inside = slot - owner * slots
+    row = token - block * UNIT
+    upper = (row >= HALF).astype(I32)
+    dest = owner * n_rep + upper
+    local_row = inside * HALF + row - upper * HALF
+    token = jnp.where(live, token, -1)
+    first_at = jnp.full((128, TOKENS), TOKENS, I32)
+    for at in range(0, TOKENS, 128):
+        column = to_column(token[:, at : at + 128])
+        same = column == token
+        first_at = jnp.minimum(first_at, jnp.where(same, iota((128, TOKENS), 0) + at, TOKENS))
+    first_at = jnp.min(first_at, 0, keepdims=True)
+    first = live & (first_at == lane)
+    chosen = ((iota((n_dest, TOKENS), 0) == dest) & first).astype(F32)
+    chosen_low = chosen.astype(BF16)
+    seen = jnp.zeros((n_dest, TOKENS), F32)
+    for at in range(0, TOKENS, 128):
+        earlier = ((iota((128, TOKENS), 0) + at) < first_at).astype(F32).astype(BF16)
+        seen = seen + dot_nn(chosen_low[:, at : at + 128], earlier)
+    rank = jnp.sum(
+        jnp.where(iota((n_dest, TOKENS), 0) == dest, seen, 0.0), 0, keepdims=True
+    ).astype(I32)
+    fits = live & (rank < cap)
+    where_row[...] = jnp.where(fits, dest * cap + rank, -1)
+    over = jnp.max((live & (rank >= cap)).astype(I32))
+    code = local_row + 1
+    high = code // 32
+    low = code - high * 32
+    spread = (iota((128, TOKENS), 0) == rank).astype(F32).astype(BF16)
+    sent_high = dot_nt((chosen * high.astype(F32)).astype(BF16), spread)
+    sent_low = dot_nt((chosen * low.astype(F32)).astype(BF16), spread)
+    request = sent_high.astype(I32) * 32 + sent_low.astype(I32) - 1
+    flag = jnp.maximum(over, tab[TAB_FLAG])
+    column_of = iota((n_dest, 128), 1)
+    out = jnp.where(column_of < cap, request, 0)
+    out = jnp.where(column_of == 124, positive[0, 0], out)
+    out = jnp.where(column_of == 125, positive[0, 1], out)
+    message[...] = jnp.where(column_of == 126, flag, out)
+
+
+def request(owners, tab, me, positive, query_lengths, passage_lengths, query_ids, passage_ids, slots, n_blk, cap):
+    n_dest = 2 * n_blk
+    table_rows = -(-TABLE_BLOCKS // 128) * 128
+    owner_row = owners[:table_rows].reshape(1, table_rows)
+    return pl.pallas_call(
+        partial(request_kernel, slots, n_blk, cap),
+        out_shape=(
+            jax.ShapeDtypeStruct((n_dest, 128), I32),
+            jax.ShapeDtypeStruct((1, TOKENS), I32),
+            jax.ShapeDtypeStruct((TAB_SIZE,), I32),
+        ),
+        in_specs=[smem, smem, smem, smem, smem, smem, vmem, vmem, vmem],
+        out_specs=(vmem, vmem, smem),
+        scratch_shapes=[pltpu.VMEM((1, TOKENS), I32), pltpu.SMEM((n_blk,), I32)],
+        compiler_params=PARAMS,
+        name="request",
+    )(owners, tab, me, positive, query_lengths, passage_lengths, owner_row, query_ids, passage_ids)
+
+
+def fetch_kernel(slots, cap, me, message, weights, rows_out, held, table, hot, sem):
+    n_dest = message.shape[0]
+    half = me[1]
+    copy = pltpu.make_async_copy(weights.at[:, pl.ds(half * HALF, HALF), :], held, sem)
+    copy.start()
+    wide = table.shape[0]
+    rows = message[...]
+    pad = -n_dest % 128
+    if pad:
+        rows = jnp.concatenate([rows, jnp.zeros((pad, 128), I32)], 0)
+    columns = rows.T
+    for s in range(n_dest):
+        hot[s * cap : (s + 1) * cap] = (
+            (iota((cap, wide), 1) == columns[:cap, s : s + 1]).astype(F32).astype(BF16)
+        )
+    copy.wait()
+    filled = slots * HALF
+    table[:filled] = held[...].reshape(filled, D).astype(BF16)
+    if wide > filled:
+        table[filled:] = jnp.zeros((wide - filled, D), BF16)
+    rows_out[...] = dot_nn(hot[...], table[...]).astype(BF16)
+
+
+def fetch(me, message, weights, cap):
+    slots = weights.shape[0]
+    n_dest = message.shape[0]
+    wide = -(-slots * HALF // 128) * 128
+    return pl.pallas_call(
+        partial(fetch_kernel, slots, cap),
+        out_shape=jax.ShapeDtypeStruct((n_dest * cap, D), BF16),
+        in_specs=[smem, vmem, hbm],
+        out_specs=vmem,
+        scratch_shapes=[
+            pltpu.VMEM((slots, HALF, D), F32),
+            pltpu.VMEM((wide, D), BF16),
+            pltpu.VMEM((n_dest * cap, wide), BF16),
+            pltpu.SemaphoreType.DMA,
+        ],
+        compiler_params=PARAMS,
+        name="fetch",
+    )(me, message, weights)
+
+
+ST_POOLED, ST_C, ST_N2, ST_N1, ST_H, ST_O, ST_Q, ST_X0 = range(0, 64, 8)
+ST_KQ, ST_B, ST_U, ST_A, ST_I1, ST_I2 = 64, 96, 128, 160, 192, 200
+ST_ROWS = 208
+
+
+def start_matrices(tab, gathered, matrices, sems, first=0):
+    for b in range(first, DENSE):
+        pltpu.make_async_copy(
+            gathered.at[tab[TAB_PLACE + b]], matrices.at[pl.ds(b * UNIT, UNIT)], sems.at[b]
+        ).start()
+
+
+def wait_matrices(gathered, matrices, sems, first=0):
+    for b in range(first, DENSE):
+        pltpu.make_async_copy(
+            gathered.at[0], matrices.at[pl.ds(b * UNIT, UNIT)], sems.at[b]
+        ).wait()
+
+
+def forward_kernel(
+    tab, query_lengths, passage_lengths, positive, rows, where_row, vectors, gathered,
+    emb_out, low_out, normed_out, scale_out, probs_out, state, matrices, embedded, sems,
+):
+    start_matrices(tab, gathered, matrices, sems)
+    taken = rows.shape[0]
+    for at in range(0, TOKENS, 128):
+        column = to_column(where_row[:, at : at + 128])
+        hot = (iota((128, taken), 1) == column).astype(F32).astype(BF16)
+        embedded[at : at + 128] = dot_nn(hot, rows[...])
+    wait_matrices(gathered, matrices, sems)
+    shift = vectors[0:1]
+    for start, length in zip(STARTS, (QROWS, QROWS, PLEN, PLEN)):
+        e = embedded[start : start + length] + matrices[:length].astype(F32) + shift
+        centred = e - jnp.mean(e, -1, keepdims=True)
+        scale = lax.rsqrt(jnp.mean(centred * centred, -1, keepdims=True) + NORM_EPS)
+        normed = centred * scale
+        normed_out[start : start + length] = normed
+        scale_out[start : start + length] = jnp.broadcast_to(scale, (length, 128))
+        x = normed * vectors[1:2] + vectors[2:3]
+        embedded[start : start + length] = x
+        low_out[start : start + length] = x.astype(BF16)
+    x0 = jnp.concatenate(
+        [embedded[s : s + 1] for s in STARTS] + [jnp.zeros((4, D), F32)], 0
+    )
+    x0_low = x0.astype(BF16)
+    q = (dot_nn(x0_low, matrices[AT_Q:AT_K]) + vectors[4:5]).astype(BF16)
+    head_of = iota((8, D), 1) // HALF
+    q_heads = jnp.concatenate(
+        [jnp.where(head_of == h, q.astype(F32), 0.0) for h in range(HEADS)], 0
+    ).astype(BF16)
+    kq = dot_nt(q_heads, matrices[AT_K:AT_V]) * (D // HEADS) ** (-0.5)
+    low = low_out[...]
+    scores = fine(dot_nt, kq, low)
+    sequence, live = token_facts(query_lengths, passage_lengths)
+    valid = ((iota((32, TOKENS), 0) & 7) == sequence) & live
+    scores = jnp.where(valid, scores, NEVER)
+    top = jnp.max(scores, -1, keepdims=True)
+    weight = jnp.where(valid, jnp.exp(scores - top), 0.0)
+    total = jnp.sum(weight, -1, keepdims=True)
+    probs = weight / jnp.where(total > 0.0, total, 1.0)
+    probs_out[...] = probs
+    mixed = dot_nn(probs.astype(BF16), low)
+    valued = fine(dot_nn, mixed, matrices[AT_V:AT_O])
+    blended = jnp.zeros((8, D), F32)
+    for h in range(HEADS):
+        blended = blended + jnp.where(head_of == h, valued[8 * h : 8 * h + 8], 0.0)
+    real = iota((8, D), 0) < 4
+    blended = jnp.where(real, blended + vectors[5:6], 0.0).astype(BF16)
+    summed = x0 + dot_nn(blended, matrices[AT_O:AT_UP]) + vectors[6:7]
+    h0, n1, i1 = norm_rows(summed, vectors[8:9], vectors[9:10])
+    h_low = h0.astype(BF16)
+    bias_up = jnp.concatenate([vectors[12 + i : 13 + i] for i in range(FF // D)], 1)
+    u = dot_nt(h_low, matrices[AT_UP:AT_DOWN]) + bias_up
+    a = (0.5 * u * (1.0 + lax.erf(u * (0.5**0.5)))).astype(BF16)
+    second = h0 + dot_nn(a, matrices[AT_DOWN:]) + vectors[7:8]
+    x, n2, i2 = norm_rows(second, vectors[10:11], vectors[11:12])
+    c = x.astype(BF16)
+    pooled = jnp.tanh(dot_nn(c, matrices[AT_POOL:AT_Q]) + vectors[3:4])
+    row8 = iota((8, 128), 0)
+    sent = jnp.concatenate(
+        [
+            jnp.where(real, pooled, 0.0),
+            jnp.where(
+                row8 == 0,
+                positive[0, 0].astype(F32),
+                jnp.where(row8 == 1, positive[0, 1].astype(F32), -1.0),
+            ),
+        ],
+        1,
+    )
+    n_blk = emb_out.shape[0] // 8
+    emb_out[...] = jnp.concatenate([sent] * n_blk, 0).astype(BF16)
+    state[ST_POOLED : ST_POOLED + 8] = pooled
+    state[ST_C : ST_C + 8] = c.astype(F32)
+    state[ST_N2 : ST_N2 + 8] = n2
+    state[ST_N1 : ST_N1 + 8] = n1
+    state[ST_H : ST_H + 8] = h_low.astype(F32)
+    state[ST_O : ST_O + 8] = blended.astype(F32)
+    state[ST_Q : ST_Q + 8] = q.astype(F32)
+    state[ST_X0 : ST_X0 + 8] = x0_low.astype(F32)
+    state[ST_KQ : ST_KQ + 32] = kq
+    state[ST_B : ST_B + 32] = mixed
+    for i in range(FF // D):
+        state[ST_U + 8 * i : ST_U + 8 * i + 8] = u[:, i * D : (i + 1) * D]
+        state[ST_A + 8 * i : ST_A + 8 * i + 8] = a[:, i * D : (i + 1) * D].astype(F32)
+    state[ST_I1 : ST_I1 + 8] = jnp.broadcast_to(i1, (8, D))
+    state[ST_I2 : ST_I2 + 8] = jnp.broadcast_to(i2, (8, D))
+
+
+def forward(tab, query_lengths, passage_lengths, positive, rows, where_row, vectors, gathered, n_blk):
+    return pl.pallas_call(
+        forward_kernel,
+        out_shape=(
+            jax.ShapeDtypeStruct((n_blk * 8, D + 128), BF16),
+            jax.ShapeDtypeStruct((TOKENS, D), BF16),
+            jax.ShapeDtypeStruct((TOKENS, D), F32),
+            jax.ShapeDtypeStruct((TOKENS, 128), F32),
+            jax.ShapeDtypeStruct((32, TOKENS), F32),
+            jax.ShapeDtypeStruct((ST_ROWS, D), F32),
+        ),
+        in_specs=[smem, smem, smem, smem, vmem, vmem, vmem, hbm],
+        out_specs=(vmem,) * 6,
+        scratch_shapes=[
+            pltpu.VMEM((DENSE * UNIT, D), BF16),
+            pltpu.VMEM((TOKENS, D), F32),
+            pltpu.SemaphoreType.DMA((DENSE,)),
+        ],
+        compiler_params=PARAMS,
+        name="forward",
+    )(tab, query_lengths, passage_lengths, positive, rows, where_row, vectors, gathered)
+
+
+def place_rows(n_dest):
+    return max(PLEN // n_dest, 16)
+
+
+def payload_rows(n_dest, cap):
+    at_place = 2 * cap
+    at_left = at_place + 2 * place_rows(n_dest)
+    at_right = at_left + L_ROWS
+    return at_place, at_left, at_right, at_right + 32
+
+
+def backward_kernel(
+    cap, tab, me, prefix_lengths, prefix_weights, emb, message, where_row, low_in, normed, scale,
+    probs_in, state, vectors, gathered, payload, loss_out, count_out,
+    matrices, received, grad_emb, dx, left, sems,
+):
+    start_matrices(tab, gathered, matrices, sems, PLACE_BLOCKS)
+    n_blk = emb.shape[0] // 8
+    n_dest = 2 * n_blk
+    for i in range(3):
+        received[i * n_blk * 8 : (i + 1) * n_blk * 8] = emb[:, 128 * i : 128 * i + 128].astype(F32)
+
+    def every(k):
+        return jnp.concatenate(
+            [received[pl.ds(i * n_blk * 8 + k, n_blk, stride=8), :] for i in range(3)], 1
+        )
+
+    queries = jnp.concatenate([every(0), every(1)], 0)
+    passages = jnp.concatenate([every(2), every(3)], 0)[:, :D].astype(BF16)
+    wanted = queries[:, D : D + 1].astype(I32)
+    queries = queries[:, :D]
+    query_low = queries.astype(BF16)
+    size = 2 * n_blk
+    counted = wanted >= 0
+    counted_f = counted.astype(F32)
+    column = iota((size, size), 1)
+    target = (column == (wanted & 1) * n_blk + wanted // 2) & counted
+    marks = message[...]
+    lane = iota(marks.shape, 1)
+    count = jnp.sum((((lane == 124) | (lane == 125)) & (marks >= 0)).astype(F32))
+    count_out[0, 0] = count
+    feature = iota((1, D), 1)
+    losses = jnp.zeros((size, 1), F32)
+    d_queries = jnp.zeros((size, D), F32)
+    d_passages = jnp.zeros((size, D), F32)
+    for k in range(prefix_lengths.shape[0]):
+        mask = (feature < prefix_lengths[k]).astype(F32)
+        prefix = jnp.full((1, 1), prefix_lengths[k], I32).astype(F32)
+        temper = TEMPER * lax.rsqrt(prefix)
+        logits = dot_nt((queries * mask).astype(BF16), passages) * temper
+        top = jnp.max(logits, -1, keepdims=True)
+        weight = jnp.exp(logits - top)
+        total = jnp.sum(weight, -1, keepdims=True)
+        hit = jnp.sum(jnp.where(target, logits, 0.0), -1, keepdims=True)
+        losses = losses + prefix_weights[k] * (top + jnp.log(total) - hit)
+        factor = counted_f * (prefix_weights[k] / count) * temper
+        grad = (weight / total - target.astype(F32)) * factor
+        high, lower = split(grad)
+        d_queries = d_queries + mask * (dot_nn(high, passages) + dot_nn(lower, passages))
+        d_passages = d_passages + mask * (dot_tn(high, query_low) + dot_tn(lower, query_low))
+    loss_out[0, 0] = jnp.sum(losses * counted_f)
+    grad_emb[:size] = d_queries
+    grad_emb[size : 2 * size] = d_passages
+    grad_pooled = jnp.concatenate(
+        [grad_emb[pl.ds(me[0] + i * n_blk, 1), :] for i in range(4)]
+        + [jnp.zeros((4, D), F32)],
+        0,
+    )
+    wait_matrices(gathered, matrices, sems, PLACE_BLOCKS)
+
+    def kept_rows(at, rows=8):
+        return state[at : at + rows]
+
+    pooled = kept_rows(ST_POOLED)
+    d_pre = grad_pooled * (1.0 - pooled * pooled)
+    d_c = fine(dot_nt, d_pre, matrices[AT_POOL:AT_Q])
+    n2 = kept_rows(ST_N2)
+    d_second, d_g2, d_s2 = norm_back(d_c, n2, kept_rows(ST_I2), vectors[10:11])
+    down_low = d_second.astype(BF16)
+    d_a = dot_nt(down_low, matrices[AT_DOWN:])
+    u = jnp.concatenate([kept_rows(ST_U + 8 * i) for i in range(FF // D)], 1)
+    slope = 0.5 * (1.0 + lax.erf(u * (0.5**0.5))) + u * jnp.exp(-0.5 * u * u) * (
+        0.3989422804014327
+    )
+    up_low = (d_a * slope).astype(BF16)
+    d_h = d_second + dot_nn(up_low, matrices[AT_UP:AT_DOWN])
+    d_summed, d_g1, d_s1 = norm_back(d_h, kept_rows(ST_N1), kept_rows(ST_I1), vectors[8:9])
+    branch_low = d_summed.astype(BF16)
+    d_o = dot_nt(branch_low, matrices[AT_O:AT_UP]).astype(BF16)
+    head_of = iota((8, D), 1) // HALF
+    o_heads = jnp.concatenate(
+        [jnp.where(head_of == h, d_o.astype(F32), 0.0) for h in range(HEADS)], 0
+    ).astype(BF16)
+    vo = dot_nt(o_heads, matrices[AT_V:AT_O])
+    low = low_in[...]
+    probs = probs_in[...]
+    d_probs = fine(dot_nt, vo, low)
+    d_scores = probs * (d_probs - jnp.sum(d_probs * probs, -1, keepdims=True))
+    score_low = d_scores.astype(BF16)
+    mixed_score = dot_nn(score_low, low)
+    keyed = fine(dot_nn, mixed_score, matrices[AT_K:AT_V])
+    d_q = jnp.zeros((8, D), F32)
+    for h in range(HEADS):
+        d_q = d_q + jnp.where(head_of == h, keyed[8 * h : 8 * h + 8], 0.0)
+    d_q_low = (d_q * (D // HEADS) ** (-0.5)).astype(BF16)
+    d_x0 = d_summed + dot_nt(d_q_low, matrices[AT_Q:AT_K])
+    kq = kept_rows(ST_KQ, 32)
+    vo_high, vo_low = split(vo)
+    kq_high, kq_low = split(kq)
+    probs_low = probs.astype(BF16)
+    dx[...] = dot_tn(
+        jnp.concatenate([probs_low, score_low, probs_low, score_low], 0),
+        jnp.concatenate([vo_high, kq_high, vo_low, kq_low], 0),
+    )
+    for i, start in enumerate(STARTS):
+        dx[start : start + 1] = dx[start : start + 1] + d_x0[i : i + 1]
+    d_gain = jnp.zeros((1, D), F32)
+    d_shift = jnp.zeros((1, D), F32)
+    d_type = jnp.zeros((1, D), F32)
+    for start in range(0, TOKENS, 256):
+        incoming = dx[start : start + 256]
+        n = normed[start : start + 256]
+        d_gain = d_gain + jnp.sum(incoming * n, 0, keepdims=True)
+        d_shift = d_shift + jnp.sum(incoming, 0, keepdims=True)
+        dn = incoming * vectors[1:2]
+        inner = (
+            dn - jnp.mean(dn, -1, keepdims=True) - n * jnp.mean(dn * n, -1, keepdims=True)
+        )
+        de = inner * scale[start : start + 256, :1]
+        d_type = d_type + jnp.sum(de, 0, keepdims=True)
+        dx[start : start + 256] = de
+    de_low = dx[...].astype(BF16)
+    at_place, at_left, at_right, n_rows = payload_rows(n_dest, cap)
+    per = max(128 // cap, 1)
+    step = per * cap
+    for at in range(0, n_dest * cap, step):
+        hot = ((iota((step, TOKENS), 0) + at) == where_row[...]).astype(F32).astype(BF16)
+        summed = dot_nn(hot, de_low).astype(BF16)
+        for i in range(per):
+            d = at // cap + i
+            if d < n_dest:
+                payload[d, :cap] = summed[i * cap : (i + 1) * cap, :128]
+                payload[d, cap : 2 * cap] = summed[i * cap : (i + 1) * cap, 128:]
+    spots = dx[STARTS[2] : STARTS[3]] + dx[STARTS[3] :]
+    dx[STARTS[2] : STARTS[3]] = spots
+    dx[STARTS[2] : STARTS[2] + QROWS] = (
+        dx[STARTS[2] : STARTS[2] + QROWS] + dx[:QROWS] + dx[QROWS : 2 * QROWS]
+    )
+    pr = place_rows(n_dest)
+    share = PLEN // n_dest
+    for d in range(n_dest):
+        spot = dx[STARTS[2] + d * share : STARTS[2] + (d + 1) * share]
+        if share < pr:
+            spot = jnp.concatenate([spot, jnp.zeros((pr - share, D), F32)], 0)
+        payload[d, at_place : at_place + pr] = spot[:, :128].astype(BF16)
+        payload[d, at_place + pr : at_place + 2 * pr] = spot[:, 128:].astype(BF16)
+    left[...] = jnp.zeros(left.shape, F32)
+    up_f = up_low.astype(F32)
+
+    def put(b, r, unit, values):
+        spot = (tab[TAB_OWNER + b] * 2 + r) * L_ROWS + (tab[TAB_UNIT + b] + unit) * 4
+        for i in range(4):
+            left[pl.ds(spot + i, 1), :] = values[i : i + 1]
+
+    for b in range(PLACE_BLOCKS, DENSE):
+        at = b * UNIT
+        if AT_K <= at < AT_O:
+            heads = mixed_score if at < AT_V else kept_rows(ST_B, 32)
+            off = (at - AT_K) % D
+            for r in range(2):
+                for j in range(2):
+                    h = 2 * r + j
+                    put(b, r, j, heads[8 * h : 8 * h + 4, off : off + UNIT])
+            continue
+        if at < AT_Q:
+            values, off = kept_rows(ST_C), at - AT_POOL
+        elif at < AT_K:
+            values, off = kept_rows(ST_X0), at - AT_Q
+        elif at < AT_UP:
+            values, off = kept_rows(ST_O), at - AT_O
+        elif at < AT_DOWN:
+            values, off = up_f, at - AT_UP
+        else:
+            off = (at - AT_DOWN) % D
+            values = kept_rows(ST_A + 8 * ((at - AT_DOWN) // D))
+        for r in range(2):
+            put(b, r, 0, values[:4, off : off + UNIT])
+    d_vectors = jnp.concatenate(
+        [
+            d_type,
+            d_gain,
+            d_shift,
+            jnp.sum(d_pre, 0, keepdims=True),
+            jnp.sum(d_q_low.astype(F32), 0, keepdims=True),
+            jnp.sum(d_o.astype(F32), 0, keepdims=True),
+            jnp.sum(branch_low.astype(F32), 0, keepdims=True),
+            jnp.sum(down_low.astype(F32), 0, keepdims=True),
+            d_g1[None],
+            d_s1[None],
+            d_g2[None],
+            d_s2[None],
+        ]
+        + [
+            jnp.sum(up_f[:, i * D : (i + 1) * D], 0, keepdims=True) for i in range(FF // D)
+        ],
+        0,
+    )
+    scaled_q = kept_rows(ST_Q) * (D // HEADS) ** (-0.5)
+    right = jnp.concatenate(
+        [
+            v.astype(F32)[:4]
+            for v in (d_pre, d_q_low, scaled_q, d_o, branch_low, kept_rows(ST_H), down_low)
+        ],
+        0,
+    )
+    for d in range(n_dest):
+        payload[d, at_left:at_right] = left[d * L_ROWS : (d + 1) * L_ROWS].astype(BF16)
+        r = d % 2
+        if d < 32:
+            share_vec = d_vectors[d // 2 : d // 2 + 1, r * 128 : (r + 1) * 128]
+        else:
+            share_vec = jnp.zeros((1, 128), F32)
+        payload[d, at_right:n_rows] = jnp.concatenate(
+            [right[:, r * 128 : (r + 1) * 128], share_vec, jnp.zeros((3, 128), F32)], 0
+        ).astype(BF16)
+
+
+def backward(tab, me, prefix_lengths, prefix_weights, emb, message, where_row, low, normed, scale, probs, state, vectors, gathered, cap):
+    n_dest = message.shape[0]
+    n_rows = payload_rows(n_dest, cap)[-1]
+    return pl.pallas_call(
+        partial(backward_kernel, cap),
+        out_shape=(
+            jax.ShapeDtypeStruct((n_dest, n_rows, 128), BF16),
+            jax.ShapeDtypeStruct((1, 1), F32),
+            jax.ShapeDtypeStruct((1, 1), F32),
+        ),
+        in_specs=[smem] * 4 + [vmem] * 9 + [hbm],
+        out_specs=(vmem, smem, smem),
+        scratch_shapes=[
+            pltpu.VMEM((DENSE * UNIT, D), BF16),
+            pltpu.VMEM((emb.shape[0] * 3, 128), F32),
+            pltpu.VMEM((emb.shape[0], D), F32),
+            pltpu.VMEM((TOKENS, D), F32),
+            pltpu.VMEM((n_dest * L_ROWS, 128), F32),
+            pltpu.SemaphoreType.DMA((DENSE,)),
+        ],
+        compiler_params=PARAMS,
+        name="backward",
+    )(tab, me, prefix_lengths, prefix_weights, emb, message, where_row, low, normed, scale, probs, state, vectors, gathered)
+
+
+def reduce_kernel(slots, cap, tab, me, loss, asked, payload, reduced, news, total, row_grads, left, right):
+    n_dest = payload.shape[0]
+    at_place, at_left, at_right, n_rows = payload_rows(n_dest, cap)
+    for d in range(n_dest):
+        row_grads[d * cap : (d + 1) * cap, :128] = payload[d, :cap]
+        row_grads[d * cap : (d + 1) * cap, 128:] = payload[d, cap : 2 * cap]
+        left[d * L_ROWS : (d + 1) * L_ROWS] = payload[d, at_left:at_right].astype(F32)
+        right[d * 32 : (d + 1) * 32] = payload[d, at_right:n_rows].astype(F32)
+    grads = row_grads[...]
+    filled = slots * HALF
+    for at in range(0, filled, 64):
+        hot = ((iota((64, n_dest * cap), 0) + at) == asked[...]).astype(F32).astype(BF16)
+        total[at : at + 64] = dot_nn(hot, grads)
+    mine = me[0]
+    odd = me[1]
+    column = iota((n_dest * 4, 128), 1)
+
+    def rows_of(ref, start, stride):
+        return jnp.concatenate(
+            [ref[pl.ds(start + q, n_dest, stride=stride), :] for q in range(4)], 0
+        ).astype(BF16)
+
+    for b in range(PLACE_BLOCKS, DENSE):
+        at = b * UNIT
+        if at < AT_Q:
+            m = 0
+        elif at < AT_UP:
+            m = 1 + (at - AT_Q) // D
+        elif at < AT_DOWN:
+            m = 5
+        else:
+            m = 6
+
+        @pl.when(tab[TAB_OWNER + b] == mine)
+        def _():
+            unit = tab[TAB_UNIT + b] * 4
+            pull = rows_of(right, m * 4, 32)
+            if AT_K <= at < AT_O:
+                grad = dot_tn(
+                    rows_of(left, unit, L_ROWS), jnp.where(column < HALF, pull, 0).astype(BF16)
+                ) + dot_tn(
+                    rows_of(left, unit + 4, L_ROWS),
+                    jnp.where(column < HALF, 0, pull).astype(BF16),
+                )
+            else:
+                grad = dot_tn(rows_of(left, unit, L_ROWS), pull)
+            spot = pl.multiple_of(tab[TAB_SLOT + b] * HALF, HALF)
+            total[pl.ds(spot, HALF), :128] = grad[:HALF]
+            total[pl.ds(spot, HALF), 128:] = grad[HALF:]
+
+    pr = place_rows(n_dest)
+    spots_low = jnp.zeros((pr, 128), F32)
+    spots_high = jnp.zeros((pr, 128), F32)
+    for d in range(n_dest):
+        spots_low = spots_low + payload[d, at_place : at_place + pr].astype(F32)
+        spots_high = spots_high + payload[d, at_place + pr : at_place + 2 * pr].astype(F32)
+    spots = jnp.concatenate([spots_low, spots_high], 1)
+    vector = jnp.sum(right[pl.ds(28, n_dest, stride=32), :], 0, keepdims=True)
+    summed = total[...]
+    reduced[...] = summed.astype(BF16).reshape(reduced.shape)
+    square = jnp.sum(summed * summed) + jnp.sum(spots * spots) + jnp.sum(vector * vector)
+    row16 = iota((pr, 128), 0)
+
+    def parts(v):
+        first = v.astype(BF16).astype(F32)
+        second = (v - first).astype(BF16).astype(F32)
+        return first, second, v - first - second
+
+    extra = jnp.zeros((pr, 128), F32)
+    for i, part in enumerate(
+        parts(vector)
+        + parts(jnp.full((1, 128), square, F32))
+        + parts(jnp.full((1, 128), loss[0, 0], F32))
+    ):
+        extra = jnp.where(row16 == i, part, extra)
+    block = jnp.concatenate([spots, extra], 1).astype(BF16)
+    for d in range(n_dest):
+        news[d * pr : (d + 1) * pr] = block
+
+
+def reduce(tab, me, loss, asked, payload, slots, cap):
+    n_dest = payload.shape[0]
+    pr = place_rows(n_dest)
+    return pl.pallas_call(
+        partial(reduce_kernel, slots, cap),
+        out_shape=(
+            jax.ShapeDtypeStruct((slots, HALF, D), BF16),
+            jax.ShapeDtypeStruct((n_dest * pr, D + 128), BF16),
+        ),
+        in_specs=[smem, smem, smem, vmem, vmem],
+        out_specs=(vmem, vmem),
+        scratch_shapes=[
+            pltpu.VMEM((slots * HALF, D), F32),
+            pltpu.VMEM((n_dest * cap, D), BF16),
+            pltpu.VMEM((n_dest * L_ROWS, 128), F32),
+            pltpu.VMEM((n_dest * 32, 128), F32),
+        ],
+        compiler_params=PARAMS,
+        name="reduce",
+    )(tab, me, loss, asked, payload)
+
+
+def update_kernel(
+    pr, tab, me, news, places, own, other, weight, first, second, vectors, vector_first,
+    vector_second, weight_out, first_out, second_out, vectors_out, vector_first_out,
+    vector_second_out, loss_out, norm_out, factor_ref,
+):
+    i = pl.program_id(0)
+    n_dest = news.shape[0] // pr
+
+    def strip(row):
+        return news[pl.ds(row, n_dest, stride=pr), D:]
+
+    @pl.when(i == 0)
+    def _():
+        extra = news[...][:, D:].astype(F32).reshape(n_dest, pr, 128)
+        sums = jnp.sum(extra[:, 3:6, :], 0)
+        square = jnp.sum(sums, 0, keepdims=True)
+        norm = jnp.sqrt(square)
+        factor = CLIP_AT / jnp.maximum(norm, CLIP_AT)
+        factor_ref[...] = jnp.broadcast_to(factor, (8, 128))
+        norm_out[0, 0] = norm[0, 0]
+        loss = jnp.sum(extra[0:2, 6:9, :], 0)
+        loss = jnp.sum(loss, 0, keepdims=True)
+        loss_out[0, 0] = loss[0, 0]
+        pieces = jnp.sum(extra[:32, 0:3, :], 1)
+        pairs = pieces.reshape(16, 2, 128)
+        grad = jnp.concatenate([pairs[:, 0], pairs[:, 1]], 1) * factor[0, 0]
+        v, m1, m2 = adam_step(
+            vectors[...], vector_first[...], vector_second[...], grad, VECTOR_RATE, 0.0
+        )
+        vectors_out[...] = v
+        vector_first_out[...] = m1
+        vector_second_out[...] = m2
+
+    kind = tab[TAB_KIND + i]
+    flip = me[1] == 0
+    mine = own[0].astype(F32)
+    theirs = other[0].astype(F32)
+    lower = jnp.where(flip, mine, theirs)
+    upper = jnp.where(flip, theirs, mine)
+
+    def step(grad):
+        w, m1, m2 = adam_step(
+            weight[0], first[0], second[0], grad * factor_ref[0:1, 0:1], RATE, DECAY
+        )
+        weight_out[0] = w
+        first_out[0] = m1
+        second_out[0] = m2
+
+    @pl.when(kind == 0)
+    def _():
+        weight_out[0] = weight[0]
+        first_out[0] = first[0]
+        second_out[0] = second[0]
+
+    @pl.when(kind == KIND_TABLE)
+    def _():
+        step(jnp.concatenate([lower, upper], 0))
+
+    @pl.when(kind == KIND_DENSE)
+    def _():
+        step(
+            jnp.concatenate(
+                [
+                    jnp.concatenate([lower[:, :128], lower[:, 128:]], 0),
+                    jnp.concatenate([upper[:, :128], upper[:, 128:]], 0),
+                ],
+                1,
+            )
+        )
+
+    @pl.when((kind >= KIND_PLACE) & (kind < KIND_DENSE))
+    def _():
+        spot = pl.multiple_of((kind - KIND_PLACE) * UNIT, UNIT)
+        step(places[pl.ds(spot, UNIT), :D].astype(F32))
+
+
+def update(tab, me, news, own, other, weights, first, second, vectors, vector_first, vector_second, pr):
+    slots = weights.shape[0]
+    n_dest = news.shape[0] // pr
+    share = PLEN // n_dest
+    places = news
+    if share < pr:
+        places = news.reshape(n_dest, pr, -1)[:, :share].reshape(PLEN, -1)
+    slot = pl.BlockSpec((1, UNIT, D), lambda i: (i, 0, 0))
+    half = pl.BlockSpec((1, HALF, D), lambda i: (i, 0, 0))
+    whole = lambda a: pl.BlockSpec(a.shape, lambda i: (0,) * a.ndim)
+    big = jax.ShapeDtypeStruct(weights.shape, F32)
+    small = jax.ShapeDtypeStruct(vectors.shape, F32)
+    one = jax.ShapeDtypeStruct((1, 1), F32)
+    return pl.pallas_call(
+        partial(update_kernel, pr),
+        grid=(slots,),
+        out_shape=(big, big, big, small, small, small, one, one),
+        in_specs=[smem, smem, whole(news), whole(places), half, half, slot, slot, slot]
+        + [whole(vectors)] * 3,
+        out_specs=(slot, slot, slot) + (whole(vectors),) * 3 + (smem, smem),
+        scratch_shapes=[pltpu.VMEM((8, 128), F32)],
+        compiler_params=PARAMS,
+        name="update",
+    )(tab, me, news, places, own, other, weights, first, second, vectors, vector_first, vector_second)
+
+
+def quick(
+    query_ids, passage_ids, query_lengths, passage_lengths, positive, prefix_lengths,
+    prefix_weights, owners, weights, first_moments, second_moments, vectors, vector_first,
+    vector_second,
+):
+    slots = weights.shape[0]
+    n_blk = lax.axis_size("blk")
+    everyone = ("blk", "rep")
+    cap = 48 if n_blk <= 16 else 16
+    dense_cap = min(7, slots)
+    me = jnp.stack([lax.axis_index("blk"), lax.axis_index("rep")]).astype(I32)
+
+    def exchange(a, axes):
+        return lax.all_to_all(a, axes, 0, 0, tiled=True)
+
+    dense, tab = prepare(owners, me, weights, n_blk, dense_cap)
+    gathered = lax.all_gather(dense, "blk", axis=0, tiled=True)
+    message, where_row, tab = request(
+        owners, tab, me, positive, query_lengths, passage_lengths, query_ids[0], passage_ids[0],
+        slots, n_blk, cap,
+    )
+    message = exchange(message, everyone)
+    rows = exchange(fetch(me, message, weights, cap), everyone)
+    emb, low, normed, scale, probs, state = forward(
+        tab, query_lengths, passage_lengths, positive, rows, where_row, vectors, gathered, n_blk
+    )
+    emb = exchange(emb, "blk")
+    payload, loss, count = backward(
+        tab, me, prefix_lengths, prefix_weights, emb, message, where_row, low, normed, scale,
+        probs, state, vectors, gathered, cap,
+    )
+    payload = exchange(payload, everyone)
+    asked = message[:, :cap].reshape(1, -1)
+    own, news = reduce(tab, me, loss, asked, payload, slots, cap)
+    other = lax.ppermute(own, "rep", [(0, 1), (1, 0)])
+    news = exchange(news, everyone)
+    overflow = jnp.max(message[:, 126]) > 0
+
+    def roomy():
+        return local(
+            query_ids, passage_ids, query_lengths, passage_lengths, positive, prefix_lengths,
+            prefix_weights, owners, weights, first_moments, second_moments, vectors, vector_first,
+            vector_second,
+        )
+
+    def usual():
+        *outs, loss_sum, norm = update(
+            tab, me, news, own, other, weights, first_moments, second_moments, vectors,
+            vector_first, vector_second, place_rows(2 * n_blk),
+        )
+        return (*outs, loss_sum.reshape(()), count.reshape(()), norm.reshape(()))
+
+    return lax.cond(overflow, roomy, usual)
+
+
 def solution(mesh):
     in_specs = (
         P("rep", "blk", None),
@@ -456,4 +1423,4 @@
         P(),
         P(),
     )
-    return jax.shard_map(local, mesh=mesh, in_specs=in_specs, out_specs=out_specs, check_vma=False)
+    return jax.shard_map(quick, mesh=mesh, in_specs=in_specs, out_specs=out_specs, check_vma=False)

time: 1130 us -> 218 us (0.19)
  waiting for transfers between devices: 463 us -> 70 us
  local copies, waits for them, and re-layouts: 196 us -> 2 us
  other arithmetic: 149 us -> 0.78 us
  blocking collectives: 192 us -> 66 us
  matrix products: 101 us -> 0 us
  Pallas kernels: 0 us -> 53.6 us
    reduce_scatter x1 -> x0, waiting for transfers between devices: 347 us -> none  [local(): reduced = lax.psum_scatter(buffer, 'blk', scatter_dimension=0, tiled=True)]
    psum x3 -> x0, blocking collectives: 111 us -> none  [the longest x1 40 us: local(): vec_total = lax.psum(vec_query + vec_pass, ('blk', 'rep'))]
    dot_general x55 -> x0, matrix products: 80.6 us -> none  [the longest x8 33.4 us: mult_nt(): lax.dot_general(left_op, right_op, (((1,), (1,)), ((), ())), preferred_el...]
    all_gather x1, waiting for transfers between devices: 90.4 us -> 14.7 us  [quick(): gathered = lax.all_gather(dense, 'blk', axis=0, tiled=True)]
    scatter x3 -> x0, local copies, waits for them, and re-layouts: 66.8 us -> none  [the longest x1 66.7 us: local(): buffer = jnp.zeros((lax.axis_size('blk') * slot_count, unit_rows, D), jnp...]
    all_to_all x0 -> x3, blocking collectives: none -> 66 us  [exchange(): return lax.all_to_all(a, axes, 0, 0, tiled=True)]
    unnamed x1 -> x0, blocking collectives: 60.9 us -> none
    pallas_call x0 -> x7, Pallas kernels: none -> 53.6 us  [the longest x1 13.4 us: update(): pl.pallas_call(partial(update_kernel, pr), grid=(slots,), out_shape=(big,...]
  transfers between devices with their start and end apart: 3 -> 4, of which waited for: 3 -> 3; matrix products, arithmetic and copies ran while one was open for 1% -> 1% of each run, Pallas kernels for 0% -> 5%
where the time goes in v1:
time: 218 us; the launch traced here: 216 us
  waiting for transfers between devices  70 us (32%)
  blocking collectives  66 us (30%)
  Pallas kernels  53.6 us (25%)
  between operations  14.9 us (7%)
  starting transfers between devices  8.69 us (4%)
    all_to_all x3, blocking collectives, exchange(): return lax.all_to_all(a, axes, 0, 0, tiled=True)  66 us
    all_to_all x2, waiting for transfers between devices, exchange(): return lax.all_to_all(a, axes, 0, 0, tiled=True)  39.4 us
    ppermute x1, waiting for transfers between devices, quick(): other = lax.ppermute(own, 'rep', [(0, 1), (1, 0)])  15.9 us
    all_gather x1, waiting for transfers between devices, quick(): gathered = lax.all_gather(dense, 'blk', axis=0, tiled=True)  14.7 us
    pallas_call x1, Pallas kernels, update(): pl.pallas_call(partial(update_kernel, pr), grid=(slots,), out_shape=(big,...  13.4 us
    pallas_call x1, Pallas kernels, backward(): pl.pallas_call(partial(backward_kernel, cap), out_shape=(jax.ShapeDtypeSt...  11.1 us
    pallas_call x1, Pallas kernels, request(): pl.pallas_call(partial(request_kernel, slots, n_blk, cap), out_shape=(jax...  7.71 us
    all_to_all x2, starting transfers between devices, exchange(): return lax.all_to_all(a, axes, 0, 0, tiled=True)  6.82 us
  transfers between devices with their start and end apart: 4, of which 3 were waited for; matrix products, arithmetic and copies ran while one was open for 1% of the time, Pallas kernels for 5%

profile of v1, /device:TPU:0, one launch (start us, length us, event | category | flops | bytes accessed | tf_op | source)
XLA Modules:
  0.0 216.2 jit_solution(5270420685415295808)
XLA Ops:
  7.2 0.0 copy-start.2
  7.2 0.0 copy-start.165
  7.2 0.0 copy-start.127
  7.2 0.0 copy-start.128
  7.2 0.0 all-gather.6.cloned.1.call-start
  7.3 0.1 pad_add_fusion.me
  7.4 5.1 %prepare.1 = (bf16[7,128,256]{2,1,0:T(8,128)(2,1)}, s32[256]{0:T(256)}) custom-call(s32[269]{0:T(512)} %owners.3, s32[2]{0:T(128)S(1)} %pad_add_fusion.me, f32[17,128,256]{2,1,0:T(8,128)} %weights.3), custom_call_target="tpu_custom_call" | custom-call | tf_op jit(solution)/shard_map/prepare/pallas_call | solution.py:572
  12.4 0.0 all-gather.6.cloned.1.call-update
  12.5 1.2 slice.295
  13.7 7.7 %request.1 = (s32[32,128]{1,0:T(8,128)}, s32[1,1280]{1,0:T(1,128)}, s32[256]{0:T(256)S(1)}) custom-call(s32[269]{0:T(512)} %owners.3, s32[256]{0:T(256)} %get-tuple-element.266.tab_in, s32[2]{0:T(128)S(1)} %pad_add_fusion.me, s32[1,2]{1,0:T(1,128)} %positive.3, s32[1,2]{1,0:T(1,128)} %query_lengths.3, s32[1,2]{1,0:T(1,128)} %passage_lengths.3, ...), custom_call_target="tpu_custom_call" | custom-call | tf_op jit(solution)/shard_map/request/pallas_call | solution.py:697
  21.4 13.8 %all_to_all.49 = s32[32,1,128]{2,1,0:T(1,128)} all-to-all(s32[32,1,128]{2,1,0:T(1,128)} %bitcast.589), channel_id=1, replica_groups=mesh['blk'=16,'rep'=2] {'blk','rep'}, dimensions={0} | all-to-all | bytes 32768 | tf_op jit(solution)/shard_map/all_to_all | solution.py:1356
  35.2 3.6 %fetch.1 = bf16[1536,256]{1,0:T(8,128)(2,1)} custom-call(s32[2]{0:T(128)S(1)} %pad_add_fusion.me, s32[32,128]{1,0:T(8,128)} %bitcast.530, f32[17,128,256]{2,1,0:T(8,128)S(1)} %copy-done.2), custom_call_target="tpu_custom_call" | custom-call | tf_op jit(solution)/shard_map/fetch/pallas_call | solution.py:739
  38.8 40.6 %all_to_all.50 = bf16[32,48,256]{2,1,0:T(8,128)(2,1)} all-to-all(bf16[32,48,256]{2,1,0:T(8,128)(2,1)} %bitcast.493), channel_id=1, replica_groups=mesh['blk'=16,'rep'=2] {'blk','rep'}, dimensions={0} | all-to-all | bytes 1572864 | tf_op jit(solution)/shard_map/all_to_all | solution.py:1356
  79.5 14.7 %all-gather.6.cloned.1.call-done.gathered = bf16[112,128,256]{2,1,0:T(8,128)(2,1)} async-done(((bf16[7,128,256]{2,1,0:T(8,128)(2,1)}), bf16[112,128,256]{2,1,0:T(8,128)(2,1)}) %all-gather.6.cloned.1.call-update) | async-done | bytes 7340048 | tf_op jit(solution)/shard_map/all_gather | solution.py:1359
  94.2 6.0 %forward.1 = (bf16[128,384]{1,0:T(8,128)(2,1)}, bf16[1280,256]{1,0:T(8,128)(2,1)}, f32[1280,256]{1,0:T(8,128)}, f32[1280,128]{1,0:T(8,128)}, f32[32,1280]{1,0:T(8,128)}, /*index=5*/f32[208,256]{1,0:T(8,128)}) custom-call(s32[256]{0:T(256)S(1)} %get-tuple-element.802.tab, s32[1,2]{1,0:T(1,128)S(1)} %copy-done.165, s32[1,2]{1,0:T(1,128)S(1)} %copy-done.127, ...), custom_call_target="tpu_custom_call" | custom-call | tf_op jit(solution)/shard_map/forward/pallas_call | solution.py:865
  100.2 11.6 %all_to_all.51 = bf16[16,8,384]{2,1,0:T(8,128)(2,1)} all-to-all(bf16[16,8,384]{2,1,0:T(8,128)(2,1)} %bitcast.550), channel_id=1, replica_groups=mesh['blk'=16,'rep'=2] {'blk'}, dimensions={0} | all-to-all | bytes 196608 | tf_op jit(solution)/shard_map/all_to_all | solution.py:1356
  111.7 11.1 %backward.1 = (bf16[32,208,128]{2,1,0:T(8,128)(2,1)}, f32[1,1]{1,0:T(1,128)}, f32[1,1]{1,0:T(1,128)}) custom-call(s32[256]{0:T(256)S(1)} %get-tuple-element.802.tab, s32[2]{0:T(128)S(1)} %pad_add_fusion.me, s32[6]{0:T(128)S(1)} %copy-done.131, f32[6]{0:T(128)S(1)} %copy-done.134, bf16[128,384]{1,0:T(8,128)(2,1)} %bitcast.534, s32[32,128]{1,0:T(8,128)} %bitcast.531, ...), custom_call_target="tpu_custom_call" | custom-call | tf_op jit(solution)/shard_map/backward/pallas_call | solution.py:1117
  122.9 0.0 copy-start.64
  122.9 0.0 copy-start.67
  122.9 0.0 copy-start.70
  122.9 0.0 copy-start.74
  122.9 0.0 copy-start.162
  122.9 3.8 %all-to-all-start.3 = ((bf16[32,208,128]{2,1,0:T(8,128)(2,1)}), bf16[32,208,128]{2,1,0:T(8,128)(2,1)}, u32[]{:S(2)}, u32[]{:S(2)}) async-start(bf16[32,208,128]{2,1,0:T(8,128)(2,1)} %get-tuple-element.278), calls=%async_computation.4 | async-start | bytes 3407872 | tf_op jit(solution)/shard_map/all_to_all | solution.py:1356
  126.7 0.7 reshape.1017.asked
  127.4 39.4 %all-to-all-done.3.payload = bf16[32,208,128]{2,1,0:T(8,128)(2,1)} async-done(((bf16[32,208,128]{2,1,0:T(8,128)(2,1)}), bf16[32,208,128]{2,1,0:T(8,128)(2,1)}, u32[]{:S(2)}, u32[]{:S(2)}) %all-to-all-start.3) | async-done | bytes 1703968 | tf_op jit(solution)/shard_map/all_to_all | solution.py:1356
  166.8 6.7 %reduce.41 = (bf16[17,64,256]{2,1,0:T(8,128)(2,1)S(1)}, bf16[512,384]{1,0:T(8,128)(2,1)}) custom-call(s32[256]{0:T(256)S(1)} %get-tuple-element.802.tab, s32[2]{0:T(128)S(1)} %pad_add_fusion.me, f32[1,1]{1,0:T(1,128)} %get-tuple-element.277.loss, s32[1,1536]{1,0:T(1,128)} %reshape.1017.asked, bf16[32,208,128]{2,1,0:T(8,128)(2,1)} %all-to-all-done.3.payload), custom_call_target="tpu_custom_call" | custom-call | tf_op jit(solution)/shard_map/reduce/pallas_call | solution.py:1222
  173.4 3.1 %all-to-all-start.4 = ((bf16[32,16,384]{2,1,0:T(8,128)(2,1)}), bf16[32,16,384]{2,1,0:T(8,128)(2,1)S(1)}, u32[]{:S(2)}, u32[]{:S(2)}) async-start(bf16[32,16,384]{2,1,0:T(8,128)(2,1)} %bitcast.535), calls=%async_computation.5 | async-start | bytes 786432 | tf_op jit(solution)/shard_map/all_to_all | solution.py:1356
  176.5 1.8 collective-permute-start
  178.3 0.7 slice_reduce_fusion
  179.7 15.9 %collective-permute-done = bf16[17,64,256]{2,1,0:T(8,128)(2,1)} collective-permute-done((bf16[17,64,256]{2,1,0:T(8,128)(2,1)S(1)}, bf16[17,64,256]{2,1,0:T(8,128)(2,1)}, u32[]{:S(2)}, u32[]{:S(2)}) %collective-permute-start) | collective-permute-done | bytes 557088 | tf_op jit(solution)/shard_map/ppermute | solution.py:1377
  195.6 13.7 %conditional.1 = (f32[17,128,256]{2,1,0:T(8,128)}, f32[17,128,256]{2,1,0:T(8,128)}, f32[17,128,256]{2,1,0:T(8,128)}, f32[16,256]{1,0:T(8,128)}, f32[16,256]{1,0:...) conditional(s32[]{:T(128)} %convert_element_type.235, (bf16[32,16,384]{2,1,0:T(8,128)(2,1)S(1)}, ...), branch_computations={%region_1.0_spmd, %region_2.92_spmd} | conditional | flops 7291003904 | bytes 1166460160 | solution.py:1395
  195.7 13.4 %update.1 = (f32[17,128,256]{2,1,0:T(8,128)}, f32[17,128,256]{2,1,0:T(8,128)}, f32[17,128,256]{2,1,0:T(8,128)}, f32[16,256]{1,0:T(8,128)}, f32[16,256]{1,0:T(8,1...) custom-call(s32[256]{0:T(256)S(1)} %get-tuple-element.181.tab, s32[2]{0:T(128)S(1)} %get-tuple-element.182.me, ...), custom_call_target="tpu_custom_call" | custom-call | tf_op jit(solution)/shard_map/cond/branch_0_fun/update/pallas_call | solution.py:1330
  (18 shorter events, 0.0 us)
Async XLA Ops:
  7.2 28.0 %copy-start.2 = (f32[17,128,256]{2,1,0:T(8,128)S(1)}, f32[17,128,256]{2,1,0:T(8,128)}, u32[]{:S(2)}) copy-start(f32[17,128,256]{2,1,0:T(8,128)} %weights.3) | copy-start | bytes 6684676
  7.2 87.0 %copy-start.165 = (s32[1,2]{1,0:T(1,128)S(1)}, s32[1,2]{1,0:T(1,128)}, u32[]{:S(2)}) copy-start(s32[1,2]{1,0:T(1,128)} %query_lengths.3) | copy-start | bytes 28
  7.2 87.0 %copy-start.127 = (s32[1,2]{1,0:T(1,128)S(1)}, s32[1,2]{1,0:T(1,128)}, u32[]{:S(2)}) copy-start(s32[1,2]{1,0:T(1,128)} %passage_lengths.3) | copy-start | bytes 28
  7.2 87.0 %copy-start.128 = (s32[1,2]{1,0:T(1,128)S(1)}, s32[1,2]{1,0:T(1,128)}, u32[]{:S(2)}) copy-start(s32[1,2]{1,0:T(1,128)} %positive.3) | copy-start | bytes 28
  7.2 86.9 %copy-start.52 = (f32[16,256]{1,0:T(8,128)S(1)}, f32[16,256]{1,0:T(8,128)}, u32[]{:S(2)}) copy-start(f32[16,256]{1,0:T(8,128)} %vectors.3) | copy-start | bytes 49156
  7.2 86.9 %all-gather.6.cloned.1.call-start = ((), (), s32[]{:S(2)}) async-start(), calls=%async_computation.9 | async-start | bytes 7798784 | tf_op jit(solution)/shard_map/all_gather | solution.py:1359
  79.5 32.3 %copy-start.131 = (s32[6]{0:T(128)S(1)}, s32[6]{0:T(128)}, u32[]{:S(2)}) copy-start(s32[6]{0:T(128)} %prefix_lengths.1) | copy-start | bytes 76
  79.5 32.3 %copy-start.134 = (f32[6]{0:T(128)S(1)}, f32[6]{0:T(128)}, u32[]{:S(2)}) copy-start(f32[6]{0:T(128)} %prefix_weights.1) | copy-start | bytes 76
  111.7 14.9 %copy-start.55 = (s32[32,1,128]{2,1,0:T(1,128)S(1)}, s32[32,1,128]{2,1,0:T(1,128)}, u32[]{:S(2)}) copy-start(s32[32,1,128]{2,1,0:T(1,128)} %all_to_all.49) | copy-start | bytes 49156
  122.9 72.8 %copy-start.64 = (f32[16,256]{1,0:T(8,128)S(1)}, f32[16,256]{1,0:T(8,128)}, u32[]{:S(2)}) copy-start(f32[16,256]{1,0:T(8,128)} %param.46) | copy-start | bytes 49156
  122.9 72.7 %copy-start.67 = (f32[16,256]{1,0:T(8,128)S(1)}, f32[16,256]{1,0:T(8,128)}, u32[]{:S(2)}) copy-start(f32[16,256]{1,0:T(8,128)} %param.47) | copy-start | bytes 49156
  122.9 72.7 %copy-start.70 = (s32[1,2,512]{2,1,0:T(2,128)S(1)}, s32[1,2,512]{2,1,0:T(2,128)}, u32[]{:S(2)}) copy-start(s32[1,2,512]{2,1,0:T(2,128)} %param.35) | copy-start | bytes 12292
  122.9 72.7 %copy-start.74 = (s32[269]{0:T(512)S(1)}, s32[269]{0:T(512)}, u32[]{:S(2)}) copy-start(s32[269]{0:T(512)} %owners.3) | copy-start | bytes 3232
  122.9 72.7 %copy-start.162 = (s32[1,2,128]{2,1,0:T(2,128)S(1)}, s32[1,2,128]{2,1,0:T(2,128)}, u32[]{:S(2)}) copy-start(s32[1,2,128]{2,1,0:T(2,128)} %param.34) | copy-start | bytes 3076
  122.9 43.8 %all-to-all-start.3 = ((bf16[32,208,128]{2,1,0:T(8,128)(2,1)}), bf16[32,208,128]{2,1,0:T(8,128)(2,1)}, u32[]{:S(2)}, u32[]{:S(2)}) async-start(bf16[32,208,128]{2,1,0:T(8,128)(2,1)} %get-tuple-element.278), calls=%async_computation.4 | async-start | bytes 3407872 | tf_op jit(solution)/shard_map/all_to_all | solution.py:1356
  173.4 22.2 %all-to-all-start.4 = ((bf16[32,16,384]{2,1,0:T(8,128)(2,1)}), bf16[32,16,384]{2,1,0:T(8,128)(2,1)S(1)}, u32[]{:S(2)}, u32[]{:S(2)}) async-start(bf16[32,16,384]{2,1,0:T(8,128)(2,1)} %bitcast.535), calls=%async_computation.5 | async-start | bytes 786432 | tf_op jit(solution)/shard_map/all_to_all | solution.py:1356
  176.5 19.1 %collective-permute-start = (bf16[17,64,256]{2,1,0:T(8,128)(2,1)S(1)}, bf16[17,64,256]{2,1,0:T(8,128)(2,1)}, u32[]{:S(2)}, u32[]{:S(2)}) collective-permute-start(bf16[17,64,256]{2,1,0:T(8,128)(2,1)S(1)} %get-tuple-element.804), channel_id=1, source_target_pairs={{0,1},{1,0},{2,3},{3,2},{4,5},{5,4},{6,7},{7,6},{8,9},{9,8},{10,11... | collective-permute-start | bytes 1671176 | tf_op jit(solution)/shard_map/ppermute | solution.py:1377
Sparse Core Ops, SparseCore 0:
  12.6 81.5 all-gather.5

commit v2 on v1

--- a/solution.py
+++ b/solution.py
@@ -327,6 +327,24 @@
     return (weight - step_rate * (update + decay_rate * weight), moment_one, moment_two)
 
 
+def gather_all(values, axes):
+    count = lax.axis_size(axes)
+    copies = jnp.broadcast_to(values[None], (count,) + values.shape)
+    return lax.all_to_all(copies, axes, 0, 0, tiled=True).reshape((-1,) + values.shape[1:])
+
+
+def sum_all(values, axes):
+    count = lax.axis_size(axes)
+    copies = jnp.broadcast_to(values[None], (count,) + values.shape)
+    return jnp.sum(lax.all_to_all(copies, axes, 0, 0, tiled=True), 0)
+
+
+def sum_share(values, axes):
+    count = lax.axis_size(axes)
+    parts = lax.all_to_all(values, axes, 0, 0, tiled=True)
+    return jnp.sum(parts.reshape((count, -1) + values.shape[1:]), 0)
+
+
 def local(
     query_ids,
     passage_ids,
@@ -344,13 +362,13 @@
     vector_second,
 ):
     slot_count, unit_rows = (weights.shape[0], weights.shape[1])
-    gathered = lax.all_gather(weights.astype(jnp.bfloat16), "blk", axis=0, tiled=True)
+    gathered = gather_all(weights.astype(jnp.bfloat16), "blk")
     flat_rows = jnp.take(gathered, owners, axis=0).reshape(-1, D)
     query_pooled, query_kept = embed_sequences(flat_rows, vectors, query_ids[0], query_lengths[0])
     passage_pooled, passage_kept = embed_sequences(
         flat_rows, vectors, passage_ids[0], passage_lengths[0]
     )
-    all_passages = lax.all_gather(passage_pooled.astype(jnp.bfloat16), "blk", axis=0, tiled=True)
+    all_passages = gather_all(passage_pooled.astype(jnp.bfloat16), "blk")
     prefix_masks = (jnp.arange(D)[None, :] < prefix_lengths[:, None]).astype(jnp.float32)
     prefix_scale = TEMPER * lax.rsqrt(prefix_lengths.astype(jnp.float32))
     queries = query_pooled.astype(jnp.bfloat16).astype(jnp.float32)
@@ -365,7 +383,7 @@
     per_query = jnp.sum(prefix_weights[:, None] * running_totals, 0)
     loss_part = jnp.sum(jnp.where(counted, per_query, 0.0))
     count_part = jnp.sum(counted.astype(jnp.float32))
-    count_total, loss_total = lax.psum((count_part, loss_part), ("blk", "rep"))
+    count_total, loss_total = sum_all(jnp.stack([count_part, loss_part]), ("blk", "rep"))
     row_factor = (prefix_weights * prefix_scale / count_total)[:, None, None] * counted.astype(
         jnp.float32
     )[None, :, None]
@@ -375,11 +393,8 @@
         * prefix_masks[:, None, :],
         0,
     )
-    grad_passage = lax.psum_scatter(
-        jnp.einsum("mpj,mpd->jd", grad_logits, masked, precision=HIGHEST),
-        "blk",
-        scatter_dimension=0,
-        tiled=True,
+    grad_passage = sum_share(
+        jnp.einsum("mpj,mpd->jd", grad_logits, masked, precision=HIGHEST), "blk"
     )
     flat_query, vec_query = encode_back(
         grad_query, query_pooled, flat_rows, vectors, query_ids[0], query_lengths[0], query_kept
@@ -393,16 +408,16 @@
         passage_lengths[0],
         passage_kept,
     )
-    vec_total = lax.psum(vec_query + vec_pass, ("blk", "rep"))
+    vec_total = sum_all(vec_query + vec_pass, ("blk", "rep"))
     buffer = (
         jnp.zeros((lax.axis_size("blk") * slot_count, unit_rows, D), jnp.float32)
         .at[owners]
         .set((flat_query + flat_pass).reshape(-1, unit_rows, D))
     )
     vec_square = jnp.sum(vec_total * vec_total)
-    reduced = lax.psum_scatter(buffer, "blk", scatter_dimension=0, tiled=True)
-    reduced = lax.psum(reduced, "rep")
-    square_sum = lax.psum(jnp.sum(reduced * reduced), "blk")
+    reduced = sum_share(buffer, "blk")
+    reduced = sum_all(reduced, "rep")
+    square_sum = sum_all(jnp.sum(reduced * reduced)[None], "blk")[0]
     old_weight, old_first, old_second = (weights, first_moments, second_moments)
     slot_ids = lax.axis_index("blk") * slot_count + jnp.arange(slot_count)
     owned_mask = jnp.any(slot_ids[:, None] == owners[None, :], 1)[:, None, None]
@@ -444,7 +459,11 @@
 UNITS_L = 12
 L_ROWS = 4 * UNITS_L
 NEVER = -1e30
-PARAMS = pltpu.CompilerParams(vmem_limit_bytes=56 << 20)
+
+
+def params(n_blk, small):
+    return pltpu.CompilerParams(vmem_limit_bytes=(small if n_blk <= 16 else 58) << 20)
+
 
 AT_POOL = PLEN
 AT_Q = AT_POOL + D
@@ -454,8 +473,14 @@
 AT_UP = AT_O + D
 AT_DOWN = AT_UP + FF
 
-TAB_PLACE, TAB_OWNER, TAB_UNIT, TAB_SLOT, TAB_KIND, TAB_FLAG = 0, 32, 64, 96, 128, 160
-TAB_SIZE = 256
+TAB_OWNER, TAB_RANK, TAB_SLOT, TAB_UNIT, TAB_KIND, TAB_ORDER = range(6)
+PIECE = 16
+PIECES = 16
+DENSE_CAP = 8
+CLASS = DENSE // 2
+HELD = DENSE_CAP // 2
+AT_ASKED = DENSE_CAP // 4 * PIECE
+MESSAGE_ROWS = AT_ASKED + 16
 
 KIND_TABLE, KIND_PLACE, KIND_DENSE = 1, 2, 8
 
@@ -517,121 +542,128 @@
     return sequence, lane < end
 
 
-def prepare_kernel(slots, cap, owners, me, weights, dense_out, tab, counts, units, block, sems):
-    n_units = owners.shape[0]
-    n_blk = counts.shape[0]
-
-    def clear(i, c):
-        counts[i] = 0
-        units[i] = 0
-        return c
-
-    lax.fori_loop(0, n_blk, clear, 0)
-
-    def wipe(i, c):
-        tab[i] = 0
-        return c
-
-    lax.fori_loop(0, TAB_SIZE, wipe, 0)
-    mine = me[0]
-    base = n_units - DENSE
-
-    def place(b, c):
-        slot = owners[base + b]
-        owner = slot // slots
-        inside = slot - owner * slots
-        rank = counts[owner]
-        counts[owner] = rank + 1
-        tab[TAB_PLACE + b] = owner * cap + jnp.minimum(rank, cap - 1)
-        tab[TAB_OWNER + b] = owner
-        tab[TAB_SLOT + b] = inside
-        tab[TAB_FLAG] = jnp.maximum(tab[TAB_FLAG], (rank >= cap).astype(I32))
-
-        @pl.when((owner == mine) & (rank < cap))
-        def _():
-            pltpu.make_async_copy(weights.at[inside], block.at[rank], sems.at[rank]).start()
-
-        return c
-
-    lax.fori_loop(0, DENSE, place, 0)
-    have = counts[mine]
-    for c in range(cap):
-
-        @pl.when(c < have)
-        def _():
-            pltpu.make_async_copy(weights.at[0], block.at[c], sems.at[c]).wait()
-            dense_out[c] = block[c].astype(BF16)
-
-        @pl.when(c >= have)
-        def _():
-            dense_out[c] = jnp.zeros((UNIT, D), BF16)
-
-
-def prepare(owners, me, weights, n_blk, cap):
-    slots = weights.shape[0]
-    return pl.pallas_call(
-        partial(prepare_kernel, slots, cap),
-        out_shape=(
-            jax.ShapeDtypeStruct((cap, UNIT, D), BF16),
-            jax.ShapeDtypeStruct((TAB_SIZE,), I32),
-        ),
-        in_specs=[smem, smem, hbm],
-        out_specs=(vmem, smem),
-        scratch_shapes=[
-            pltpu.SMEM((n_blk,), I32),
-            pltpu.SMEM((n_blk,), I32),
-            pltpu.VMEM((cap, UNIT, D), F32),
-            pltpu.SemaphoreType.DMA((cap,)),
-        ],
-        compiler_params=PARAMS,
-        name="prepare",
-    )(owners, me, weights)
+def across(values, n_blk, step):
+    pairs = [(i, i // PIECES * PIECES + step(i % PIECES)) for i in range(n_blk)]
+    return lax.ppermute(values, "blk", pairs)
+
+
+def along_z(mine, n_blk):
+    return jnp.stack(
+        [mine] + [across(mine, n_blk, lambda i, k=k: (i + 4 * k) % PIECES) for k in (1, 2, 3)]
+    )
+
+
+def spread(first, n_blk):
+    arrays = [first, lax.ppermute(first, "rep", [(0, 1), (1, 0)])]
+    arrays = arrays + [across(a, n_blk, lambda i: i ^ 2) for a in arrays]
+    return arrays + [across(a, n_blk, lambda i: i ^ 1) for a in arrays]
+
+
+def piece_copies(me, gathered, matrices, sems):
+    copies = []
+    for part, array in enumerate(gathered):
+        low = (me[0] % 4) ^ (part & 2) ^ (part // 4)
+        odd = me[1] ^ (part % 2)
+        for k in range(4):
+            p = low + (me[0] % PIECES // 4 * 4 + 4 * (4 - k)) % PIECES
+            row = pl.multiple_of((p % 8) * PIECE, PIECE)
+            lane = pl.multiple_of((p // 8) * 128, 128)
+            copies.append(
+                pltpu.make_async_copy(
+                    array.at[k],
+                    matrices.at[:, odd, pl.ds(row, PIECE), pl.ds(lane, 128)],
+                    sems.at[4 * part + k],
+                )
+            )
+    return copies
+
+
+def rows_at(matrices, tab, start, stop):
+    blocks = []
+    for b in range(start // UNIT, stop // UNIT):
+        order = tab[b, TAB_ORDER]
+        blocks.append(matrices[order // 2, order % 2])
+    return jnp.concatenate(blocks, 0)
+
+
+def owner_of(slot, slots, n_blk):
+    owner = jnp.zeros(slot.shape, I32)
+    for k in range(1, n_blk):
+        owner = owner + (slot >= k * slots).astype(I32)
+    return owner
 
 
 def request_kernel(
-    slots, n_blk, cap, owners, tab_in, me, positive, query_lengths, passage_lengths, owner_row,
-    query_ids, passage_ids, message, where_row, tab, ids, units,
+    slots, n_blk, cap, owners, me, positive, query_lengths, passage_lengths, owner_line,
+    query_ids, passage_ids, weights, message, where_row, tab, ids, owner_row, loaded, sems,
 ):
     n_rep = 2
     n_dest = n_blk * n_rep
-    mine = me[0]
     n_units = owners.shape[0]
-
-    def copy(i, c):
-        tab[i] = tab_in[i]
-        return c
-
-    lax.fori_loop(0, TAB_SIZE, copy, 0)
-
-    def clear(i, c):
-        units[i] = 0
-        return c
-
-    lax.fori_loop(0, n_blk, clear, 0)
-
-    def kind(b, c):
-        inside = owners[b] - mine * slots
-
-        @pl.when((inside >= 0) & (inside < slots))
+    start = me[0] * slots
+
+    def take(b, carry):
+        before, have = carry
+        slot = owners[n_units - DENSE + b]
+        inside = slot - start
+        mine = (inside >= 0) & (inside < slots)
+
+        @pl.when(mine & (have // 2 % 2 == me[1]) & (have < DENSE_CAP))
         def _():
-            tab[TAB_KIND + inside] = jnp.where(
-                b < TABLE_BLOCKS,
-                KIND_TABLE,
+            spot = have // 4 * 2 + have % 2
+            pltpu.make_async_copy(weights.at[inside], loaded.at[spot], sems.at[spot]).start()
+
+        return before + (slot < start).astype(I32), have + mine.astype(I32)
+
+    before, have = lax.fori_loop(0, DENSE, take, (0, 0))
+    owner_row[...] = jnp.full(owner_row.shape, -1, I32)
+    owner_row[:, :n_units] = owner_line[...]
+    every_slot = owner_row[...]
+    wide = every_slot.shape[1]
+    base = n_units - DENSE
+    low = base // 128 * 128
+    rolled = pltpu.roll(every_slot[:, low:], wide - low - (base - low), 1)[:, :128]
+    dense_owner = owner_of(rolled, slots, n_blk)
+    owner_column = to_column(dense_owner)[:32]
+    slot_column = to_column(rolled)[:32]
+    block_row = iota((32, 128), 1)
+    block_column = iota((32, 128), 0)
+    same = (owner_column == dense_owner) & (block_row < block_column) & (block_row < DENSE)
+    rank = jnp.sum(same.astype(I32), 1, keepdims=True)
+    at = block_row * UNIT
+    need = jnp.where(block_row < PLACE_BLOCKS, 0, jnp.where((at >= AT_K) & (at < AT_O), 2, 1))
+    unit = jnp.sum(jnp.where(same, need, 0), 1, keepdims=True)
+    lower = (dense_owner < owner_column) & (block_row < DENSE)
+    order = rank + jnp.sum(lower.astype(I32), 1, keepdims=True)
+    crowded = jnp.max(((rank >= DENSE_CAP) & (iota((32, 1), 0) < DENSE)).astype(I32))
+    which = iota((32, wide), 1)
+    code = jnp.where(
+        which < TABLE_BLOCKS,
+        KIND_TABLE,
+        jnp.where(
+            which < TABLE_BLOCKS + PLACE_BLOCKS, KIND_PLACE + which - TABLE_BLOCKS, KIND_DENSE
+        ),
+    )
+    here = (every_slot == me[0] * slots + iota((32, wide), 0)) & (which < n_units)
+    kind = jnp.sum(jnp.where(here, code, 0), 1, keepdims=True)
+    entry = block_row
+    tab[...] = jnp.where(
+        entry == TAB_OWNER,
+        owner_column,
+        jnp.where(
+            entry == TAB_RANK,
+            jnp.minimum(rank, DENSE_CAP - 1),
+            jnp.where(
+                entry == TAB_SLOT,
+                slot_column - owner_column * slots,
                 jnp.where(
-                    b < TABLE_BLOCKS + PLACE_BLOCKS, KIND_PLACE + b - TABLE_BLOCKS, KIND_DENSE
+                    entry == TAB_UNIT,
+                    jnp.minimum(unit, UNITS_L - 2),
+                    jnp.where(entry == TAB_KIND, kind, jnp.minimum(order, DENSE - 1)),
                 ),
-            )
-
-        return c
-
-    lax.fori_loop(0, n_units, kind, 0)
-    for b in range(PLACE_BLOCKS, DENSE):
-        owner = tab_in[TAB_OWNER + b]
-        used = units[owner]
-        need = 2 if AT_K <= b * UNIT < AT_O else 1
-        units[owner] = used + need
-        tab[TAB_UNIT + b] = jnp.minimum(used, UNITS_L - need)
-        tab[TAB_FLAG] = jnp.maximum(tab[TAB_FLAG], (used + need > UNITS_L).astype(I32))
+            ),
+        ),
+    )
 
     ids[:, 0:QROWS] = query_ids[0:1]
     ids[:, QROWS : 2 * QROWS] = query_ids[1:2]
@@ -647,9 +679,7 @@
         column = to_column(owner_row[:, at : at + 128])
         hit = (iota((128, TOKENS), 0) + at) == block
         slot = slot + jnp.sum(jnp.where(hit, column, 0), 0, keepdims=True)
-    owner = jnp.zeros((1, TOKENS), I32)
-    for k in range(1, n_blk):
-        owner = owner + (slot >= k * slots).astype(I32)
+    owner = owner_of(slot, slots, n_blk)
     inside = slot - owner * slots
     row = token - block * UNIT
     upper = (row >= HALF).astype(I32)
@@ -681,41 +711,105 @@
     spread = (iota((128, TOKENS), 0) == rank).astype(F32).astype(BF16)
     sent_high = dot_nt((chosen * high.astype(F32)).astype(BF16), spread)
     sent_low = dot_nt((chosen * low.astype(F32)).astype(BF16), spread)
-    request = sent_high.astype(I32) * 32 + sent_low.astype(I32) - 1
-    flag = jnp.maximum(over, tab[TAB_FLAG])
-    column_of = iota((n_dest, 128), 1)
-    out = jnp.where(column_of < cap, request, 0)
-    out = jnp.where(column_of == 124, positive[0, 0], out)
-    out = jnp.where(column_of == 125, positive[0, 1], out)
-    message[...] = jnp.where(column_of == 126, flag, out)
-
-
-def request(owners, tab, me, positive, query_lengths, passage_lengths, query_ids, passage_ids, slots, n_blk, cap):
+    flag = jnp.maximum(over, crowded)
+    column_of = iota((1, 128), 1)
+    marks = jnp.where(
+        column_of == 0,
+        positive[0, 0],
+        jnp.where(column_of == 1, positive[0, 1], jnp.where(column_of == 2, flag, 0)),
+    ).astype(F32)
+    row16 = iota((16, 128), 0)
+    for d in range(n_dest):
+        asked = jnp.where(
+            row16 == 0,
+            sent_high[d : d + 1],
+            jnp.where(row16 == 1, sent_low[d : d + 1], jnp.where(row16 == 2, marks, 0.0)),
+        )
+        message[d, AT_ASKED:] = asked.astype(BF16)
+    for spot in range(HELD):
+        present = spot // 2 * 4 + 2 * me[1] + spot % 2 < have
+
+        @pl.when(present)
+        def _():
+            pltpu.make_async_copy(weights.at[0], loaded.at[spot], sems.at[spot]).wait()
+
+        @pl.when(jnp.logical_not(present))
+        def _():
+            loaded[spot] = jnp.zeros((UNIT, D), F32)
+
+    for odd in range(2):
+        for c in range(DENSE_CAP // 4):
+            whole = loaded[2 * c + (odd + before) % 2].astype(BF16)
+            for s in range(n_blk):
+                p = s % PIECES
+                message[2 * s + odd, PIECE * c : PIECE * (c + 1)] = whole[
+                    PIECE * (p % 8) : PIECE * (p % 8 + 1), 128 * (p // 8) : 128 * (p // 8 + 1)
+                ]
+
+
+def request(owners, me, positive, query_lengths, passage_lengths, query_ids, passage_ids, weights, n_blk, cap):
+    slots = weights.shape[0]
     n_dest = 2 * n_blk
-    table_rows = -(-TABLE_BLOCKS // 128) * 128
-    owner_row = owners[:table_rows].reshape(1, table_rows)
+    n_units = owners.shape[0]
+    owner_row = owners.reshape(1, n_units)
     return pl.pallas_call(
         partial(request_kernel, slots, n_blk, cap),
         out_shape=(
-            jax.ShapeDtypeStruct((n_dest, 128), I32),
+            jax.ShapeDtypeStruct((n_dest, MESSAGE_ROWS, 128), BF16),
             jax.ShapeDtypeStruct((1, TOKENS), I32),
-            jax.ShapeDtypeStruct((TAB_SIZE,), I32),
+            jax.ShapeDtypeStruct((32, 128), I32),
         ),
-        in_specs=[smem, smem, smem, smem, smem, smem, vmem, vmem, vmem],
-        out_specs=(vmem, vmem, smem),
-        scratch_shapes=[pltpu.VMEM((1, TOKENS), I32), pltpu.SMEM((n_blk,), I32)],
-        compiler_params=PARAMS,
+        in_specs=[smem] * 5 + [vmem] * 3 + [hbm],
+        out_specs=(vmem, vmem, vmem),
+        scratch_shapes=[
+            pltpu.VMEM((1, TOKENS), I32),
+            pltpu.VMEM((1, -(-n_units // 128) * 128), I32),
+            pltpu.VMEM((HELD, UNIT, D), F32),
+            pltpu.SemaphoreType.DMA((HELD,)),
+        ],
+        compiler_params=params(n_blk, 12),
         name="request",
-    )(owners, tab, me, positive, query_lengths, passage_lengths, owner_row, query_ids, passage_ids)
-
-
-def fetch_kernel(slots, cap, me, message, weights, rows_out, held, table, hot, sem):
+    )(owners, me, positive, query_lengths, passage_lengths, owner_row, query_ids, passage_ids, weights)
+
+
+def collect_kernel(tab, me, message, mine_out):
+    for b in range(DENSE):
+        order = tab[b, TAB_ORDER]
+        rank = tab[b, TAB_RANK]
+
+        @pl.when(order % 2 == me[1])
+        def _():
+            spot = pl.multiple_of(rank // 4 * PIECE, PIECE)
+            sender = 2 * tab[b, TAB_OWNER] + rank // 2 % 2
+            mine_out[order // 2] = message[sender, pl.ds(spot, PIECE), :]
+
+
+def collect(tab, me, message):
+    return pl.pallas_call(
+        collect_kernel,
+        out_shape=jax.ShapeDtypeStruct((CLASS, PIECE, 128), BF16),
+        in_specs=[smem, smem, vmem],
+        out_specs=vmem,
+        compiler_params=params(message.shape[0] // 2, 2),
+        name="collect",
+    )(tab, me, message)
+
+
+def fetch_kernel(slots, cap, me, message, weights, rows_out, asked_out, held, table, hot, sem):
     n_dest = message.shape[0]
-    half = me[1]
-    copy = pltpu.make_async_copy(weights.at[:, pl.ds(half * HALF, HALF), :], held, sem)
+    copy = pltpu.make_async_copy(weights.at[:, pl.ds(me[1] * HALF, HALF), :], held, sem)
     copy.start()
+    column_of = iota((1, 128), 1)
+    for s in range(n_dest):
+        part = message[s, AT_ASKED:].astype(F32)
+        wanted = part[0:1] * 32.0 + part[1:2] - 1.0
+        marks = part[2:3]
+        row = jnp.where(column_of < cap, wanted, 0.0)
+        for i in range(3):
+            row = jnp.where(column_of == 124 + i, marks[:, i : i + 1], row)
+        asked_out[s : s + 1] = row.astype(I32)
     wide = table.shape[0]
-    rows = message[...]
+    rows = asked_out[...]
     pad = -n_dest % 128
     if pad:
         rows = jnp.concatenate([rows, jnp.zeros((pad, 128), I32)], 0)
@@ -738,16 +832,19 @@
     wide = -(-slots * HALF // 128) * 128
     return pl.pallas_call(
         partial(fetch_kernel, slots, cap),
-        out_shape=jax.ShapeDtypeStruct((n_dest * cap, D), BF16),
+        out_shape=(
+            jax.ShapeDtypeStruct((n_dest * cap, D), BF16),
+            jax.ShapeDtypeStruct((n_dest, 128), I32),
+        ),
         in_specs=[smem, vmem, hbm],
-        out_specs=vmem,
+        out_specs=(vmem, vmem),
         scratch_shapes=[
             pltpu.VMEM((slots, HALF, D), F32),
             pltpu.VMEM((wide, D), BF16),
             pltpu.VMEM((n_dest * cap, wide), BF16),
             pltpu.SemaphoreType.DMA,
         ],
-        compiler_params=PARAMS,
+        compiler_params=params(n_dest // 2, 16),
         name="fetch",
     )(me, message, weights)
 
@@ -757,34 +854,24 @@
 ST_ROWS = 208
 
 
-def start_matrices(tab, gathered, matrices, sems, first=0):
-    for b in range(first, DENSE):
-        pltpu.make_async_copy(
-            gathered.at[tab[TAB_PLACE + b]], matrices.at[pl.ds(b * UNIT, UNIT)], sems.at[b]
-        ).start()
-
-
-def wait_matrices(gathered, matrices, sems, first=0):
-    for b in range(first, DENSE):
-        pltpu.make_async_copy(
-            gathered.at[0], matrices.at[pl.ds(b * UNIT, UNIT)], sems.at[b]
-        ).wait()
-
-
 def forward_kernel(
-    tab, query_lengths, passage_lengths, positive, rows, where_row, vectors, gathered,
-    emb_out, low_out, normed_out, scale_out, probs_out, state, matrices, embedded, sems,
+    tab, me, query_lengths, passage_lengths, positive, rows, where_row, vectors, g0, g1, g2, g3,
+    g4, g5, g6, g7, emb_out, low_out, normed_out, scale_out, probs_out, state, matrices, embedded,
+    sems,
 ):
-    start_matrices(tab, gathered, matrices, sems)
+    copies = piece_copies(me, (g0, g1, g2, g3, g4, g5, g6, g7), matrices, sems)
+    for copy in copies:
+        copy.start()
     taken = rows.shape[0]
     for at in range(0, TOKENS, 128):
         column = to_column(where_row[:, at : at + 128])
         hot = (iota((128, taken), 1) == column).astype(F32).astype(BF16)
         embedded[at : at + 128] = dot_nn(hot, rows[...])
-    wait_matrices(gathered, matrices, sems)
+    for copy in copies:
+        copy.wait()
     shift = vectors[0:1]
     for start, length in zip(STARTS, (QROWS, QROWS, PLEN, PLEN)):
-        e = embedded[start : start + length] + matrices[:length].astype(F32) + shift
+        e = embedded[start : start + length] + rows_at(matrices, tab, 0, length).astype(F32) + shift
         centred = e - jnp.mean(e, -1, keepdims=True)
         scale = lax.rsqrt(jnp.mean(centred * centred, -1, keepdims=True) + NORM_EPS)
         normed = centred * scale
@@ -797,12 +884,12 @@
         [embedded[s : s + 1] for s in STARTS] + [jnp.zeros((4, D), F32)], 0
     )
     x0_low = x0.astype(BF16)
-    q = (dot_nn(x0_low, matrices[AT_Q:AT_K]) + vectors[4:5]).astype(BF16)
+    q = (dot_nn(x0_low, rows_at(matrices, tab, AT_Q, AT_K)) + vectors[4:5]).astype(BF16)
     head_of = iota((8, D), 1) // HALF
     q_heads = jnp.concatenate(
         [jnp.where(head_of == h, q.astype(F32), 0.0) for h in range(HEADS)], 0
     ).astype(BF16)
-    kq = dot_nt(q_heads, matrices[AT_K:AT_V]) * (D // HEADS) ** (-0.5)
+    kq = dot_nt(q_heads, rows_at(matrices, tab, AT_K, AT_V)) * (D // HEADS) ** (-0.5)
     low = low_out[...]
     scores = fine(dot_nt, kq, low)
     sequence, live = token_facts(query_lengths, passage_lengths)
@@ -814,22 +901,22 @@
     probs = weight / jnp.where(total > 0.0, total, 1.0)
     probs_out[...] = probs
     mixed = dot_nn(probs.astype(BF16), low)
-    valued = fine(dot_nn, mixed, matrices[AT_V:AT_O])
+    valued = fine(dot_nn, mixed, rows_at(matrices, tab, AT_V, AT_O))
     blended = jnp.zeros((8, D), F32)
     for h in range(HEADS):
         blended = blended + jnp.where(head_of == h, valued[8 * h : 8 * h + 8], 0.0)
     real = iota((8, D), 0) < 4
     blended = jnp.where(real, blended + vectors[5:6], 0.0).astype(BF16)
-    summed = x0 + dot_nn(blended, matrices[AT_O:AT_UP]) + vectors[6:7]
+    summed = x0 + dot_nn(blended, rows_at(matrices, tab, AT_O, AT_UP)) + vectors[6:7]
     h0, n1, i1 = norm_rows(summed, vectors[8:9], vectors[9:10])
     h_low = h0.astype(BF16)
     bias_up = jnp.concatenate([vectors[12 + i : 13 + i] for i in range(FF // D)], 1)
-    u = dot_nt(h_low, matrices[AT_UP:AT_DOWN]) + bias_up
+    u = dot_nt(h_low, rows_at(matrices, tab, AT_UP, AT_DOWN)) + bias_up
     a = (0.5 * u * (1.0 + lax.erf(u * (0.5**0.5)))).astype(BF16)
-    second = h0 + dot_nn(a, matrices[AT_DOWN:]) + vectors[7:8]
+    second = h0 + dot_nn(a, rows_at(matrices, tab, AT_DOWN, DENSE * UNIT)) + vectors[7:8]
     x, n2, i2 = norm_rows(second, vectors[10:11], vectors[11:12])
     c = x.astype(BF16)
-    pooled = jnp.tanh(dot_nn(c, matrices[AT_POOL:AT_Q]) + vectors[3:4])
+    pooled = jnp.tanh(dot_nn(c, rows_at(matrices, tab, AT_POOL, AT_Q)) + vectors[3:4])
     row8 = iota((8, 128), 0)
     sent = jnp.concatenate(
         [
@@ -861,7 +948,7 @@
     state[ST_I2 : ST_I2 + 8] = jnp.broadcast_to(i2, (8, D))
 
 
-def forward(tab, query_lengths, passage_lengths, positive, rows, where_row, vectors, gathered, n_blk):
+def forward(tab, me, query_lengths, passage_lengths, positive, rows, where_row, vectors, gathered, n_blk):
     return pl.pallas_call(
         forward_kernel,
         out_shape=(
@@ -871,17 +958,20 @@
             jax.ShapeDtypeStruct((TOKENS, 128), F32),
             jax.ShapeDtypeStruct((32, TOKENS), F32),
             jax.ShapeDtypeStruct((ST_ROWS, D), F32),
+            jax.ShapeDtypeStruct((CLASS, 2, UNIT, D), BF16),
         ),
-        in_specs=[smem, smem, smem, smem, vmem, vmem, vmem, hbm],
-        out_specs=(vmem,) * 6,
+        in_specs=[smem] * 5 + [vmem] * 3 + [hbm] * 8,
+        out_specs=(vmem,) * 7,
         scratch_shapes=[
-            pltpu.VMEM((DENSE * UNIT, D), BF16),
             pltpu.VMEM((TOKENS, D), F32),
-            pltpu.SemaphoreType.DMA((DENSE,)),
+            pltpu.SemaphoreType.DMA((2 * PIECES,)),
         ],
-        compiler_params=PARAMS,
+        compiler_params=params(n_blk, 12),
         name="forward",
-    )(tab, query_lengths, passage_lengths, positive, rows, where_row, vectors, gathered)
+    )(
+        tab, me, query_lengths, passage_lengths, positive, rows, where_row, vectors,
+        *[pltpu.with_memory_space_constraint(a, pltpu.HBM) for a in gathered],
+    )
 
 
 def place_rows(n_dest):
@@ -897,10 +987,9 @@
 
 def backward_kernel(
     cap, tab, me, prefix_lengths, prefix_weights, emb, message, where_row, low_in, normed, scale,
-    probs_in, state, vectors, gathered, payload, loss_out, count_out,
-    matrices, received, grad_emb, dx, left, sems,
+    probs_in, state, vectors, matrices, payload, loss_out, count_out,
+    received, grad_emb, dx, left,
 ):
-    start_matrices(tab, gathered, matrices, sems, PLACE_BLOCKS)
     n_blk = emb.shape[0] // 8
     n_dest = 2 * n_blk
     for i in range(3):
@@ -952,44 +1041,43 @@
         + [jnp.zeros((4, D), F32)],
         0,
     )
-    wait_matrices(gathered, matrices, sems, PLACE_BLOCKS)
 
     def kept_rows(at, rows=8):
         return state[at : at + rows]
 
     pooled = kept_rows(ST_POOLED)
     d_pre = grad_pooled * (1.0 - pooled * pooled)
-    d_c = fine(dot_nt, d_pre, matrices[AT_POOL:AT_Q])
+    d_c = fine(dot_nt, d_pre, rows_at(matrices, tab, AT_POOL, AT_Q))
     n2 = kept_rows(ST_N2)
     d_second, d_g2, d_s2 = norm_back(d_c, n2, kept_rows(ST_I2), vectors[10:11])
     down_low = d_second.astype(BF16)
-    d_a = dot_nt(down_low, matrices[AT_DOWN:])
+    d_a = dot_nt(down_low, rows_at(matrices, tab, AT_DOWN, DENSE * UNIT))
     u = jnp.concatenate([kept_rows(ST_U + 8 * i) for i in range(FF // D)], 1)
     slope = 0.5 * (1.0 + lax.erf(u * (0.5**0.5))) + u * jnp.exp(-0.5 * u * u) * (
         0.3989422804014327
     )
     up_low = (d_a * slope).astype(BF16)
-    d_h = d_second + dot_nn(up_low, matrices[AT_UP:AT_DOWN])
+    d_h = d_second + dot_nn(up_low, rows_at(matrices, tab, AT_UP, AT_DOWN))
     d_summed, d_g1, d_s1 = norm_back(d_h, kept_rows(ST_N1), kept_rows(ST_I1), vectors[8:9])
     branch_low = d_summed.astype(BF16)
-    d_o = dot_nt(branch_low, matrices[AT_O:AT_UP]).astype(BF16)
+    d_o = dot_nt(branch_low, rows_at(matrices, tab, AT_O, AT_UP)).astype(BF16)
     head_of = iota((8, D), 1) // HALF
     o_heads = jnp.concatenate(
         [jnp.where(head_of == h, d_o.astype(F32), 0.0) for h in range(HEADS)], 0
     ).astype(BF16)
-    vo = dot_nt(o_heads, matrices[AT_V:AT_O])
+    vo = dot_nt(o_heads, rows_at(matrices, tab, AT_V, AT_O))
     low = low_in[...]
     probs = probs_in[...]
     d_probs = fine(dot_nt, vo, low)
     d_scores = probs * (d_probs - jnp.sum(d_probs * probs, -1, keepdims=True))
     score_low = d_scores.astype(BF16)
     mixed_score = dot_nn(score_low, low)
-    keyed = fine(dot_nn, mixed_score, matrices[AT_K:AT_V])
+    keyed = fine(dot_nn, mixed_score, rows_at(matrices, tab, AT_K, AT_V))
     d_q = jnp.zeros((8, D), F32)
     for h in range(HEADS):
         d_q = d_q + jnp.where(head_of == h, keyed[8 * h : 8 * h + 8], 0.0)
     d_q_low = (d_q * (D // HEADS) ** (-0.5)).astype(BF16)
-    d_x0 = d_summed + dot_nt(d_q_low, matrices[AT_Q:AT_K])
+    d_x0 = d_summed + dot_nt(d_q_low, rows_at(matrices, tab, AT_Q, AT_K))
     kq = kept_rows(ST_KQ, 32)
     vo_high, vo_low = split(vo)
     kq_high, kq_low = split(kq)
@@ -1044,7 +1132,7 @@
     up_f = up_low.astype(F32)
 
     def put(b, r, unit, values):
-        spot = (tab[TAB_OWNER + b] * 2 + r) * L_ROWS + (tab[TAB_UNIT + b] + unit) * 4
+        spot = (tab[b, TAB_OWNER] * 2 + r) * L_ROWS + (tab[b, TAB_UNIT] + unit) * 4
         for i in range(4):
             left[pl.ds(spot + i, 1), :] = values[i : i + 1]
 
@@ -1111,7 +1199,7 @@
         ).astype(BF16)
 
 
-def backward(tab, me, prefix_lengths, prefix_weights, emb, message, where_row, low, normed, scale, probs, state, vectors, gathered, cap):
+def backward(tab, me, prefix_lengths, prefix_weights, emb, message, where_row, low, normed, scale, probs, state, vectors, matrices, cap):
     n_dest = message.shape[0]
     n_rows = payload_rows(n_dest, cap)[-1]
     return pl.pallas_call(
@@ -1121,19 +1209,17 @@
             jax.ShapeDtypeStruct((1, 1), F32),
             jax.ShapeDtypeStruct((1, 1), F32),
         ),
-        in_specs=[smem] * 4 + [vmem] * 9 + [hbm],
+        in_specs=[smem] * 4 + [vmem] * 10,
         out_specs=(vmem, smem, smem),
         scratch_shapes=[
-            pltpu.VMEM((DENSE * UNIT, D), BF16),
             pltpu.VMEM((emb.shape[0] * 3, 128), F32),
             pltpu.VMEM((emb.shape[0], D), F32),
             pltpu.VMEM((TOKENS, D), F32),
             pltpu.VMEM((n_dest * L_ROWS, 128), F32),
-            pltpu.SemaphoreType.DMA((DENSE,)),
         ],
-        compiler_params=PARAMS,
+        compiler_params=params(n_dest // 2, 16),
         name="backward",
-    )(tab, me, prefix_lengths, prefix_weights, emb, message, where_row, low, normed, scale, probs, state, vectors, gathered)
+    )(tab, me, prefix_lengths, prefix_weights, emb, message, where_row, low, normed, scale, probs, state, vectors, matrices)
 
 
 def reduce_kernel(slots, cap, tab, me, loss, asked, payload, reduced, news, total, row_grads, left, right):
@@ -1169,9 +1255,9 @@
         else:
             m = 6
 
-        @pl.when(tab[TAB_OWNER + b] == mine)
+        @pl.when(tab[b, TAB_OWNER] == mine)
         def _():
-            unit = tab[TAB_UNIT + b] * 4
+            unit = tab[b, TAB_UNIT] * 4
             pull = rows_of(right, m * 4, 32)
             if AT_K <= at < AT_O:
                 grad = dot_tn(
@@ -1182,7 +1268,7 @@
                 )
             else:
                 grad = dot_tn(rows_of(left, unit, L_ROWS), pull)
-            spot = pl.multiple_of(tab[TAB_SLOT + b] * HALF, HALF)
+            spot = pl.multiple_of(tab[b, TAB_SLOT] * HALF, HALF)
             total[pl.ds(spot, HALF), :128] = grad[:HALF]
             total[pl.ds(spot, HALF), 128:] = grad[HALF:]
 
@@ -1233,109 +1319,140 @@
             pltpu.VMEM((n_dest * L_ROWS, 128), F32),
             pltpu.VMEM((n_dest * 32, 128), F32),
         ],
-        compiler_params=PARAMS,
+        compiler_params=params(n_dest // 2, 16),
         name="reduce",
     )(tab, me, loss, asked, payload)
+
+
+RING = 4
 
 
 def update_kernel(
     pr, tab, me, news, places, own, other, weight, first, second, vectors, vector_first,
     vector_second, weight_out, first_out, second_out, vectors_out, vector_first_out,
-    vector_second_out, loss_out, norm_out, factor_ref,
+    vector_second_out, loss_out, norm_out, grad, held, done, in_sems, sems,
 ):
-    i = pl.program_id(0)
     n_dest = news.shape[0] // pr
-
-    def strip(row):
-        return news[pl.ds(row, n_dest, stride=pr), D:]
-
-    @pl.when(i == 0)
-    def _():
-        extra = news[...][:, D:].astype(F32).reshape(n_dest, pr, 128)
-        sums = jnp.sum(extra[:, 3:6, :], 0)
-        square = jnp.sum(sums, 0, keepdims=True)
-        norm = jnp.sqrt(square)
-        factor = CLIP_AT / jnp.maximum(norm, CLIP_AT)
-        factor_ref[...] = jnp.broadcast_to(factor, (8, 128))
-        norm_out[0, 0] = norm[0, 0]
-        loss = jnp.sum(extra[0:2, 6:9, :], 0)
-        loss = jnp.sum(loss, 0, keepdims=True)
-        loss_out[0, 0] = loss[0, 0]
-        pieces = jnp.sum(extra[:32, 0:3, :], 1)
-        pairs = pieces.reshape(16, 2, 128)
-        grad = jnp.concatenate([pairs[:, 0], pairs[:, 1]], 1) * factor[0, 0]
-        v, m1, m2 = adam_step(
-            vectors[...], vector_first[...], vector_second[...], grad, VECTOR_RATE, 0.0
-        )
-        vectors_out[...] = v
-        vector_first_out[...] = m1
-        vector_second_out[...] = m2
-
-    kind = tab[TAB_KIND + i]
+    slots = weight.shape[0]
+
+    def in_copies(i):
+        return [
+            pltpu.make_async_copy(a.at[i], held.at[k, i], in_sems.at[k, i])
+            for k, a in enumerate((weight, first, second))
+        ]
+
+    def fetch_one(i, c):
+        for copy in in_copies(i):
+            copy.start()
+        return c
+
+    lax.fori_loop(0, slots, fetch_one, 0)
+    extra = news[:, D:].astype(F32).reshape(n_dest, pr, 128)
+    square = jnp.sum(jnp.sum(extra[:, 3:6, :], 0), 0, keepdims=True)
+    norm = jnp.sqrt(square)
+    factor = CLIP_AT / jnp.maximum(norm, CLIP_AT)
+    norm_out[0, 0] = norm[0, 0]
+    loss = jnp.sum(jnp.sum(extra[0:2, 6:9, :], 0), 0, keepdims=True)
+    loss_out[0, 0] = loss[0, 0]
+    pairs = jnp.sum(extra[:32, 0:3, :], 1).reshape(16, 2, 128)
+    vector_grad = jnp.concatenate([pairs[:, 0], pairs[:, 1]], 1) * factor[:, :1]
+    v, m1, m2 = adam_step(
+        vectors[...], vector_first[...], vector_second[...], vector_grad, VECTOR_RATE, 0.0
+    )
+    vectors_out[...] = v
+    vector_first_out[...] = m1
+    vector_second_out[...] = m2
     flip = me[1] == 0
-    mine = own[0].astype(F32)
-    theirs = other[0].astype(F32)
-    lower = jnp.where(flip, mine, theirs)
-    upper = jnp.where(flip, theirs, mine)
-
-    def step(grad):
-        w, m1, m2 = adam_step(
-            weight[0], first[0], second[0], grad * factor_ref[0:1, 0:1], RATE, DECAY
-        )
-        weight_out[0] = w
-        first_out[0] = m1
-        second_out[0] = m2
-
-    @pl.when(kind == 0)
-    def _():
-        weight_out[0] = weight[0]
-        first_out[0] = first[0]
-        second_out[0] = second[0]
-
-    @pl.when(kind == KIND_TABLE)
-    def _():
-        step(jnp.concatenate([lower, upper], 0))
-
-    @pl.when(kind == KIND_DENSE)
-    def _():
-        step(
-            jnp.concatenate(
-                [
-                    jnp.concatenate([lower[:, :128], lower[:, 128:]], 0),
-                    jnp.concatenate([upper[:, :128], upper[:, 128:]], 0),
-                ],
-                1,
-            )
-        )
-
-    @pl.when((kind >= KIND_PLACE) & (kind < KIND_DENSE))
-    def _():
-        spot = pl.multiple_of((kind - KIND_PLACE) * UNIT, UNIT)
-        step(places[pl.ds(spot, UNIT), :D].astype(F32))
+    scale = jnp.broadcast_to(jnp.concatenate([factor, factor], 1), (UNIT, D))
+    first_scale = -RATE / (1.0 - BETA_ONE**STEP)
+    second_scale = 1.0 / (1.0 - BETA_TWO**STEP)
+
+    def out_copies(i, b):
+        return [
+            pltpu.make_async_copy(done.at[b, k], out.at[i], sems.at[b, k])
+            for k, out in enumerate((weight_out, first_out, second_out))
+        ]
+
+    def one(i, c):
+        kind = tab[i, TAB_KIND]
+        b = lax.rem(i, RING)
+        mine = own[i].astype(F32)
+        theirs = other[i].astype(F32)
+        lower = jnp.where(flip, mine, theirs)
+        upper = jnp.where(flip, theirs, mine)
+
+        @pl.when(kind == KIND_TABLE)
+        def _():
+            grad[:HALF] = lower
+            grad[HALF:] = upper
+
+        @pl.when(kind == KIND_DENSE)
+        def _():
+            grad[:HALF, :128] = lower[:, :128]
+            grad[HALF:, :128] = lower[:, 128:]
+            grad[:HALF, 128:] = upper[:, :128]
+            grad[HALF:, 128:] = upper[:, 128:]
+
+        @pl.when((kind >= KIND_PLACE) & (kind < KIND_DENSE))
+        def _():
+            spot = pl.multiple_of((kind - KIND_PLACE) * UNIT, UNIT)
+            grad[...] = places[pl.ds(spot, UNIT), :D].astype(F32)
+
+        @pl.when(i >= RING)
+        def _():
+            for copy in out_copies(i - RING, b):
+                copy.wait()
+
+        for copy in in_copies(i):
+            copy.wait()
+
+        @pl.when(kind == 0)
+        def _():
+            for k in range(3):
+                done[b, k] = held[k, i]
+
+        @pl.when(kind > 0)
+        def _():
+            g = grad[...] * scale
+            m1 = BETA_ONE * held[1, i] + (1.0 - BETA_ONE) * g
+            m2 = BETA_TWO * held[2, i] + (1.0 - BETA_TWO) * (g * g)
+            root = jnp.sqrt(m2 * second_scale) + EPSILON
+            done[b, 0] = held[0, i] * (1.0 - RATE * DECAY) + (m1 * first_scale) / root
+            done[b, 1] = m1
+            done[b, 2] = m2
+
+        for copy in out_copies(i, b):
+            copy.start()
+        return c
+
+    lax.fori_loop(0, slots, one, 0)
+    for i in range(max(slots - RING, 0), slots):
+        for copy in out_copies(i, i % RING):
+            copy.wait()
 
 
 def update(tab, me, news, own, other, weights, first, second, vectors, vector_first, vector_second, pr):
-    slots = weights.shape[0]
     n_dest = news.shape[0] // pr
     share = PLEN // n_dest
     places = news
     if share < pr:
         places = news.reshape(n_dest, pr, -1)[:, :share].reshape(PLEN, -1)
-    slot = pl.BlockSpec((1, UNIT, D), lambda i: (i, 0, 0))
-    half = pl.BlockSpec((1, HALF, D), lambda i: (i, 0, 0))
-    whole = lambda a: pl.BlockSpec(a.shape, lambda i: (0,) * a.ndim)
     big = jax.ShapeDtypeStruct(weights.shape, F32)
     small = jax.ShapeDtypeStruct(vectors.shape, F32)
     one = jax.ShapeDtypeStruct((1, 1), F32)
     return pl.pallas_call(
         partial(update_kernel, pr),
-        grid=(slots,),
         out_shape=(big, big, big, small, small, small, one, one),
-        in_specs=[smem, smem, whole(news), whole(places), half, half, slot, slot, slot]
-        + [whole(vectors)] * 3,
-        out_specs=(slot, slot, slot) + (whole(vectors),) * 3 + (smem, smem),
-        scratch_shapes=[pltpu.VMEM((8, 128), F32)],
-        compiler_params=PARAMS,
+        in_specs=[smem, smem] + [vmem] * 4 + [hbm] * 3 + [vmem] * 3,
+        out_specs=(hbm, hbm, hbm, vmem, vmem, vmem, smem, smem),
+        scratch_shapes=[
+            pltpu.VMEM((UNIT, D), F32),
+            pltpu.VMEM((3,) + weights.shape, F32),
+            pltpu.VMEM((RING, 3, UNIT, D), F32),
+            pltpu.SemaphoreType.DMA((3, weights.shape[0])),
+            pltpu.SemaphoreType.DMA((RING, 3)),
+        ],
+        compiler_params=params(n_dest // 2, 14),
         name="update",
     )(tab, me, news, places, own, other, weights, first, second, vectors, vector_first, vector_second)
 
@@ -1349,50 +1466,48 @@
     n_blk = lax.axis_size("blk")
     everyone = ("blk", "rep")
     cap = 48 if n_blk <= 16 else 16
-    dense_cap = min(7, slots)
     me = jnp.stack([lax.axis_index("blk"), lax.axis_index("rep")]).astype(I32)
 
     def exchange(a, axes):
         return lax.all_to_all(a, axes, 0, 0, tiled=True)
 
-    dense, tab = prepare(owners, me, weights, n_blk, dense_cap)
-    gathered = lax.all_gather(dense, "blk", axis=0, tiled=True)
     message, where_row, tab = request(
-        owners, tab, me, positive, query_lengths, passage_lengths, query_ids[0], passage_ids[0],
-        slots, n_blk, cap,
+        owners, me, positive, query_lengths, passage_lengths, query_ids[0], passage_ids[0],
+        weights, n_blk, cap,
     )
     message = exchange(message, everyone)
-    rows = exchange(fetch(me, message, weights, cap), everyone)
-    emb, low, normed, scale, probs, state = forward(
-        tab, query_lengths, passage_lengths, positive, rows, where_row, vectors, gathered, n_blk
+    first = along_z(collect(tab, me, message), n_blk)
+    rows, message = fetch(me, message, weights, cap)
+    rows, first = lax.optimization_barrier((rows, first))
+    rows = exchange(rows, everyone)
+    gathered = spread(first, n_blk)
+    emb, low, normed, scale, probs, state, matrices = forward(
+        tab, me, query_lengths, passage_lengths, positive, rows, where_row, vectors, gathered, n_blk
     )
     emb = exchange(emb, "blk")
     payload, loss, count = backward(
         tab, me, prefix_lengths, prefix_weights, emb, message, where_row, low, normed, scale,
-        probs, state, vectors, gathered, cap,
+        probs, state, vectors, matrices, cap,
     )
     payload = exchange(payload, everyone)
     asked = message[:, :cap].reshape(1, -1)
     own, news = reduce(tab, me, loss, asked, payload, slots, cap)
     other = lax.ppermute(own, "rep", [(0, 1), (1, 0)])
     news = exchange(news, everyone)
-    overflow = jnp.max(message[:, 126]) > 0
-
-    def roomy():
-        return local(
+    *outs, loss_sum, norm = update(
+        tab, me, news, own, other, weights, first_moments, second_moments, vectors, vector_first,
+        vector_second, place_rows(2 * n_blk),
+    )
+
+    def general(carry):
+        return 0, local(
             query_ids, passage_ids, query_lengths, passage_lengths, positive, prefix_lengths,
             prefix_weights, owners, weights, first_moments, second_moments, vectors, vector_first,
             vector_second,
         )
 
-    def usual():
-        *outs, loss_sum, norm = update(
-            tab, me, news, own, other, weights, first_moments, second_moments, vectors,
-            vector_first, vector_second, place_rows(2 * n_blk),
-        )
-        return (*outs, loss_sum.reshape(()), count.reshape(()), norm.reshape(()))
-
-    return lax.cond(overflow, roomy, usual)
+    outs = (*outs, loss_sum.reshape(()), count.reshape(()), norm.reshape(()))
+    return lax.while_loop(lambda c: c[0] > 0, general, (jnp.max(message[:, 126]), outs))[1]
 
 
 def solution(mesh):

time: 218 us -> 172 us (0.79)
  blocking collectives: 66 us -> 32.5 us
  Pallas kernels: 53.6 us -> 36.4 us
  between operations: 14.9 us -> 1.13 us
  starting transfers between devices: 8.69 us -> 20.2 us
  waiting for transfers between devices: 70 us -> 77.7 us
    all_to_all x3 -> x2, blocking collectives: 66 us -> 32.5 us  [exchange(): return lax.all_to_all(a, axes, 0, 0, tiled=True)]
    ppermute x0 -> x10, waiting for transfers between devices: none -> 21.2 us  [the longest x1 12.2 us: spread(): arrays = [first, lax.ppermute(first, 'rep', [(0, 1), (1, 0)])]]
    all_gather x1 -> x0, waiting for transfers between devices: 14.7 us -> none  [quick(): gathered = lax.all_gather(dense, 'blk', axis=0, tiled=True)]
    pallas_call x3, Pallas kernels: 22.1 us -> 12.6 us  [the longest x1 7.61 us: update(): pl.pallas_call(partial(update_kernel, pr), out_shape=(big, big, big, smal...]
    ppermute x0 -> x10, starting transfers between devices: none -> 9.42 us  [the longest x9 7.59 us: across(): return lax.ppermute(values, 'blk', pairs)]
    pallas_call x1, Pallas kernels: 7.71 us -> 4.33 us  [request(): pl.pallas_call(partial(request_kernel, slots, n_blk, cap), out_shape=(jax...]
    pallas_call x1, Pallas kernels: 11.1 us -> 8.39 us  [backward(): pl.pallas_call(partial(backward_kernel, cap), out_shape=(jax.ShapeDtypeSt...]
    all_to_all x2 -> x3, starting transfers between devices: 6.82 us -> 8.99 us  [exchange(): return lax.all_to_all(a, axes, 0, 0, tiled=True)]
  transfers between devices with their start and end apart: 4 -> 14, of which waited for: 3 -> 6; matrix products, arithmetic and copies ran while one was open for 1% -> 1% of each run, Pallas kernels for 5% -> 2%
where the time goes in v2:
time: 172 us; the launch traced here: 171 us
  waiting for transfers between devices  77.7 us (45%)
  Pallas kernels  36.4 us (21%)
  blocking collectives  32.5 us (19%)
  starting transfers between devices  20.2 us (12%)
    all_to_all x3, waiting for transfers between devices, exchange(): return lax.all_to_all(a, axes, 0, 0, tiled=True)  40.2 us
    all_to_all x2, blocking collectives, exchange(): return lax.all_to_all(a, axes, 0, 0, tiled=True)  32.5 us
    ppermute x1, waiting for transfers between devices, quick(): other = lax.ppermute(own, 'rep', [(0, 1), (1, 0)])  16.4 us
    ppermute x1, waiting for transfers between devices, spread(): arrays = [first, lax.ppermute(first, 'rep', [(0, 1), (1, 0)])]  12.2 us
    all_to_all x3, starting transfers between devices, exchange(): return lax.all_to_all(a, axes, 0, 0, tiled=True)  8.99 us
    ppermute x9, waiting for transfers between devices, across(): return lax.ppermute(values, 'blk', pairs)  8.96 us
    pallas_call x1, Pallas kernels, backward(): pl.pallas_call(partial(backward_kernel, cap), out_shape=(jax.ShapeDtypeSt...  8.39 us
    pallas_call x1, Pallas kernels, update(): pl.pallas_call(partial(update_kernel, pr), out_shape=(big, big, big, smal...  7.61 us
  transfers between devices with their start and end apart: 14, of which 6 were waited for; matrix products, arithmetic and copies ran while one was open for 1% of the time, Pallas kernels for 2%

profile of v2, /device:TPU:0, one launch (start us, length us, event | category | flops | bytes accessed | tf_op | source)
XLA Modules:
  0.0 171.5 jit_solution(12798775680089460476)
XLA Ops:
  0.7 0.8 reshape.1273.owner_line
  1.5 0.1 pad_add_fusion.me
  1.6 4.3 %request.1 = (bf16[32,48,128]{2,1,0:T(8,128)(2,1)S(1)}, s32[1,1280]{1,0:T(1,128)S(1)}, s32[32,128]{1,0:T(8,128)S(1)}) custom-call(s32[269]{0:T(512)} %owners.1, s32[2]{0:T(128)S(1)} %pad_add_fusion.me, s32[1,2]{1,0:T(1,128)} %positive.3, s32[1,2]{1,0:T(1,128)} %query_lengths.3, s32[1,2]{1,0:T(1,128)} %passage_lengths.3, s32[1,269]{1,0:T(1,128)S(1)} %reshape.1273.owner_line, ...), custom_call_target="tpu_custom_call" | custom-call | tf_op jit(solution)/shard_map/request/pallas_call | solution.py:755
  6.0 19.9 %all_to_all.80.message = bf16[32,48,128]{2,1,0:T(8,128)(2,1)S(1)} all-to-all(bf16[32,48,128]{2,1,0:T(8,128)(2,1)S(1)} %get-tuple-element.310), channel_id=1, replica_groups=mesh['blk'=16,'rep'=2] {'blk','rep'}, dimensions={0} | all-to-all | bytes 786432 | tf_op jit(solution)/shard_map/all_to_all | solution.py:1472
  25.8 1.4 collect.1
  27.2 0.4 collective-permute-start
  27.6 1.4 collective-permute-start.1
  29.0 2.8 %collective-permute-start.2 = (bf16[15,16,128]{2,1,0:T(8,128)(2,1)S(1)}, bf16[15,16,128]{2,1,0:T(8,128)(2,1)S(1)}, u32[]{:S(2)}, u32[]{:S(2)}) collective-permute-start(bf16[15,16,128]{2,1,0:T(8,128)(2,1)S(1)} %collect.1), channel_id=1, source_target_pairs={{0,24},{2,26},{4,28},{6,30},{8,0},{10,2},{12,4},{14,6},{16,8},{18,... | collective-permute-start | bytes 184328 | tf_op jit(solution)/shard_map/ppermute | solution.py:547
  31.9 3.6 %fetch.1 = (bf16[1536,256]{1,0:T(8,128)(2,1)}, s32[32,128]{1,0:T(8,128)S(1)}) custom-call(s32[2]{0:T(128)S(1)} %pad_add_fusion.me, bf16[32,48,128]{2,1,0:T(8,128)(2,1)S(1)} %all_to_all.80.message, f32[17,128,256]{2,1,0:T(8,128)S(1)} %copy-done.7), custom_call_target="tpu_custom_call" | custom-call | tf_op jit(solution)/shard_map/fetch/pallas_call | solution.py:833
  35.5 0.5 collective-permute-done.1
  36.1 2.9 %all-to-all-start.9 = ((bf16[32,48,256]{2,1,0:T(8,128)(2,1)}), bf16[32,48,256]{2,1,0:T(8,128)(2,1)S(1)}, u32[]{:S(2)}, u32[]{:S(2)}) async-start(bf16[32,48,256]{2,1,0:T(8,128)(2,1)} %bitcast.138), calls=%async_computation.9 | async-start | bytes 1572864 | tf_op jit(solution)/shard_map/all_to_all | solution.py:1472
  39.0 1.8 %collective-permute-start.3 = (bf16[4,15,16,128]{3,2,1,0:T(8,128)(2,1)S(1)}, bf16[4,15,16,128]{3,2,1,0:T(8,128)(2,1)S(1)}, u32[]{:S(2)}, u32[]{:S(2)}) collective-permute-start(bf16[4,15,16,128]{3,2,1,0:T(8,128)(2,1)S(1)} %pad_maximum_fusion.7.g0), channel_id=1, source_target_pairs={{0,1},{1,0},{2,3},{3,2},{4,5},{5,4},{6,7},{7,6},{8,9},{9,8},{10,11... | collective-permute-start | bytes 737288 | tf_op jit(solution)/shard_map/ppermute | solution.py:557
  40.8 1.5 collective-permute-start.4
  42.3 12.2 %collective-permute-done.3.g1 = bf16[4,15,16,128]{3,2,1,0:T(8,128)(2,1)S(1)} collective-permute-done((bf16[4,15,16,128]{3,2,1,0:T(8,128)(2,1)S(1)}, bf16[4,15,16,128]{3,2,1,0:T(8,128)(2,1)S(1)}, u32[]{:S(2)}, u32[]{:S(2)}) %collective-permute-start.3) | collective-permute-done | bytes 245792 | tf_op jit(solution)/shard_map/ppermute | solution.py:557
  54.5 0.9 collective-permute-start.5
  55.4 0.5 collective-permute-start.7
  56.0 6.9 %collective-permute-done.5.g3 = bf16[4,15,16,128]{3,2,1,0:T(8,128)(2,1)S(1)} collective-permute-done((bf16[4,15,16,128]{3,2,1,0:T(8,128)(2,1)S(1)}, bf16[4,15,16,128]{3,2,1,0:T(8,128)(2,1)S(1)}, u32[]{:S(2)}, u32[]{:S(2)}) %collective-permute-start.5) | collective-permute-done | bytes 245792 | tf_op jit(solution)/shard_map/ppermute | solution.py:547
  63.0 1.5 collective-permute-done.9.g7
  64.5 0.6 copy-done.107
  65.1 5.2 %forward.1 = (bf16[128,384]{1,0:T(8,128)(2,1)S(1)}, bf16[1280,256]{1,0:T(8,128)(2,1)S(1)}, f32[1280,256]{1,0:T(8,128)S(1)}, f32[1280,128]{1,0:T(8,128)S(1)}, f32...) custom-call(s32[32,128]{1,0:T(8,128)S(1)} %get-tuple-element.312.tab, ...), custom_call_target="tpu_custom_call" | custom-call | tf_op jit(solution)/shard_map/forward/pallas_call | solution.py:952
  70.4 12.6 %all_to_all.81 = bf16[16,8,384]{2,1,0:T(8,128)(2,1)S(1)} all-to-all(bf16[16,8,384]{2,1,0:T(8,128)(2,1)S(1)} %bitcast.457), channel_id=1, replica_groups=mesh['blk'=16,'rep'=2] {'blk'}, dimensions={0} | all-to-all | bytes 196608 | tf_op jit(solution)/shard_map/all_to_all | solution.py:1472
  83.0 8.4 %backward.1 = (bf16[32,208,128]{2,1,0:T(8,128)(2,1)}, f32[1,1]{1,0:T(1,128)}, f32[1,1]{1,0:T(1,128)}) custom-call(s32[32,128]{1,0:T(8,128)S(1)} %get-tuple-element.312.tab, s32[2]{0:T(128)S(1)} %pad_add_fusion.me, s32[6]{0:T(128)S(1)} %copy-done.146, f32[6]{0:T(128)S(1)} %copy-done.148, bf16[128,384]{1,0:T(8,128)(2,1)S(1)} %bitcast.454, ...), custom_call_target="tpu_custom_call" | custom-call | tf_op jit(solution)/shard_map/backward/pallas_call | solution.py:1205
  91.4 2.7 %all-to-all-start.11 = ((bf16[32,208,128]{2,1,0:T(8,128)(2,1)}), bf16[32,208,128]{2,1,0:T(8,128)(2,1)S(1)}, u32[]{:S(2)}, u32[]{:S(2)}) async-start(bf16[32,208,128]{2,1,0:T(8,128)(2,1)} %get-tuple-element.325), calls=%async_computation.11 | async-start | bytes 3407872 | tf_op jit(solution)/shard_map/all_to_all | solution.py:1472
  94.1 0.1 reshape.1274.asked
  94.2 40.2 %all-to-all-done.11.payload = bf16[32,208,128]{2,1,0:T(8,128)(2,1)S(1)} async-done(((bf16[32,208,128]{2,1,0:T(8,128)(2,1)}), bf16[32,208,128]{2,1,0:T(8,128)(2,1)S(1)}, u32[]{:S(2)}, u32[]{:S(2)}) %all-to-all-start.11) | async-done | bytes 1703968 | tf_op jit(solution)/shard_map/all_to_all | solution.py:1472
  134.4 5.8 %reduce.47 = (bf16[17,64,256]{2,1,0:T(8,128)(2,1)S(1)}, bf16[512,384]{1,0:T(8,128)(2,1)}) custom-call(s32[32,128]{1,0:T(8,128)S(1)} %get-tuple-element.312.tab, s32[2]{0:T(128)S(1)} %pad_add_fusion.me, f32[1,1]{1,0:T(1,128)} %get-tuple-element.324.loss, s32[1,1536]{1,0:T(1,128)S(1)} %reshape.1274.asked, bf16[32,208,128]{2,1,0:T(8,128)(2,1)S(1)} %all-to-all-done.11.payload), custom_call_target="tpu_custom_call" | custom-call | tf_op jit(solution)/shard_map/reduce/pallas_call | solution.py:1308
  140.3 3.4 %all-to-all-start.12 = ((bf16[32,16,384]{2,1,0:T(8,128)(2,1)}), bf16[32,16,384]{2,1,0:T(8,128)(2,1)S(1)}, u32[]{:S(2)}, u32[]{:S(2)}) async-start(bf16[32,16,384]{2,1,0:T(8,128)(2,1)} %bitcast.142), calls=%async_computation.12 | async-start | bytes 786432 | tf_op jit(solution)/shard_map/all_to_all | solution.py:1472
  143.7 1.8 %collective-permute-start.10 = (bf16[17,64,256]{2,1,0:T(8,128)(2,1)S(1)}, bf16[17,64,256]{2,1,0:T(8,128)(2,1)S(1)}, u32[]{:S(2)}, u32[]{:S(2)}) collective-permute-start(bf16[17,64,256]{2,1,0:T(8,128)(2,1)S(1)} %get-tuple-element.327.own), channel_id=1, source_target_pairs={{0,1},{1,0},{2,3},{3,2},{4,5},{5,4},{6,7},{7,6},{8,9},{9,8},{10,11... | collective-permute-start | bytes 1671176 | tf_op jit(solution)/shard_map/ppermute | solution.py:1495
  145.5 0.8 slice_reduce_fusion
  146.3 16.4 %collective-permute-done.10.other = bf16[17,64,256]{2,1,0:T(8,128)(2,1)S(1)} collective-permute-done((bf16[17,64,256]{2,1,0:T(8,128)(2,1)S(1)}, bf16[17,64,256]{2,1,0:T(8,128)(2,1)S(1)}, u32[]{:S(2)}, u32[]{:S(2)}) %collective-permute-start.10) | collective-permute-done | bytes 557088 | tf_op jit(solution)/shard_map/ppermute | solution.py:1495
  162.7 7.6 %update.1 = (f32[17,128,256]{2,1,0:T(8,128)}, f32[17,128,256]{2,1,0:T(8,128)}, f32[17,128,256]{2,1,0:T(8,128)}, f32[16,256]{1,0:T(8,128)}, f32[16,256]{1,0:T(8,1...) custom-call(s32[32,128]{1,0:T(8,128)S(1)} %get-tuple-element.312.tab, s32[2]{0:T(128)S(1)} %pad_add_fusion.me, ...), custom_call_target="tpu_custom_call" | custom-call | tf_op jit(solution)/shard_map/update/pallas_call | solution.py:1443
  170.3 1.0 while.66
  (47 shorter events, 0.2 us)
Async XLA Ops:
  0.6 64.5 %copy-start.160 = (s32[1,2]{1,0:T(1,128)S(1)}, s32[1,2]{1,0:T(1,128)}, u32[]{:S(2)}) copy-start(s32[1,2]{1,0:T(1,128)} %query_lengths.3) | copy-start | bytes 28
  0.7 64.5 %copy-start.155 = (s32[1,2]{1,0:T(1,128)S(1)}, s32[1,2]{1,0:T(1,128)}, u32[]{:S(2)}) copy-start(s32[1,2]{1,0:T(1,128)} %passage_lengths.3) | copy-start | bytes 28
  0.7 64.5 %copy-start.157 = (s32[1,2]{1,0:T(1,128)S(1)}, s32[1,2]{1,0:T(1,128)}, u32[]{:S(2)}) copy-start(s32[1,2]{1,0:T(1,128)} %positive.3) | copy-start | bytes 28
  0.7 31.2 %copy-start.7 = (f32[17,128,256]{2,1,0:T(8,128)S(1)}, f32[17,128,256]{2,1,0:T(8,128)}, u32[]{:S(2)}) copy-start(f32[17,128,256]{2,1,0:T(8,128)} %weight.1) | copy-start | bytes 6684676
  0.7 64.5 %copy-start.50 = (f32[16,256]{1,0:T(8,128)S(1)}, f32[16,256]{1,0:T(8,128)}, u32[]{:S(2)}) copy-start(f32[16,256]{1,0:T(8,128)} %vectors.5) | copy-start | bytes 49156
  25.8 57.2 %copy-start.146 = (s32[6]{0:T(128)S(1)}, s32[6]{0:T(128)}, u32[]{:S(2)}) copy-start(s32[6]{0:T(128)} %prefix_lengths.1) | copy-start | bytes 76
  25.8 57.2 %copy-start.148 = (f32[6]{0:T(128)S(1)}, f32[6]{0:T(128)}, u32[]{:S(2)}) copy-start(f32[6]{0:T(128)} %prefix_weights.1) | copy-start | bytes 76
  27.2 8.2 %collective-permute-start = (bf16[15,16,128]{2,1,0:T(8,128)(2,1)S(1)}, bf16[15,16,128]{2,1,0:T(8,128)(2,1)S(1)}, u32[]{:S(2)}, u32[]{:S(2)}) collective-permute-start(bf16[15,16,128]{2,1,0:T(8,128)(2,1)S(1)} %collect.1), channel_id=1, source_target_pairs={{0,8},{2,10},{4,12},{6,14},{8,16},{10,18},{12,20},{14,22},{16,24},... | collective-permute-start | bytes 184328 | tf_op jit(solution)/shard_map/ppermute | solution.py:547
  27.6 8.4 %collective-permute-start.1 = (bf16[15,16,128]{2,1,0:T(8,128)(2,1)S(1)}, bf16[15,16,128]{2,1,0:T(8,128)(2,1)S(1)}, u32[]{:S(2)}, u32[]{:S(2)}) collective-permute-start(bf16[15,16,128]{2,1,0:T(8,128)(2,1)S(1)} %collect.1), channel_id=1, source_target_pairs={{0,16},{2,18},{4,20},{6,22},{8,24},{10,26},{12,28},{14,30},{16,0},... | collective-permute-start | bytes 184328 | tf_op jit(solution)/shard_map/ppermute | solution.py:547
  29.0 7.0 %collective-permute-start.2 = (bf16[15,16,128]{2,1,0:T(8,128)(2,1)S(1)}, bf16[15,16,128]{2,1,0:T(8,128)(2,1)S(1)}, u32[]{:S(2)}, u32[]{:S(2)}) collective-permute-start(bf16[15,16,128]{2,1,0:T(8,128)(2,1)S(1)} %collect.1), channel_id=1, source_target_pairs={{0,24},{2,26},{4,28},{6,30},{8,0},{10,2},{12,4},{14,6},{16,8},{18,... | collective-permute-start | bytes 184328 | tf_op jit(solution)/shard_map/ppermute | solution.py:547
  36.1 28.4 %copy-start.63 = (bf16[4,15,16,128]{3,2,1,0:T(8,128)(2,1)}, bf16[4,15,16,128]{3,2,1,0:T(8,128)(2,1)S(1)}, u32[]{:S(2)}) copy-start(bf16[4,15,16,128]{3,2,1,0:T(8,128)(2,1)S(1)} %pad_maximum_fusion.7.g0) | copy-start | bytes 737284
  36.1 28.4 %all-to-all-start.9 = ((bf16[32,48,256]{2,1,0:T(8,128)(2,1)}), bf16[32,48,256]{2,1,0:T(8,128)(2,1)S(1)}, u32[]{:S(2)}, u32[]{:S(2)}) async-start(bf16[32,48,256]{2,1,0:T(8,128)(2,1)} %bitcast.138), calls=%async_computation.9 | async-start | bytes 1572864 | tf_op jit(solution)/shard_map/all_to_all | solution.py:1472
  39.0 15.5 %collective-permute-start.3 = (bf16[4,15,16,128]{3,2,1,0:T(8,128)(2,1)S(1)}, bf16[4,15,16,128]{3,2,1,0:T(8,128)(2,1)S(1)}, u32[]{:S(2)}, u32[]{:S(2)}) collective-permute-start(bf16[4,15,16,128]{3,2,1,0:T(8,128)(2,1)S(1)} %pad_maximum_fusion.7.g0), channel_id=1, source_target_pairs={{0,1},{1,0},{2,3},{3,2},{4,5},{5,4},{6,7},{7,6},{8,9},{9,8},{10,11... | collective-permute-start | bytes 737288 | tf_op jit(solution)/shard_map/ppermute | solution.py:557
  40.8 15.1 %collective-permute-start.4 = (bf16[4,15,16,128]{3,2,1,0:T(8,128)(2,1)S(1)}, bf16[4,15,16,128]{3,2,1,0:T(8,128)(2,1)S(1)}, u32[]{:S(2)}, u32[]{:S(2)}) collective-permute-start(bf16[4,15,16,128]{3,2,1,0:T(8,128)(2,1)S(1)} %pad_maximum_fusion.7.g0), channel_id=1, source_target_pairs={{0,4},{2,6},{4,0},{6,2},{8,12},{10,14},{12,8},{14,10},{16,20},{18,... | collective-permute-start | bytes 737288 | tf_op jit(solution)/shard_map/ppermute | solution.py:547
  54.5 10.0 %copy-start.101 = (bf16[4,15,16,128]{3,2,1,0:T(8,128)(2,1)}, bf16[4,15,16,128]{3,2,1,0:T(8,128)(2,1)S(1)}, u32[]{:S(2)}) copy-start(bf16[4,15,16,128]{3,2,1,0:T(8,128)(2,1)S(1)} %collective-permute-done.3.g1) | copy-start | bytes 737284
  54.5 8.4 %collective-permute-start.5 = (bf16[4,15,16,128]{3,2,1,0:T(8,128)(2,1)S(1)}, bf16[4,15,16,128]{3,2,1,0:T(8,128)(2,1)S(1)}, u32[]{:S(2)}, u32[]{:S(2)}) collective-permute-start(bf16[4,15,16,128]{3,2,1,0:T(8,128)(2,1)S(1)} %collective-permute-done.3.g1), channel_id=1, source_target_pairs={{0,4},{2,6},{4,0},{6,2},{8,12},{10,14},{12,8},{14,10},{16,20},{18,... | collective-permute-start | bytes 737288 | tf_op jit(solution)/shard_map/ppermute | solution.py:547
  55.4 7.5 %collective-permute-start.6 = (bf16[4,15,16,128]{3,2,1,0:T(8,128)(2,1)S(1)}, bf16[4,15,16,128]{3,2,1,0:T(8,128)(2,1)S(1)}, u32[]{:S(2)}, u32[]{:S(2)}) collective-permute-start(bf16[4,15,16,128]{3,2,1,0:T(8,128)(2,1)S(1)} %pad_maximum_fusion.7.g0), channel_id=1, source_target_pairs={{0,2},{2,0},{4,6},{6,4},{8,10},{10,8},{12,14},{14,12},{16,18},{18,... | collective-permute-start | bytes 737288 | tf_op jit(solution)/shard_map/ppermute | solution.py:547
  55.4 7.6 %collective-permute-start.7 = (bf16[4,15,16,128]{3,2,1,0:T(8,128)(2,1)S(1)}, bf16[4,15,16,128]{3,2,1,0:T(8,128)(2,1)S(1)}, u32[]{:S(2)}, u32[]{:S(2)}) collective-permute-start(bf16[4,15,16,128]{3,2,1,0:T(8,128)(2,1)S(1)} %collective-permute-done.3.g1), channel_id=1, source_target_pairs={{0,2},{2,0},{4,6},{6,4},{8,10},{10,8},{12,14},{14,12},{16,18},{18,... | collective-permute-start | bytes 737288 | tf_op jit(solution)/shard_map/ppermute | solution.py:547
  55.9 8.6 %copy-start.102 = (bf16[4,15,16,128]{3,2,1,0:T(8,128)(2,1)}, bf16[4,15,16,128]{3,2,1,0:T(8,128)(2,1)S(1)}, u32[]{:S(2)}) copy-start(bf16[4,15,16,128]{3,2,1,0:T(8,128)(2,1)S(1)} %collective-permute-done.4.g2) | copy-start | bytes 737284
  55.9 7.1 %collective-permute-start.8 = (bf16[4,15,16,128]{3,2,1,0:T(8,128)(2,1)S(1)}, bf16[4,15,16,128]{3,2,1,0:T(8,128)(2,1)S(1)}, u32[]{:S(2)}, u32[]{:S(2)}) collective-permute-start(bf16[4,15,16,128]{3,2,1,0:T(8,128)(2,1)S(1)} %collective-permute-done.4.g2), channel_id=1, source_target_pairs={{0,2},{2,0},{4,6},{6,4},{8,10},{10,8},{12,14},{14,12},{16,18},{18,... | collective-permute-start | bytes 737288 | tf_op jit(solution)/shard_map/ppermute | solution.py:547
  62.9 1.5 copy-start.103
  62.9 1.5 collective-permute-start.9
  62.9 1.5 copy-start.104
  62.9 1.5 copy-start.105
  63.0 1.5 copy-start.106
  64.4 0.7 copy-start.107
  91.4 71.3 %copy-start.80 = (f32[16,256]{1,0:T(8,128)S(1)}, f32[16,256]{1,0:T(8,128)}, u32[]{:S(2)}) copy-start(f32[16,256]{1,0:T(8,128)} %vector_first.1) | copy-start | bytes 49156
  91.4 71.3 %copy-start.82 = (f32[16,256]{1,0:T(8,128)S(1)}, f32[16,256]{1,0:T(8,128)}, u32[]{:S(2)}) copy-start(f32[16,256]{1,0:T(8,128)} %vector_second.1) | copy-start | bytes 49156
  91.4 43.0 %all-to-all-start.11 = ((bf16[32,208,128]{2,1,0:T(8,128)(2,1)}), bf16[32,208,128]{2,1,0:T(8,128)(2,1)S(1)}, u32[]{:S(2)}, u32[]{:S(2)}) async-start(bf16[32,208,128]{2,1,0:T(8,128)(2,1)} %get-tuple-element.325), calls=%async_computation.11 | async-start | bytes 3407872 | tf_op jit(solution)/shard_map/all_to_all | solution.py:1472
  140.3 22.4 %all-to-all-start.12 = ((bf16[32,16,384]{2,1,0:T(8,128)(2,1)}), bf16[32,16,384]{2,1,0:T(8,128)(2,1)S(1)}, u32[]{:S(2)}, u32[]{:S(2)}) async-start(bf16[32,16,384]{2,1,0:T(8,128)(2,1)} %bitcast.142), calls=%async_computation.12 | async-start | bytes 786432 | tf_op jit(solution)/shard_map/all_to_all | solution.py:1472
  143.7 19.0 %collective-permute-start.10 = (bf16[17,64,256]{2,1,0:T(8,128)(2,1)S(1)}, bf16[17,64,256]{2,1,0:T(8,128)(2,1)S(1)}, u32[]{:S(2)}, u32[]{:S(2)}) collective-permute-start(bf16[17,64,256]{2,1,0:T(8,128)(2,1)S(1)} %get-tuple-element.327.own), channel_id=1, source_target_pairs={{0,1},{1,0},{2,3},{3,2},{4,5},{5,4},{6,7},{7,6},{8,9},{9,8},{10,11... | collective-permute-start | bytes 1671176 | tf_op jit(solution)/shard_map/ppermute | solution.py:1495
  162.7 7.6 %copy-start.150 = (s32[1,2,128]{2,1,0:T(2,128)S(1)}, s32[1,2,128]{2,1,0:T(2,128)}, u32[]{:S(2)}) copy-start(s32[1,2,128]{2,1,0:T(2,128)} %param.34) | copy-start | bytes 3076

commit v3 on v2

--- a/solution.py
+++ b/solution.py
@@ -456,7 +456,7 @@
 QROWS = 128
 TOKENS = 2 * QROWS + 2 * PLEN
 STARTS = (0, QROWS, 2 * QROWS, 2 * QROWS + PLEN)
-UNITS_L = 12
+UNITS_L = 10
 L_ROWS = 4 * UNITS_L
 NEVER = -1e30
 
@@ -480,13 +480,18 @@
 CLASS = DENSE // 2
 HELD = DENSE_CAP // 2
 AT_ASKED = DENSE_CAP // 4 * PIECE
-MESSAGE_ROWS = AT_ASKED + 16
+MESSAGE_ROWS = AT_ASKED + 8
 
 KIND_TABLE, KIND_PLACE, KIND_DENSE = 1, 2, 8
 
 vmem = pl.BlockSpec(memory_space=pltpu.VMEM)
 smem = pl.BlockSpec(memory_space=pltpu.SMEM)
 hbm = pl.BlockSpec(memory_space=pl.ANY)
+in_hbm = pl.BlockSpec(memory_space=pltpu.HBM)
+
+
+def stay(*arrays):
+    return [pltpu.with_memory_space_constraint(a, pltpu.HBM) for a in arrays]
 
 
 def iota(shape, axis):
@@ -594,7 +599,7 @@
 
 
 def request_kernel(
-    slots, n_blk, cap, owners, me, positive, query_lengths, passage_lengths, owner_line,
+    slots, n_blk, cap, take_cap, owners, me, positive, query_lengths, passage_lengths, owner_line,
     query_ids, passage_ids, weights, message, where_row, tab, ids, owner_row, loaded, sems,
 ):
     n_rep = 2
@@ -635,7 +640,15 @@
     unit = jnp.sum(jnp.where(same, need, 0), 1, keepdims=True)
     lower = (dense_owner < owner_column) & (block_row < DENSE)
     order = rank + jnp.sum(lower.astype(I32), 1, keepdims=True)
-    crowded = jnp.max(((rank >= DENSE_CAP) & (iota((32, 1), 0) < DENSE)).astype(I32))
+    is_dense = (iota((32, 1), 0) >= PLACE_BLOCKS) & (iota((32, 1), 0) < DENSE)
+    at = iota((32, 1), 0) * UNIT
+    needs = jnp.where((at >= AT_K) & (at < AT_O), 2, 1)
+    crowded = jnp.max(
+        (
+            ((rank >= DENSE_CAP) & (iota((32, 1), 0) < DENSE))
+            | (is_dense & (unit + needs > UNITS_L))
+        ).astype(I32)
+    )
     which = iota((32, wide), 1)
     code = jnp.where(
         which < TABLE_BLOCKS,
@@ -699,18 +712,26 @@
     for at in range(0, TOKENS, 128):
         earlier = ((iota((128, TOKENS), 0) + at) < first_at).astype(F32).astype(BF16)
         seen = seen + dot_nn(chosen_low[:, at : at + 128], earlier)
-    rank = jnp.sum(
-        jnp.where(iota((n_dest, TOKENS), 0) == dest, seen, 0.0), 0, keepdims=True
-    ).astype(I32)
-    fits = live & (rank < cap)
-    where_row[...] = jnp.where(fits, dest * cap + rank, -1)
-    over = jnp.max((live & (rank >= cap)).astype(I32))
-    code = local_row + 1
-    high = code // 32
-    low = code - high * 32
-    spread = (iota((128, TOKENS), 0) == rank).astype(F32).astype(BF16)
-    sent_high = dot_nt((chosen * high.astype(F32)).astype(BF16), spread)
-    sent_low = dot_nt((chosen * low.astype(F32)).astype(BF16), spread)
+    to = iota((n_dest, TOKENS), 0)
+    rank = jnp.sum(jnp.where(to == dest, seen, 0.0), 0, keepdims=True).astype(I32)
+    turn = jnp.sum(jnp.where(to // n_rep == owner, seen, 0.0), 0, keepdims=True).astype(I32)
+    source = owner * n_rep + turn % n_rep
+    spot = turn // n_rep
+    where_row[0:1] = jnp.where(live & (spot < take_cap), source * take_cap + spot, -1)
+    where_row[1:2] = jnp.where(live & (rank < cap), dest * cap + rank, -1)
+    over = jnp.max((live & ((rank >= cap) | (spot >= take_cap))).astype(I32))
+
+    def listed(dest, spot, code):
+        high = code // 32
+        low = code - high * 32
+        chosen = ((to == dest) & first).astype(F32)
+        both = jnp.concatenate([chosen * high.astype(F32), chosen * low.astype(F32)], 0)
+        spread = (iota((128, TOKENS), 0) == spot).astype(F32).astype(BF16)
+        both = dot_nt(both.astype(BF16), spread)
+        return both[:n_dest], both[n_dest:]
+
+    take_high, take_low = listed(source, spot, inside * UNIT + row + 1)
+    sent_high, sent_low = listed(dest, rank, local_row + 1)
     flag = jnp.maximum(over, crowded)
     column_of = iota((1, 128), 1)
     marks = jnp.where(
@@ -718,13 +739,11 @@
         positive[0, 0],
         jnp.where(column_of == 1, positive[0, 1], jnp.where(column_of == 2, flag, 0)),
     ).astype(F32)
-    row16 = iota((16, 128), 0)
+    row8 = iota((8, 128), 0)
     for d in range(n_dest):
-        asked = jnp.where(
-            row16 == 0,
-            sent_high[d : d + 1],
-            jnp.where(row16 == 1, sent_low[d : d + 1], jnp.where(row16 == 2, marks, 0.0)),
-        )
+        asked = jnp.where(row8 == 0, take_high[d : d + 1], marks)
+        for i, part in ((1, take_low), (3, sent_high), (4, sent_low)):
+            asked = jnp.where(row8 == i, part[d : d + 1], asked)
         message[d, AT_ASKED:] = asked.astype(BF16)
     for spot in range(HELD):
         present = spot // 2 * 4 + 2 * me[1] + spot % 2 < have
@@ -747,19 +766,19 @@
                 ]
 
 
-def request(owners, me, positive, query_lengths, passage_lengths, query_ids, passage_ids, weights, n_blk, cap):
+def request(owners, me, positive, query_lengths, passage_lengths, query_ids, passage_ids, weights, n_blk, cap, take_cap):
     slots = weights.shape[0]
     n_dest = 2 * n_blk
     n_units = owners.shape[0]
     owner_row = owners.reshape(1, n_units)
     return pl.pallas_call(
-        partial(request_kernel, slots, n_blk, cap),
+        partial(request_kernel, slots, n_blk, cap, take_cap),
         out_shape=(
             jax.ShapeDtypeStruct((n_dest, MESSAGE_ROWS, 128), BF16),
-            jax.ShapeDtypeStruct((1, TOKENS), I32),
+            jax.ShapeDtypeStruct((2, TOKENS), I32),
             jax.ShapeDtypeStruct((32, 128), I32),
         ),
-        in_specs=[smem] * 5 + [vmem] * 3 + [hbm],
+        in_specs=[smem] * 5 + [vmem] * 3 + [in_hbm],
         out_specs=(vmem, vmem, vmem),
         scratch_shapes=[
             pltpu.VMEM((1, TOKENS), I32),
@@ -769,7 +788,7 @@
         ],
         compiler_params=params(n_blk, 12),
         name="request",
-    )(owners, me, positive, query_lengths, passage_lengths, owner_row, query_ids, passage_ids, weights)
+    )(owners, me, positive, query_lengths, passage_lengths, owner_row, query_ids, passage_ids, *stay(weights))
 
 
 def collect_kernel(tab, me, message, mine_out):
@@ -795,58 +814,52 @@
     )(tab, me, message)
 
 
-def fetch_kernel(slots, cap, me, message, weights, rows_out, asked_out, held, table, hot, sem):
+def fetch_kernel(slots, cap, take_cap, message, weights, rows_out, asked_out, wanted, held, table, hot, sem):
     n_dest = message.shape[0]
-    copy = pltpu.make_async_copy(weights.at[:, pl.ds(me[1] * HALF, HALF), :], held, sem)
+    copy = pltpu.make_async_copy(weights, held, sem)
     copy.start()
     column_of = iota((1, 128), 1)
+    wanted[...] = jnp.zeros(wanted.shape, I32)
     for s in range(n_dest):
         part = message[s, AT_ASKED:].astype(F32)
-        wanted = part[0:1] * 32.0 + part[1:2] - 1.0
+        wanted[s : s + 1] = (part[0:1] * 32.0 + part[1:2] - 1.0).astype(I32)
         marks = part[2:3]
-        row = jnp.where(column_of < cap, wanted, 0.0)
+        row = jnp.where(column_of < cap, part[3:4] * 32.0 + part[4:5] - 1.0, 0.0)
         for i in range(3):
             row = jnp.where(column_of == 124 + i, marks[:, i : i + 1], row)
         asked_out[s : s + 1] = row.astype(I32)
     wide = table.shape[0]
-    rows = asked_out[...]
-    pad = -n_dest % 128
-    if pad:
-        rows = jnp.concatenate([rows, jnp.zeros((pad, 128), I32)], 0)
-    columns = rows.T
+    columns = wanted[...].T
     for s in range(n_dest):
-        hot[s * cap : (s + 1) * cap] = (
-            (iota((cap, wide), 1) == columns[:cap, s : s + 1]).astype(F32).astype(BF16)
+        hot[s * take_cap : (s + 1) * take_cap] = (
+            (iota((take_cap, wide), 1) == columns[:take_cap, s : s + 1]).astype(F32).astype(BF16)
         )
     copy.wait()
-    filled = slots * HALF
-    table[:filled] = held[...].reshape(filled, D).astype(BF16)
-    if wide > filled:
-        table[filled:] = jnp.zeros((wide - filled, D), BF16)
+    table[...] = held[...].reshape(wide, D).astype(BF16)
     rows_out[...] = dot_nn(hot[...], table[...]).astype(BF16)
 
 
-def fetch(me, message, weights, cap):
+def fetch(message, weights, cap, take_cap):
     slots = weights.shape[0]
     n_dest = message.shape[0]
-    wide = -(-slots * HALF // 128) * 128
     return pl.pallas_call(
-        partial(fetch_kernel, slots, cap),
+        partial(fetch_kernel, slots, cap, take_cap),
         out_shape=(
-            jax.ShapeDtypeStruct((n_dest * cap, D), BF16),
+            jax.ShapeDtypeStruct((n_dest * take_cap, D), BF16),
             jax.ShapeDtypeStruct((n_dest, 128), I32),
         ),
-        in_specs=[smem, vmem, hbm],
+        in_specs=[vmem, in_hbm],
         out_specs=(vmem, vmem),
         scratch_shapes=[
-            pltpu.VMEM((slots, HALF, D), F32),
-            pltpu.VMEM((wide, D), BF16),
-            pltpu.VMEM((n_dest * cap, wide), BF16),
+            pltpu.VMEM((-(-n_dest // 128) * 128, 128), I32),
+            pltpu.VMEM(weights.shape, F32),
+            pltpu.VMEM((slots * UNIT, D), BF16),
+            pltpu.VMEM((n_dest * take_cap, slots * UNIT), BF16),
             pltpu.SemaphoreType.DMA,
         ],
-        compiler_params=params(n_dest // 2, 16),
+        compiler_params=params(n_dest // 2, 20),
         name="fetch",
-    )(me, message, weights)
+    )(message, *stay(weights))
 
 
 ST_POOLED, ST_C, ST_N2, ST_N1, ST_H, ST_O, ST_Q, ST_X0 = range(0, 64, 8)
@@ -864,7 +877,7 @@
         copy.start()
     taken = rows.shape[0]
     for at in range(0, TOKENS, 128):
-        column = to_column(where_row[:, at : at + 128])
+        column = to_column(where_row[0:1, at : at + 128])
         hot = (iota((128, taken), 1) == column).astype(F32).astype(BF16)
         embedded[at : at + 128] = dot_nn(hot, rows[...])
     for copy in copies:
@@ -974,6 +987,10 @@
     )
 
 
+def news_rows(n_dest):
+    return 2 * place_rows(n_dest) + 8
+
+
 def place_rows(n_dest):
     return max(PLEN // n_dest, 16)
 
@@ -1004,7 +1021,6 @@
     passages = jnp.concatenate([every(2), every(3)], 0)[:, :D].astype(BF16)
     wanted = queries[:, D : D + 1].astype(I32)
     queries = queries[:, :D]
-    query_low = queries.astype(BF16)
     size = 2 * n_blk
     counted = wanted >= 0
     counted_f = counted.astype(F32)
@@ -1014,26 +1030,32 @@
     lane = iota(marks.shape, 1)
     count = jnp.sum((((lane == 124) | (lane == 125)) & (marks >= 0)).astype(F32))
     count_out[0, 0] = count
-    feature = iota((1, D), 1)
-    losses = jnp.zeros((size, 1), F32)
-    d_queries = jnp.zeros((size, D), F32)
-    d_passages = jnp.zeros((size, D), F32)
-    for k in range(prefix_lengths.shape[0]):
-        mask = (feature < prefix_lengths[k]).astype(F32)
-        prefix = jnp.full((1, 1), prefix_lengths[k], I32).astype(F32)
-        temper = TEMPER * lax.rsqrt(prefix)
-        logits = dot_nt((queries * mask).astype(BF16), passages) * temper
-        top = jnp.max(logits, -1, keepdims=True)
-        weight = jnp.exp(logits - top)
-        total = jnp.sum(weight, -1, keepdims=True)
-        hit = jnp.sum(jnp.where(target, logits, 0.0), -1, keepdims=True)
-        losses = losses + prefix_weights[k] * (top + jnp.log(total) - hit)
-        factor = counted_f * (prefix_weights[k] / count) * temper
-        grad = (weight / total - target.astype(F32)) * factor
-        high, lower = split(grad)
-        d_queries = d_queries + mask * (dot_nn(high, passages) + dot_nn(lower, passages))
-        d_passages = d_passages + mask * (dot_tn(high, query_low) + dot_tn(lower, query_low))
-    loss_out[0, 0] = jnp.sum(losses * counted_f)
+    n_pre = prefix_lengths.shape[0]
+    prefix_of = iota((n_pre * size, 1), 0) // size
+    prefix = jnp.zeros((n_pre * size, 1), I32)
+    share = jnp.zeros((n_pre * size, 1), F32)
+    for k in range(n_pre):
+        prefix = jnp.where(prefix_of == k, prefix_lengths[k], prefix)
+        share = jnp.where(prefix_of == k, prefix_weights[k], share)
+    temper = TEMPER * lax.rsqrt(prefix.astype(F32))
+    mask = iota((n_pre * size, D), 1) < prefix
+    masked = jnp.where(mask, jnp.concatenate([queries] * n_pre, 0), 0.0).astype(BF16)
+    logits = dot_nt(masked, passages) * temper
+    targets = jnp.concatenate([target.astype(F32)] * n_pre, 0)
+    counts = jnp.concatenate([counted_f] * n_pre, 0)
+    top = jnp.max(logits, -1, keepdims=True)
+    weight = jnp.exp(logits - top)
+    total = jnp.sum(weight, -1, keepdims=True)
+    hit = jnp.sum(logits * targets, -1, keepdims=True)
+    losses = share * (top + jnp.log(total) - hit) * counts
+    grad = (weight / total - targets) * (counts * (share / count) * temper)
+    high, lower = split(grad)
+    spread_queries = jnp.where(mask, dot_nn(high, passages) + dot_nn(lower, passages), 0.0)
+    d_queries = spread_queries[:size]
+    for k in range(1, n_pre):
+        d_queries = d_queries + spread_queries[k * size : (k + 1) * size]
+    d_passages = dot_tn(high, masked) + dot_tn(lower, masked)
+    loss_out[0, 0] = jnp.sum(losses)
     grad_emb[:size] = d_queries
     grad_emb[size : 2 * size] = d_passages
     grad_pooled = jnp.concatenate(
@@ -1108,7 +1130,7 @@
     per = max(128 // cap, 1)
     step = per * cap
     for at in range(0, n_dest * cap, step):
-        hot = ((iota((step, TOKENS), 0) + at) == where_row[...]).astype(F32).astype(BF16)
+        hot = ((iota((step, TOKENS), 0) + at) == where_row[1:2]).astype(F32).astype(BF16)
         summed = dot_nn(hot, de_low).astype(BF16)
         for i in range(per):
             d = at // cap + i
@@ -1283,23 +1305,21 @@
     summed = total[...]
     reduced[...] = summed.astype(BF16).reshape(reduced.shape)
     square = jnp.sum(summed * summed) + jnp.sum(spots * spots) + jnp.sum(vector * vector)
-    row16 = iota((pr, 128), 0)
+    row8 = iota((8, 128), 0)
 
     def parts(v):
         first = v.astype(BF16).astype(F32)
         second = (v - first).astype(BF16).astype(F32)
         return first, second, v - first - second
 
-    extra = jnp.zeros((pr, 128), F32)
+    extra = jnp.where(row8 == 0, vector, 0.0)
     for i, part in enumerate(
-        parts(vector)
-        + parts(jnp.full((1, 128), square, F32))
-        + parts(jnp.full((1, 128), loss[0, 0], F32))
+        parts(jnp.full((1, 128), square, F32)) + parts(jnp.full((1, 128), loss[0, 0], F32))
     ):
-        extra = jnp.where(row16 == i, part, extra)
-    block = jnp.concatenate([spots, extra], 1).astype(BF16)
+        extra = jnp.where(row8 == 1 + i, part, extra)
+    block = jnp.concatenate([spots[:, :128], spots[:, 128:], extra], 0).astype(BF16)
     for d in range(n_dest):
-        news[d * pr : (d + 1) * pr] = block
+        news[d] = block
 
 
 def reduce(tab, me, loss, asked, payload, slots, cap):
@@ -1309,7 +1329,7 @@
         partial(reduce_kernel, slots, cap),
         out_shape=(
             jax.ShapeDtypeStruct((slots, HALF, D), BF16),
-            jax.ShapeDtypeStruct((n_dest * pr, D + 128), BF16),
+            jax.ShapeDtypeStruct((n_dest, news_rows(n_dest), 128), BF16),
         ),
         in_specs=[smem, smem, smem, vmem, vmem],
         out_specs=(vmem, vmem),
@@ -1324,137 +1344,182 @@
     )(tab, me, loss, asked, payload)
 
 
-RING = 4
+def update_slots(tab, half, rest, grads, places, scale, arrays, outs, held, in_sems, out_sems):
+    slots = held.shape[1]
+    first_scale = -RATE / (1.0 - BETA_ONE**STEP)
+    second_scale = 1.0 / (1.0 - BETA_TWO**STEP)
+    rows = (pl.ds(pl.multiple_of(half * HALF, HALF), HALF), slice(None))
+    columns = (slice(None), pl.ds(pl.multiple_of(half * 128, 128), 128))
+    whole = (slice(None), slice(None))
+
+    def each(i, action):
+        kind = tab[i, TAB_KIND]
+
+        def other():
+            pl.when(kind == KIND_DENSE)(lambda: action(KIND_DENSE, columns))
+            if rest:
+                pl.when(kind != KIND_DENSE)(lambda: action(KIND_PLACE, whole))
+
+        lax.cond(kind == KIND_TABLE, lambda: action(KIND_TABLE, rows), other)
+
+    def loop(act):
+        def body(i, c):
+            each(i, partial(act, i))
+            return c
+
+        lax.fori_loop(0, slots, body, 0)
+
+    def in_copies(i, region):
+        return [
+            pltpu.make_async_copy(a.at[(i,) + region], held.at[(k, i) + region], in_sems.at[k, i])
+            for k, a in enumerate(arrays)
+        ]
+
+    def out_copies(i, region):
+        return [
+            pltpu.make_async_copy(held.at[(k, i) + region], out.at[(i,) + region], out_sems.at[k, i])
+            for k, out in enumerate(outs)
+        ]
+
+    def start(i, case, region):
+        for copy in in_copies(i, region):
+            copy.start()
+
+    def step(i, region, g):
+        g = g * scale[: g.shape[0], : g.shape[1]]
+        m1 = BETA_ONE * held[(1, i) + region] + (1.0 - BETA_ONE) * g
+        m2 = BETA_TWO * held[(2, i) + region] + (1.0 - BETA_TWO) * (g * g)
+        root = jnp.sqrt(m2 * second_scale) + EPSILON
+        held[(0, i) + region] = (
+            held[(0, i) + region] * (1.0 - RATE * DECAY) + (m1 * first_scale) / root
+        )
+        held[(1, i) + region] = m1
+        held[(2, i) + region] = m2
+
+    def act(i, case, region):
+        for copy in in_copies(i, region):
+            copy.wait()
+        if case == KIND_TABLE:
+            step(i, region, grads[i].astype(F32))
+        elif case == KIND_DENSE:
+            g = grads[i].astype(F32)
+            step(i, region, jnp.concatenate([g[:, :128], g[:, 128:]], 0))
+        else:
+
+            @pl.when(tab[i, TAB_KIND] > 0)
+            def _():
+                spot = pl.multiple_of((tab[i, TAB_KIND] - KIND_PLACE) * UNIT, UNIT)
+                step(i, region, places[pl.ds(spot, UNIT), :])
+
+        for copy in out_copies(i, region):
+            copy.start()
+
+    def finish(i, case, region):
+        for copy in out_copies(i, region):
+            copy.wait()
+
+    loop(start)
+    yield
+    loop(act)
+    loop(finish)
+    yield
 
 
 def update_kernel(
-    pr, tab, me, news, places, own, other, weight, first, second, vectors, vector_first,
-    vector_second, weight_out, first_out, second_out, vectors_out, vector_first_out,
-    vector_second_out, loss_out, norm_out, grad, held, done, in_sems, sems,
+    tab, me, news, own, weight, first, second, vectors, vector_first, vector_second,
+    weight_out, first_out, second_out, vectors_out, vector_first_out, vector_second_out, loss_out,
+    norm_out, factor_out, places, held, in_sems, out_sems,
 ):
-    n_dest = news.shape[0] // pr
-    slots = weight.shape[0]
-
-    def in_copies(i):
-        return [
-            pltpu.make_async_copy(a.at[i], held.at[k, i], in_sems.at[k, i])
-            for k, a in enumerate((weight, first, second))
-        ]
-
-    def fetch_one(i, c):
-        for copy in in_copies(i):
-            copy.start()
-        return c
-
-    lax.fori_loop(0, slots, fetch_one, 0)
-    extra = news[:, D:].astype(F32).reshape(n_dest, pr, 128)
-    square = jnp.sum(jnp.sum(extra[:, 3:6, :], 0), 0, keepdims=True)
+    n_dest = news.shape[0]
+    pr = place_rows(n_dest)
+    share = PLEN // n_dest
+    scale = factor_out
+    steps = update_slots(
+        tab, me[1], True, own, places, scale, (weight, first, second),
+        (weight_out, first_out, second_out), held, in_sems, out_sems,
+    )
+    next(steps)
+    extras = []
+    for d in range(n_dest):
+        part = news[d].astype(F32)
+        places[d * share : (d + 1) * share, :128] = part[:share]
+        places[d * share : (d + 1) * share, 128:] = part[pr : pr + share]
+        extras.append(part[2 * pr :])
+    sums = extras[0]
+    for extra in extras[1:]:
+        sums = sums + extra
+    square = sums[1:2] + sums[2:3] + sums[3:4]
     norm = jnp.sqrt(square)
     factor = CLIP_AT / jnp.maximum(norm, CLIP_AT)
     norm_out[0, 0] = norm[0, 0]
-    loss = jnp.sum(jnp.sum(extra[0:2, 6:9, :], 0), 0, keepdims=True)
+    losses = extras[0] + extras[1]
+    loss = losses[4:5] + losses[5:6] + losses[6:7]
     loss_out[0, 0] = loss[0, 0]
-    pairs = jnp.sum(extra[:32, 0:3, :], 1).reshape(16, 2, 128)
-    vector_grad = jnp.concatenate([pairs[:, 0], pairs[:, 1]], 1) * factor[:, :1]
+    vector_grad = jnp.concatenate(
+        [
+            jnp.concatenate([extras[2 * i][0:1], extras[2 * i + 1][0:1]], 1)
+            for i in range(vectors.shape[0])
+        ],
+        0,
+    ) * jnp.concatenate([factor, factor], 1)
     v, m1, m2 = adam_step(
         vectors[...], vector_first[...], vector_second[...], vector_grad, VECTOR_RATE, 0.0
     )
     vectors_out[...] = v
     vector_first_out[...] = m1
     vector_second_out[...] = m2
-    flip = me[1] == 0
-    scale = jnp.broadcast_to(jnp.concatenate([factor, factor], 1), (UNIT, D))
-    first_scale = -RATE / (1.0 - BETA_ONE**STEP)
-    second_scale = 1.0 / (1.0 - BETA_TWO**STEP)
-
-    def out_copies(i, b):
-        return [
-            pltpu.make_async_copy(done.at[b, k], out.at[i], sems.at[b, k])
-            for k, out in enumerate((weight_out, first_out, second_out))
-        ]
-
-    def one(i, c):
-        kind = tab[i, TAB_KIND]
-        b = lax.rem(i, RING)
-        mine = own[i].astype(F32)
-        theirs = other[i].astype(F32)
-        lower = jnp.where(flip, mine, theirs)
-        upper = jnp.where(flip, theirs, mine)
-
-        @pl.when(kind == KIND_TABLE)
-        def _():
-            grad[:HALF] = lower
-            grad[HALF:] = upper
-
-        @pl.when(kind == KIND_DENSE)
-        def _():
-            grad[:HALF, :128] = lower[:, :128]
-            grad[HALF:, :128] = lower[:, 128:]
-            grad[:HALF, 128:] = upper[:, :128]
-            grad[HALF:, 128:] = upper[:, 128:]
-
-        @pl.when((kind >= KIND_PLACE) & (kind < KIND_DENSE))
-        def _():
-            spot = pl.multiple_of((kind - KIND_PLACE) * UNIT, UNIT)
-            grad[...] = places[pl.ds(spot, UNIT), :D].astype(F32)
-
-        @pl.when(i >= RING)
-        def _():
-            for copy in out_copies(i - RING, b):
-                copy.wait()
-
-        for copy in in_copies(i):
-            copy.wait()
-
-        @pl.when(kind == 0)
-        def _():
-            for k in range(3):
-                done[b, k] = held[k, i]
-
-        @pl.when(kind > 0)
-        def _():
-            g = grad[...] * scale
-            m1 = BETA_ONE * held[1, i] + (1.0 - BETA_ONE) * g
-            m2 = BETA_TWO * held[2, i] + (1.0 - BETA_TWO) * (g * g)
-            root = jnp.sqrt(m2 * second_scale) + EPSILON
-            done[b, 0] = held[0, i] * (1.0 - RATE * DECAY) + (m1 * first_scale) / root
-            done[b, 1] = m1
-            done[b, 2] = m2
-
-        for copy in out_copies(i, b):
-            copy.start()
-        return c
-
-    lax.fori_loop(0, slots, one, 0)
-    for i in range(max(slots - RING, 0), slots):
-        for copy in out_copies(i, i % RING):
-            copy.wait()
-
-
-def update(tab, me, news, own, other, weights, first, second, vectors, vector_first, vector_second, pr):
-    n_dest = news.shape[0] // pr
-    share = PLEN // n_dest
-    places = news
-    if share < pr:
-        places = news.reshape(n_dest, pr, -1)[:, :share].reshape(PLEN, -1)
-    big = jax.ShapeDtypeStruct(weights.shape, F32)
+    factor_out[...] = jnp.broadcast_to(jnp.concatenate([factor, factor], 1), (UNIT, D))
+    next(steps)
+
+
+def finish_kernel(
+    tab, me, factor, other, weight, first, second, weight_in, first_in, second_in, weight_out,
+    first_out, second_out, held, in_sems, out_sems,
+):
+    steps = update_slots(
+        tab, 1 - me[1], False, other, None, factor, (weight, first, second),
+        (weight_out, first_out, second_out), held, in_sems, out_sems,
+    )
+    next(steps)
+    next(steps)
+
+
+def update_scratch(shape):
+    return [
+        pltpu.VMEM((3,) + shape, F32),
+        pltpu.SemaphoreType.DMA((3, shape[0])),
+        pltpu.SemaphoreType.DMA((3, shape[0])),
+    ]
+
+
+def update(tab, me, news, own, weights, first, second, vectors, vector_first, vector_second):
+    n_dest = news.shape[0]
+    big = pltpu.HBM(weights.shape, F32)
     small = jax.ShapeDtypeStruct(vectors.shape, F32)
     one = jax.ShapeDtypeStruct((1, 1), F32)
     return pl.pallas_call(
-        partial(update_kernel, pr),
-        out_shape=(big, big, big, small, small, small, one, one),
-        in_specs=[smem, smem] + [vmem] * 4 + [hbm] * 3 + [vmem] * 3,
-        out_specs=(hbm, hbm, hbm, vmem, vmem, vmem, smem, smem),
-        scratch_shapes=[
-            pltpu.VMEM((UNIT, D), F32),
-            pltpu.VMEM((3,) + weights.shape, F32),
-            pltpu.VMEM((RING, 3, UNIT, D), F32),
-            pltpu.SemaphoreType.DMA((3, weights.shape[0])),
-            pltpu.SemaphoreType.DMA((RING, 3)),
-        ],
+        update_kernel,
+        out_shape=(big, big, big, small, small, small, one, one, jax.ShapeDtypeStruct((UNIT, D), F32)),
+        in_specs=[smem, smem] + [vmem] * 2 + [in_hbm] * 3 + [vmem] * 3,
+        out_specs=(in_hbm, in_hbm, in_hbm, vmem, vmem, vmem, smem, smem, vmem),
+        scratch_shapes=[pltpu.VMEM((PLEN, D), F32)] + update_scratch(weights.shape),
         compiler_params=params(n_dest // 2, 14),
         name="update",
-    )(tab, me, news, places, own, other, weights, first, second, vectors, vector_first, vector_second)
+    )(tab, me, news, own, *stay(weights, first, second), vectors, vector_first, vector_second)
+
+
+def finish(tab, me, factor, other, weights, first, second, started, n_blk):
+    big = pltpu.HBM(weights.shape, F32)
+    return pl.pallas_call(
+        finish_kernel,
+        out_shape=(big, big, big),
+        in_specs=[smem, smem, vmem, vmem] + [in_hbm] * 6,
+        out_specs=(in_hbm, in_hbm, in_hbm),
+        scratch_shapes=update_scratch(weights.shape),
+        input_output_aliases={7: 0, 8: 1, 9: 2},
+        compiler_params=params(n_blk, 14),
+        name="finish",
+    )(tab, me, factor, other, *stay(weights, first, second, *started))
 
 
 def quick(
@@ -1466,6 +1531,7 @@
     n_blk = lax.axis_size("blk")
     everyone = ("blk", "rep")
     cap = 48 if n_blk <= 16 else 16
+    take_cap = 40 if n_blk <= 16 else 16
     me = jnp.stack([lax.axis_index("blk"), lax.axis_index("rep")]).astype(I32)
 
     def exchange(a, axes):
@@ -1473,11 +1539,11 @@
 
     message, where_row, tab = request(
         owners, me, positive, query_lengths, passage_lengths, query_ids[0], passage_ids[0],
-        weights, n_blk, cap,
+        weights, n_blk, cap, take_cap,
     )
     message = exchange(message, everyone)
     first = along_z(collect(tab, me, message), n_blk)
-    rows, message = fetch(me, message, weights, cap)
+    rows, message = fetch(message, weights, cap, take_cap)
     rows, first = lax.optimization_barrier((rows, first))
     rows = exchange(rows, everyone)
     gathered = spread(first, n_blk)
@@ -1494,9 +1560,12 @@
     own, news = reduce(tab, me, loss, asked, payload, slots, cap)
     other = lax.ppermute(own, "rep", [(0, 1), (1, 0)])
     news = exchange(news, everyone)
-    *outs, loss_sum, norm = update(
-        tab, me, news, own, other, weights, first_moments, second_moments, vectors, vector_first,
-        vector_second, place_rows(2 * n_blk),
+    *outs, loss_sum, norm, factor = update(
+        tab, me, news, own, weights, first_moments, second_moments, vectors, vector_first,
+        vector_second,
+    )
+    outs[:3] = finish(
+        tab, me, factor, other, weights, first_moments, second_moments, outs[:3], n_blk
     )
 
     def general(carry):

time: 172 us -> 164 us (0.953)
  waiting for transfers between devices: 77.7 us -> 67.6 us
  Pallas kernels: 36.4 us -> 38.5 us
    ppermute x1, waiting for transfers between devices: 16.4 us -> 1.16 us  [quick(): other = lax.ppermute(own, 'rep', [(0, 1), (1, 0)])]
    all_to_all x3, waiting for transfers between devices: 40.2 us -> 47.9 us  [exchange(): return lax.all_to_all(a, axes, 0, 0, tiled=True)]
    pallas_call x3 -> x4, Pallas kernels: 15.5 us -> 18.8 us  [the longest x1 5.4 us: update(): pl.pallas_call(update_kernel, out_shape=(big, big, big, small, small, sma...]
  transfers between devices with their start and end apart: 14 -> 14, of which waited for: 6 -> 6; matrix products, arithmetic and copies ran while one was open for 1% -> 1% of each run, Pallas kernels for 2% -> 6%
where the time goes in v3:
time: 164 us; the launch traced here: 163 us
  waiting for transfers between devices  67.6 us (41%)
  Pallas kernels  38.5 us (23%)
  blocking collectives  32.1 us (20%)
  starting transfers between devices  20.6 us (13%)
    all_to_all x3, waiting for transfers between devices, exchange(): return lax.all_to_all(a, axes, 0, 0, tiled=True)  47.9 us
    all_to_all x2, blocking collectives, exchange(): return lax.all_to_all(a, axes, 0, 0, tiled=True)  32.1 us
    ppermute x1, waiting for transfers between devices, spread(): arrays = [first, lax.ppermute(first, 'rep', [(0, 1), (1, 0)])]  11 us
    all_to_all x3, starting transfers between devices, exchange(): return lax.all_to_all(a, axes, 0, 0, tiled=True)  9.36 us
    ppermute x9, waiting for transfers between devices, across(): return lax.ppermute(values, 'blk', pairs)  7.61 us
    ppermute x9, starting transfers between devices, across(): return lax.ppermute(values, 'blk', pairs)  7.54 us
    pallas_call x1, Pallas kernels, backward(): pl.pallas_call(partial(backward_kernel, cap), out_shape=(jax.ShapeDtypeSt...  6.93 us
    pallas_call x1, Pallas kernels, reduce(): pl.pallas_call(partial(reduce_kernel, slots, cap), out_shape=(jax.ShapeDt...  5.96 us
  transfers between devices with their start and end apart: 14, of which 6 were waited for; matrix products, arithmetic and copies ran while one was open for 1% of the time, Pallas kernels for 6%

profile of v3, /device:TPU:0, one launch (start us, length us, event | category | flops | bytes accessed | tf_op | source)
XLA Modules:
  0.0 163.2 jit_solution(15205402657273018040)
XLA Ops:
  0.7 0.7 reshape.1271.owner_line
  1.5 4.3 %request.1 = (bf16[32,40,128]{2,1,0:T(8,128)(2,1)S(1)}, s32[2,1280]{1,0:T(2,128)S(1)}, s32[32,128]{1,0:T(8,128)S(1)}) custom-call(s32[269]{0:T(512)} %owners.1, s32[2]{0:T(128)S(1)} %pad_add_fusion.me, s32[1,2]{1,0:T(1,128)} %positive.3, s32[1,2]{1,0:T(1,128)} %query_lengths.3, s32[1,2]{1,0:T(1,128)} %passage_lengths.3, s32[1,269]{1,0:T(1,128)S(1)} %reshape.1271.owner_line, ...), custom_call_target="tpu_custom_call" | custom-call | tf_op jit(solution)/shard_map/request/pallas_call | solution.py:774
  5.8 18.8 %all_to_all.74.message = bf16[32,40,128]{2,1,0:T(8,128)(2,1)S(1)} all-to-all(bf16[32,40,128]{2,1,0:T(8,128)(2,1)S(1)} %get-tuple-element.314), channel_id=1, replica_groups=mesh['blk'=16,'rep'=2] {'blk','rep'}, dimensions={0} | all-to-all | bytes 655360 | tf_op jit(solution)/shard_map/all_to_all | solution.py:1538
  24.6 1.4 collect.1
  26.0 0.1 collective-permute-start
  26.1 1.3 collective-permute-start.1
  27.4 2.8 %collective-permute-start.2 = (bf16[15,16,128]{2,1,0:T(8,128)(2,1)S(1)}, bf16[15,16,128]{2,1,0:T(8,128)(2,1)S(1)}, u32[]{:S(2)}, u32[]{:S(2)}) collective-permute-start(bf16[15,16,128]{2,1,0:T(8,128)(2,1)S(1)} %collect.1), channel_id=1, source_target_pairs={{0,24},{2,26},{4,28},{6,30},{8,0},{10,2},{12,4},{14,6},{16,8},{18,... | collective-permute-start | bytes 184328 | tf_op jit(solution)/shard_map/ppermute | solution.py:552
  30.3 4.5 %fetch.1 = (bf16[1280,256]{1,0:T(8,128)(2,1)}, s32[32,128]{1,0:T(8,128)S(1)}) custom-call(bf16[32,40,128]{2,1,0:T(8,128)(2,1)S(1)} %all_to_all.74.message, f32[17,128,256]{2,1,0:T(8,128)} %weight.3), custom_call_target="tpu_custom_call" | custom-call | tf_op jit(solution)/shard_map/fetch/pallas_call | solution.py:845
  34.8 2.9 %all-to-all-start.9 = ((bf16[32,40,256]{2,1,0:T(8,128)(2,1)}), bf16[32,40,256]{2,1,0:T(8,128)(2,1)S(1)}, u32[]{:S(2)}, u32[]{:S(2)}) async-start(bf16[32,40,256]{2,1,0:T(8,128)(2,1)} %bitcast.138), calls=%async_computation.9 | async-start | bytes 1310720 | tf_op jit(solution)/shard_map/all_to_all | solution.py:1538
  37.7 1.8 %collective-permute-start.3 = (bf16[4,15,16,128]{3,2,1,0:T(8,128)(2,1)S(1)}, bf16[4,15,16,128]{3,2,1,0:T(8,128)(2,1)S(1)}, u32[]{:S(2)}, u32[]{:S(2)}) collective-permute-start(bf16[4,15,16,128]{3,2,1,0:T(8,128)(2,1)S(1)} %pad_maximum_fusion.7.g0), channel_id=1, source_target_pairs={{0,1},{1,0},{2,3},{3,2},{4,5},{5,4},{6,7},{7,6},{8,9},{9,8},{10,11... | collective-permute-start | bytes 737288 | tf_op jit(solution)/shard_map/ppermute | solution.py:562
  39.5 1.5 collective-permute-start.4
  41.0 11.0 %collective-permute-done.3.g1 = bf16[4,15,16,128]{3,2,1,0:T(8,128)(2,1)S(1)} collective-permute-done((bf16[4,15,16,128]{3,2,1,0:T(8,128)(2,1)S(1)}, bf16[4,15,16,128]{3,2,1,0:T(8,128)(2,1)S(1)}, u32[]{:S(2)}, u32[]{:S(2)}) %collective-permute-start.3) | collective-permute-done | bytes 245792 | tf_op jit(solution)/shard_map/ppermute | solution.py:562
  52.0 1.2 collective-permute-start.5
  53.2 0.5 collective-permute-start.7
  53.8 6.1 %collective-permute-done.5.g3 = bf16[4,15,16,128]{3,2,1,0:T(8,128)(2,1)S(1)} collective-permute-done((bf16[4,15,16,128]{3,2,1,0:T(8,128)(2,1)S(1)}, bf16[4,15,16,128]{3,2,1,0:T(8,128)(2,1)S(1)}, u32[]{:S(2)}, u32[]{:S(2)}) %collective-permute-start.5) | collective-permute-done | bytes 245792 | tf_op jit(solution)/shard_map/ppermute | solution.py:552
  60.0 1.5 collective-permute-done.9.g7
  61.5 0.6 copy-done.110
  62.2 5.4 %forward.1 = (bf16[128,384]{1,0:T(8,128)(2,1)S(1)}, bf16[1280,256]{1,0:T(8,128)(2,1)S(1)}, f32[1280,256]{1,0:T(8,128)S(1)}, f32[1280,128]{1,0:T(8,128)S(1)}, f32...) custom-call(s32[32,128]{1,0:T(8,128)S(1)} %get-tuple-element.316.tab, ...), custom_call_target="tpu_custom_call" | custom-call | tf_op jit(solution)/shard_map/forward/pallas_call | solution.py:965
  67.5 13.3 %all_to_all.75 = bf16[16,8,384]{2,1,0:T(8,128)(2,1)S(1)} all-to-all(bf16[16,8,384]{2,1,0:T(8,128)(2,1)S(1)} %bitcast.453), channel_id=1, replica_groups=mesh['blk'=16,'rep'=2] {'blk'}, dimensions={0} | all-to-all | bytes 196608 | tf_op jit(solution)/shard_map/all_to_all | solution.py:1538
  80.8 6.9 %backward.1 = (bf16[32,200,128]{2,1,0:T(8,128)(2,1)}, f32[1,1]{1,0:T(1,128)}, f32[1,1]{1,0:T(1,128)}) custom-call(s32[32,128]{1,0:T(8,128)S(1)} %get-tuple-element.316.tab, s32[2]{0:T(128)S(1)} %pad_add_fusion.me, s32[6]{0:T(128)S(1)} %copy-done.149, f32[6]{0:T(128)S(1)} %copy-done.151, bf16[128,384]{1,0:T(8,128)(2,1)S(1)} %bitcast.450, ...), custom_call_target="tpu_custom_call" | custom-call | tf_op jit(solution)/shard_map/backward/pallas_call | solution.py:1227
  87.8 2.7 %all-to-all-start.11 = ((bf16[32,200,128]{2,1,0:T(8,128)(2,1)}), bf16[32,200,128]{2,1,0:T(8,128)(2,1)S(1)}, u32[]{:S(2)}, u32[]{:S(2)}) async-start(bf16[32,200,128]{2,1,0:T(8,128)(2,1)} %get-tuple-element.329), calls=%async_computation.11 | async-start | bytes 3276800 | tf_op jit(solution)/shard_map/all_to_all | solution.py:1538
  90.5 0.1 reshape.1272.asked
  90.6 38.8 %all-to-all-done.11.payload = bf16[32,200,128]{2,1,0:T(8,128)(2,1)S(1)} async-done(((bf16[32,200,128]{2,1,0:T(8,128)(2,1)}), bf16[32,200,128]{2,1,0:T(8,128)(2,1)S(1)}, u32[]{:S(2)}, u32[]{:S(2)}) %all-to-all-start.11) | async-done | bytes 1638432 | tf_op jit(solution)/shard_map/all_to_all | solution.py:1538
  129.3 6.0 %reduce.47 = (bf16[17,64,256]{2,1,0:T(8,128)(2,1)S(1)}, bf16[32,40,128]{2,1,0:T(8,128)(2,1)}) custom-call(s32[32,128]{1,0:T(8,128)S(1)} %get-tuple-element.316.tab, s32[2]{0:T(128)S(1)} %pad_add_fusion.me, f32[1,1]{1,0:T(1,128)} %get-tuple-element.328.loss, s32[1,1536]{1,0:T(1,128)S(1)} %reshape.1272.asked, bf16[32,200,128]{2,1,0:T(8,128)(2,1)S(1)} %all-to-all-done.11.payload), custom_call_target="tpu_custom_call" | custom-call | tf_op jit(solution)/shard_map/reduce/pallas_call | solution.py:1328
  135.3 3.8 %all-to-all-start.12 = ((bf16[32,40,128]{2,1,0:T(8,128)(2,1)}), bf16[32,40,128]{2,1,0:T(8,128)(2,1)S(1)}, u32[]{:S(2)}, u32[]{:S(2)}) async-start(bf16[32,40,128]{2,1,0:T(8,128)(2,1)} %get-tuple-element.330), calls=%async_computation.12 | async-start | bytes 655360 | tf_op jit(solution)/shard_map/all_to_all | solution.py:1538
  139.1 1.8 %collective-permute-start.10 = (bf16[17,64,256]{2,1,0:T(8,128)(2,1)S(1)}, bf16[17,64,256]{2,1,0:T(8,128)(2,1)S(1)}, u32[]{:S(2)}, u32[]{:S(2)}) collective-permute-start(bf16[17,64,256]{2,1,0:T(8,128)(2,1)S(1)} %get-tuple-element.331.own), channel_id=1, source_target_pairs={{0,1},{1,0},{2,3},{3,2},{4,5},{5,4},{6,7},{7,6},{8,9},{9,8},{10,11... | collective-permute-start | bytes 1671176 | tf_op jit(solution)/shard_map/ppermute | solution.py:1561
  140.9 0.8 slice_reduce_fusion
  141.7 9.1 %all-to-all-done.12.news = bf16[32,40,128]{2,1,0:T(8,128)(2,1)S(1)} async-done(((bf16[32,40,128]{2,1,0:T(8,128)(2,1)}), bf16[32,40,128]{2,1,0:T(8,128)(2,1)S(1)}, u32[]{:S(2)}, u32[]{:S(2)}) %all-to-all-start.12) | async-done | bytes 327712 | tf_op jit(solution)/shard_map/all_to_all | solution.py:1538
  150.8 5.4 %update.1 = (f32[17,128,256]{2,1,0:T(8,128)}, f32[17,128,256]{2,1,0:T(8,128)}, f32[17,128,256]{2,1,0:T(8,128)}, f32[16,256]{1,0:T(8,128)}, f32[16,256]{1,0:T(8,1...) custom-call(s32[32,128]{1,0:T(8,128)S(1)} %get-tuple-element.316.tab, ...), custom_call_target="tpu_custom_call" | custom-call | tf_op jit(solution)/shard_map/update/pallas_call | solution.py:1500
  156.2 1.2 collective-permute-done.10.other
  157.4 4.7 %finish.1 = (f32[17,128,256]{2,1,0:T(8,128)}, f32[17,128,256]{2,1,0:T(8,128)}, f32[17,128,256]{2,1,0:T(8,128)}) custom-call(s32[32,128]{1,0:T(8,128)S(1)} %get-tuple-element.316.tab, s32[2]{0:T(128)S(1)} %pad_add_fusion.me, f32[128,256]{1,0:T(8,128)S(1)} %get-tuple-element.332.factor, ...), custom_call_target="tpu_custom_call", output_to_operand_aliasing={{0}: (7, {}), {1}: (8, {}), {2}: (9, {})} | custom-call | tf_op jit(solution)/shard_map/finish/pallas_call | solution.py:1513
  162.1 0.9 while.66
  (50 shorter events, 0.3 us)
Async XLA Ops:
  0.6 61.5 %copy-start.163 = (s32[1,2]{1,0:T(1,128)S(1)}, s32[1,2]{1,0:T(1,128)}, u32[]{:S(2)}) copy-start(s32[1,2]{1,0:T(1,128)} %query_lengths.3) | copy-start | bytes 28
  0.7 61.5 %copy-start.158 = (s32[1,2]{1,0:T(1,128)S(1)}, s32[1,2]{1,0:T(1,128)}, u32[]{:S(2)}) copy-start(s32[1,2]{1,0:T(1,128)} %passage_lengths.3) | copy-start | bytes 28
  0.7 61.5 %copy-start.160 = (s32[1,2]{1,0:T(1,128)S(1)}, s32[1,2]{1,0:T(1,128)}, u32[]{:S(2)}) copy-start(s32[1,2]{1,0:T(1,128)} %positive.3) | copy-start | bytes 28
  0.7 61.5 %copy-start.49 = (f32[16,256]{1,0:T(8,128)S(1)}, f32[16,256]{1,0:T(8,128)}, u32[]{:S(2)}) copy-start(f32[16,256]{1,0:T(8,128)} %vectors.5) | copy-start | bytes 49156
  5.7 75.1 %copy-start.149 = (s32[6]{0:T(128)S(1)}, s32[6]{0:T(128)}, u32[]{:S(2)}) copy-start(s32[6]{0:T(128)} %prefix_lengths.1) | copy-start | bytes 76
  5.7 75.1 %copy-start.151 = (f32[6]{0:T(128)S(1)}, f32[6]{0:T(128)}, u32[]{:S(2)}) copy-start(f32[6]{0:T(128)} %prefix_weights.1) | copy-start | bytes 76
  26.0 8.8 %collective-permute-start = (bf16[15,16,128]{2,1,0:T(8,128)(2,1)S(1)}, bf16[15,16,128]{2,1,0:T(8,128)(2,1)S(1)}, u32[]{:S(2)}, u32[]{:S(2)}) collective-permute-start(bf16[15,16,128]{2,1,0:T(8,128)(2,1)S(1)} %collect.1), channel_id=1, source_target_pairs={{0,8},{2,10},{4,12},{6,14},{8,16},{10,18},{12,20},{14,22},{16,24},... | collective-permute-start | bytes 184328 | tf_op jit(solution)/shard_map/ppermute | solution.py:552
  26.1 8.6 %collective-permute-start.1 = (bf16[15,16,128]{2,1,0:T(8,128)(2,1)S(1)}, bf16[15,16,128]{2,1,0:T(8,128)(2,1)S(1)}, u32[]{:S(2)}, u32[]{:S(2)}) collective-permute-start(bf16[15,16,128]{2,1,0:T(8,128)(2,1)S(1)} %collect.1), channel_id=1, source_target_pairs={{0,16},{2,18},{4,20},{6,22},{8,24},{10,26},{12,28},{14,30},{16,0},... | collective-permute-start | bytes 184328 | tf_op jit(solution)/shard_map/ppermute | solution.py:552
  27.4 7.3 %collective-permute-start.2 = (bf16[15,16,128]{2,1,0:T(8,128)(2,1)S(1)}, bf16[15,16,128]{2,1,0:T(8,128)(2,1)S(1)}, u32[]{:S(2)}, u32[]{:S(2)}) collective-permute-start(bf16[15,16,128]{2,1,0:T(8,128)(2,1)S(1)} %collect.1), channel_id=1, source_target_pairs={{0,24},{2,26},{4,28},{6,30},{8,0},{10,2},{12,4},{14,6},{16,8},{18,... | collective-permute-start | bytes 184328 | tf_op jit(solution)/shard_map/ppermute | solution.py:552
  34.8 26.6 %copy-start.64 = (bf16[4,15,16,128]{3,2,1,0:T(8,128)(2,1)}, bf16[4,15,16,128]{3,2,1,0:T(8,128)(2,1)S(1)}, u32[]{:S(2)}) copy-start(bf16[4,15,16,128]{3,2,1,0:T(8,128)(2,1)S(1)} %pad_maximum_fusion.7.g0) | copy-start | bytes 737284
  34.8 26.6 %all-to-all-start.9 = ((bf16[32,40,256]{2,1,0:T(8,128)(2,1)}), bf16[32,40,256]{2,1,0:T(8,128)(2,1)S(1)}, u32[]{:S(2)}, u32[]{:S(2)}) async-start(bf16[32,40,256]{2,1,0:T(8,128)(2,1)} %bitcast.138), calls=%async_computation.9 | async-start | bytes 1310720 | tf_op jit(solution)/shard_map/all_to_all | solution.py:1538
  37.7 14.3 %collective-permute-start.3 = (bf16[4,15,16,128]{3,2,1,0:T(8,128)(2,1)S(1)}, bf16[4,15,16,128]{3,2,1,0:T(8,128)(2,1)S(1)}, u32[]{:S(2)}, u32[]{:S(2)}) collective-permute-start(bf16[4,15,16,128]{3,2,1,0:T(8,128)(2,1)S(1)} %pad_maximum_fusion.7.g0), channel_id=1, source_target_pairs={{0,1},{1,0},{2,3},{3,2},{4,5},{5,4},{6,7},{7,6},{8,9},{9,8},{10,11... | collective-permute-start | bytes 737288 | tf_op jit(solution)/shard_map/ppermute | solution.py:562
  39.5 14.2 %collective-permute-start.4 = (bf16[4,15,16,128]{3,2,1,0:T(8,128)(2,1)S(1)}, bf16[4,15,16,128]{3,2,1,0:T(8,128)(2,1)S(1)}, u32[]{:S(2)}, u32[]{:S(2)}) collective-permute-start(bf16[4,15,16,128]{3,2,1,0:T(8,128)(2,1)S(1)} %pad_maximum_fusion.7.g0), channel_id=1, source_target_pairs={{0,4},{2,6},{4,0},{6,2},{8,12},{10,14},{12,8},{14,10},{16,20},{18,... | collective-permute-start | bytes 737288 | tf_op jit(solution)/shard_map/ppermute | solution.py:552
  52.0 9.5 %copy-start.104 = (bf16[4,15,16,128]{3,2,1,0:T(8,128)(2,1)}, bf16[4,15,16,128]{3,2,1,0:T(8,128)(2,1)S(1)}, u32[]{:S(2)}) copy-start(bf16[4,15,16,128]{3,2,1,0:T(8,128)(2,1)S(1)} %collective-permute-done.3.g1) | copy-start | bytes 737284
  52.0 7.9 %collective-permute-start.5 = (bf16[4,15,16,128]{3,2,1,0:T(8,128)(2,1)S(1)}, bf16[4,15,16,128]{3,2,1,0:T(8,128)(2,1)S(1)}, u32[]{:S(2)}, u32[]{:S(2)}) collective-permute-start(bf16[4,15,16,128]{3,2,1,0:T(8,128)(2,1)S(1)} %collective-permute-done.3.g1), channel_id=1, source_target_pairs={{0,4},{2,6},{4,0},{6,2},{8,12},{10,14},{12,8},{14,10},{16,20},{18,... | collective-permute-start | bytes 737288 | tf_op jit(solution)/shard_map/ppermute | solution.py:552
  53.2 6.7 %collective-permute-start.6 = (bf16[4,15,16,128]{3,2,1,0:T(8,128)(2,1)S(1)}, bf16[4,15,16,128]{3,2,1,0:T(8,128)(2,1)S(1)}, u32[]{:S(2)}, u32[]{:S(2)}) collective-permute-start(bf16[4,15,16,128]{3,2,1,0:T(8,128)(2,1)S(1)} %pad_maximum_fusion.7.g0), channel_id=1, source_target_pairs={{0,2},{2,0},{4,6},{6,4},{8,10},{10,8},{12,14},{14,12},{16,18},{18,... | collective-permute-start | bytes 737288 | tf_op jit(solution)/shard_map/ppermute | solution.py:552
  53.2 6.8 %collective-permute-start.7 = (bf16[4,15,16,128]{3,2,1,0:T(8,128)(2,1)S(1)}, bf16[4,15,16,128]{3,2,1,0:T(8,128)(2,1)S(1)}, u32[]{:S(2)}, u32[]{:S(2)}) collective-permute-start(bf16[4,15,16,128]{3,2,1,0:T(8,128)(2,1)S(1)} %collective-permute-done.3.g1), channel_id=1, source_target_pairs={{0,2},{2,0},{4,6},{6,4},{8,10},{10,8},{12,14},{14,12},{16,18},{18,... | collective-permute-start | bytes 737288 | tf_op jit(solution)/shard_map/ppermute | solution.py:552
  53.7 7.8 %copy-start.105 = (bf16[4,15,16,128]{3,2,1,0:T(8,128)(2,1)}, bf16[4,15,16,128]{3,2,1,0:T(8,128)(2,1)S(1)}, u32[]{:S(2)}) copy-start(bf16[4,15,16,128]{3,2,1,0:T(8,128)(2,1)S(1)} %collective-permute-done.4.g2) | copy-start | bytes 737284
  53.7 6.3 %collective-permute-start.8 = (bf16[4,15,16,128]{3,2,1,0:T(8,128)(2,1)S(1)}, bf16[4,15,16,128]{3,2,1,0:T(8,128)(2,1)S(1)}, u32[]{:S(2)}, u32[]{:S(2)}) collective-permute-start(bf16[4,15,16,128]{3,2,1,0:T(8,128)(2,1)S(1)} %collective-permute-done.4.g2), channel_id=1, source_target_pairs={{0,2},{2,0},{4,6},{6,4},{8,10},{10,8},{12,14},{14,12},{16,18},{18,... | collective-permute-start | bytes 737288 | tf_op jit(solution)/shard_map/ppermute | solution.py:552
  59.9 1.5 copy-start.106
  59.9 1.5 collective-permute-start.9
  59.9 1.5 copy-start.107
  59.9 1.5 copy-start.108
  60.0 1.5 copy-start.109
  80.8 70.0 %copy-start.83 = (f32[16,256]{1,0:T(8,128)S(1)}, f32[16,256]{1,0:T(8,128)}, u32[]{:S(2)}) copy-start(f32[16,256]{1,0:T(8,128)} %vector_first.1) | copy-start | bytes 49156
  80.8 70.0 %copy-start.85 = (f32[16,256]{1,0:T(8,128)S(1)}, f32[16,256]{1,0:T(8,128)}, u32[]{:S(2)}) copy-start(f32[16,256]{1,0:T(8,128)} %vector_second.1) | copy-start | bytes 49156
  87.8 41.6 %all-to-all-start.11 = ((bf16[32,200,128]{2,1,0:T(8,128)(2,1)}), bf16[32,200,128]{2,1,0:T(8,128)(2,1)S(1)}, u32[]{:S(2)}, u32[]{:S(2)}) async-start(bf16[32,200,128]{2,1,0:T(8,128)(2,1)} %get-tuple-element.329), calls=%async_computation.11 | async-start | bytes 3276800 | tf_op jit(solution)/shard_map/all_to_all | solution.py:1538
  135.3 15.5 %all-to-all-start.12 = ((bf16[32,40,128]{2,1,0:T(8,128)(2,1)}), bf16[32,40,128]{2,1,0:T(8,128)(2,1)S(1)}, u32[]{:S(2)}, u32[]{:S(2)}) async-start(bf16[32,40,128]{2,1,0:T(8,128)(2,1)} %get-tuple-element.330), calls=%async_computation.12 | async-start | bytes 655360 | tf_op jit(solution)/shard_map/all_to_all | solution.py:1538
  139.1 18.3 %collective-permute-start.10 = (bf16[17,64,256]{2,1,0:T(8,128)(2,1)S(1)}, bf16[17,64,256]{2,1,0:T(8,128)(2,1)S(1)}, u32[]{:S(2)}, u32[]{:S(2)}) collective-permute-start(bf16[17,64,256]{2,1,0:T(8,128)(2,1)S(1)} %get-tuple-element.331.own), channel_id=1, source_target_pairs={{0,1},{1,0},{2,3},{3,2},{4,5},{5,4},{6,7},{7,6},{8,9},{9,8},{10,11... | collective-permute-start | bytes 1671176 | tf_op jit(solution)/shard_map/ppermute | solution.py:1561
  157.4 4.7 %copy-start.62 = (s32[1,2,512]{2,1,0:T(2,128)S(1)}, s32[1,2,512]{2,1,0:T(2,128)}, u32[]{:S(2)}) copy-start(s32[1,2,512]{2,1,0:T(2,128)} %param.35) | copy-start | bytes 12292
  157.4 4.7 %copy-start.81 = (s32[269]{0:T(512)S(1)}, s32[269]{0:T(512)}, u32[]{:S(2)}) copy-start(s32[269]{0:T(512)} %owners.1) | copy-start | bytes 3232
  157.4 4.7 %copy-start.153 = (s32[1,2,128]{2,1,0:T(2,128)S(1)}, s32[1,2,128]{2,1,0:T(2,128)}, u32[]{:S(2)}) copy-start(s32[1,2,128]{2,1,0:T(2,128)} %param.34) | copy-start | bytes 3076
  (1 other events, 0.7 us)

commit v4 on v3

--- a/solution.py
+++ b/solution.py
@@ -473,7 +473,7 @@
 AT_UP = AT_O + D
 AT_DOWN = AT_UP + FF
 
-TAB_OWNER, TAB_RANK, TAB_SLOT, TAB_UNIT, TAB_KIND, TAB_ORDER = range(6)
+TAB_OWNER, TAB_RANK, TAB_SLOT, TAB_UNIT, TAB_KIND, TAB_ORDER, TAB_SORTED, TAB_ENDS = range(8)
 PIECE = 16
 PIECES = 16
 DENSE_CAP = 8
@@ -622,7 +622,7 @@
 
     before, have = lax.fori_loop(0, DENSE, take, (0, 0))
     owner_row[...] = jnp.full(owner_row.shape, -1, I32)
-    owner_row[:, :n_units] = owner_line[...]
+    owner_row[:, :n_units] = owner_line[...].reshape(1, n_units)
     every_slot = owner_row[...]
     wide = every_slot.shape[1]
     base = n_units - DENSE
@@ -659,6 +659,24 @@
     )
     here = (every_slot == me[0] * slots + iota((32, wide), 0)) & (which < n_units)
     kind = jnp.sum(jnp.where(here, code, 0), 1, keepdims=True)
+    sort = jnp.where(
+        kind == KIND_TABLE,
+        0,
+        jnp.where(kind == KIND_DENSE, 1, jnp.where(kind >= KIND_PLACE, 2, 3)),
+    )
+    sort = jnp.where(iota((32, 1), 0) < slots, sort, 4)
+
+    def to_row(column):
+        wide = jnp.concatenate([column, jnp.full((96, 1), 5, I32)], 0)
+        return jnp.broadcast_to(wide, (128, 128)).T[:1]
+
+    sort_row = to_row(sort)
+    ahead = (sort_row < sort) | ((sort_row == sort) & (block_row < block_column))
+    place_row = to_row(jnp.sum(ahead.astype(I32), 1, keepdims=True))
+    sorted_slot = jnp.sum(
+        jnp.where((place_row == block_column) & (block_row < 32), block_row, 0), 1, keepdims=True
+    )
+    ends = jnp.sum((sort_row <= iota((32, 1), 0)).astype(I32), 1, keepdims=True)
     entry = block_row
     tab[...] = jnp.where(
         entry == TAB_OWNER,
@@ -672,7 +690,15 @@
                 jnp.where(
                     entry == TAB_UNIT,
                     jnp.minimum(unit, UNITS_L - 2),
-                    jnp.where(entry == TAB_KIND, kind, jnp.minimum(order, DENSE - 1)),
+                    jnp.where(
+                        entry == TAB_KIND,
+                        kind,
+                        jnp.where(
+                            entry == TAB_ORDER,
+                            jnp.minimum(order, DENSE - 1),
+                            jnp.where(entry == TAB_SORTED, sorted_slot, ends),
+                        ),
+                    ),
                 ),
             ),
         ),
@@ -699,27 +725,31 @@
     dest = owner * n_rep + upper
     local_row = inside * HALF + row - upper * HALF
     token = jnp.where(live, token, -1)
-    first_at = jnp.full((128, TOKENS), TOKENS, I32)
-    for at in range(0, TOKENS, 128):
-        column = to_column(token[:, at : at + 128])
-        same = column == token
-        first_at = jnp.minimum(first_at, jnp.where(same, iota((128, TOKENS), 0) + at, TOKENS))
-    first_at = jnp.min(first_at, 0, keepdims=True)
+    first_at = []
+    columns = [to_column(token[:, at : at + 128]) for at in range(0, TOKENS, 128)]
+    for to_at in range(0, TOKENS, 128):
+        best = jnp.full((128, 128), TOKENS, I32)
+        for at in range(0, to_at + 128, 128):
+            same = columns[at // 128] == token[:, to_at : to_at + 128]
+            best = jnp.minimum(best, jnp.where(same, iota((128, 128), 0) + at, TOKENS))
+        first_at.append(jnp.min(best, 0, keepdims=True))
+    first_at = jnp.concatenate(first_at, 1)
     first = live & (first_at == lane)
     chosen = ((iota((n_dest, TOKENS), 0) == dest) & first).astype(F32)
     chosen_low = chosen.astype(BF16)
-    seen = jnp.zeros((n_dest, TOKENS), F32)
-    for at in range(0, TOKENS, 128):
-        earlier = ((iota((128, TOKENS), 0) + at) < first_at).astype(F32).astype(BF16)
-        seen = seen + dot_nn(chosen_low[:, at : at + 128], earlier)
+    seen = []
+    for to_at in range(0, TOKENS, 256):
+        above = to_at + 256
+        earlier = iota((above, 256), 0) < first_at[:, to_at:above]
+        seen.append(dot_nn(chosen_low[:, :above], earlier.astype(F32).astype(BF16)))
+    seen = jnp.concatenate(seen, 1)
     to = iota((n_dest, TOKENS), 0)
     rank = jnp.sum(jnp.where(to == dest, seen, 0.0), 0, keepdims=True).astype(I32)
     turn = jnp.sum(jnp.where(to // n_rep == owner, seen, 0.0), 0, keepdims=True).astype(I32)
-    source = owner * n_rep + turn % n_rep
-    spot = turn // n_rep
-    where_row[0:1] = jnp.where(live & (spot < take_cap), source * take_cap + spot, -1)
+    source = owner * n_rep + me[1]
+    where_row[0:1] = jnp.where(live & (turn < take_cap), owner * take_cap + turn, -1)
     where_row[1:2] = jnp.where(live & (rank < cap), dest * cap + rank, -1)
-    over = jnp.max((live & ((rank >= cap) | (spot >= take_cap))).astype(I32))
+    over = jnp.max((live & ((rank >= cap) | (turn >= take_cap))).astype(I32))
 
     def listed(dest, spot, code):
         high = code // 32
@@ -730,7 +760,7 @@
         both = dot_nt(both.astype(BF16), spread)
         return both[:n_dest], both[n_dest:]
 
-    take_high, take_low = listed(source, spot, inside * UNIT + row + 1)
+    take_high, take_low = listed(source, turn, inside * UNIT + row + 1)
     sent_high, sent_low = listed(dest, rank, local_row + 1)
     flag = jnp.maximum(over, crowded)
     column_of = iota((1, 128), 1)
@@ -770,7 +800,7 @@
     slots = weights.shape[0]
     n_dest = 2 * n_blk
     n_units = owners.shape[0]
-    owner_row = owners.reshape(1, n_units)
+    owner_row = owners
     return pl.pallas_call(
         partial(request_kernel, slots, n_blk, cap, take_cap),
         out_shape=(
@@ -814,7 +844,7 @@
     )(tab, me, message)
 
 
-def fetch_kernel(slots, cap, take_cap, message, weights, rows_out, asked_out, wanted, held, table, hot, sem):
+def fetch_kernel(slots, cap, take_cap, me, message, weights, rows_out, asked_out, wanted, held, table, sem):
     n_dest = message.shape[0]
     copy = pltpu.make_async_copy(weights, held, sem)
     copy.start()
@@ -822,7 +852,11 @@
     wanted[...] = jnp.zeros(wanted.shape, I32)
     for s in range(n_dest):
         part = message[s, AT_ASKED:].astype(F32)
-        wanted[s : s + 1] = (part[0:1] * 32.0 + part[1:2] - 1.0).astype(I32)
+        want = (part[0:1] * 32.0 + part[1:2] - 1.0).astype(I32)
+        if s % 2 == 0:
+            even = want
+        else:
+            wanted[s // 2 : s // 2 + 1] = jnp.where(me[1] == 0, even, want)
         marks = part[2:3]
         row = jnp.where(column_of < cap, part[3:4] * 32.0 + part[4:5] - 1.0, 0.0)
         for i in range(3):
@@ -830,36 +864,40 @@
         asked_out[s : s + 1] = row.astype(I32)
     wide = table.shape[0]
     columns = wanted[...].T
-    for s in range(n_dest):
-        hot[s * take_cap : (s + 1) * take_cap] = (
-            (iota((take_cap, wide), 1) == columns[:take_cap, s : s + 1]).astype(F32).astype(BF16)
-        )
     copy.wait()
     table[...] = held[...].reshape(wide, D).astype(BF16)
-    rows_out[...] = dot_nn(hot[...], table[...]).astype(BF16)
-
-
-def fetch(message, weights, cap, take_cap):
+    row_of = iota((take_cap, wide), 1)
+    for at in range(0, n_dest // 2, 4):
+        hot = jnp.concatenate(
+            [
+                (row_of == columns[:take_cap, s : s + 1]).astype(F32)
+                for s in range(at, at + 4)
+            ],
+            0,
+        ).astype(BF16)
+        rows_out[at * take_cap : (at + 4) * take_cap] = dot_nn(hot, table[...]).astype(BF16)
+
+
+def fetch(me, message, weights, cap, take_cap):
     slots = weights.shape[0]
     n_dest = message.shape[0]
     return pl.pallas_call(
         partial(fetch_kernel, slots, cap, take_cap),
         out_shape=(
-            jax.ShapeDtypeStruct((n_dest * take_cap, D), BF16),
+            jax.ShapeDtypeStruct((n_dest // 2 * take_cap, D), BF16),
             jax.ShapeDtypeStruct((n_dest, 128), I32),
         ),
-        in_specs=[vmem, in_hbm],
+        in_specs=[smem, vmem, in_hbm],
         out_specs=(vmem, vmem),
         scratch_shapes=[
-            pltpu.VMEM((-(-n_dest // 128) * 128, 128), I32),
+            pltpu.VMEM((-(-n_dest // 256) * 128, 128), I32),
             pltpu.VMEM(weights.shape, F32),
             pltpu.VMEM((slots * UNIT, D), BF16),
-            pltpu.VMEM((n_dest * take_cap, slots * UNIT), BF16),
             pltpu.SemaphoreType.DMA,
         ],
         compiler_params=params(n_dest // 2, 20),
         name="fetch",
-    )(message, *stay(weights))
+    )(me, message, *stay(weights))
 
 
 ST_POOLED, ST_C, ST_N2, ST_N1, ST_H, ST_O, ST_Q, ST_X0 = range(0, 64, 8)
@@ -876,10 +914,12 @@
     for copy in copies:
         copy.start()
     taken = rows.shape[0]
-    for at in range(0, TOKENS, 128):
-        column = to_column(where_row[0:1, at : at + 128])
-        hot = (iota((128, taken), 1) == column).astype(F32).astype(BF16)
-        embedded[at : at + 128] = dot_nn(hot, rows[...])
+    for at in range(0, TOKENS, 256):
+        column = jnp.concatenate(
+            [to_column(where_row[0:1, i : i + 128]) for i in (at, at + 128)], 0
+        )
+        hot = (iota((256, taken), 1) == column).astype(F32).astype(BF16)
+        embedded[at : at + 256] = dot_nn(hot, rows[...])
     for copy in copies:
         copy.wait()
     shift = vectors[0:1]
@@ -983,7 +1023,7 @@
         name="forward",
     )(
         tab, me, query_lengths, passage_lengths, positive, rows, where_row, vectors,
-        *[pltpu.with_memory_space_constraint(a, pltpu.HBM) for a in gathered],
+        *stay(*gathered[:4]), *gathered[4:],
     )
 
 
@@ -1127,7 +1167,7 @@
         dx[start : start + 256] = de
     de_low = dx[...].astype(BF16)
     at_place, at_left, at_right, n_rows = payload_rows(n_dest, cap)
-    per = max(128 // cap, 1)
+    per = 8
     step = per * cap
     for at in range(0, n_dest * cap, step):
         hot = ((iota((step, TOKENS), 0) + at) == where_row[1:2]).astype(F32).astype(BF16)
@@ -1254,9 +1294,10 @@
         right[d * 32 : (d + 1) * 32] = payload[d, at_right:n_rows].astype(F32)
     grads = row_grads[...]
     filled = slots * HALF
-    for at in range(0, filled, 64):
-        hot = ((iota((64, n_dest * cap), 0) + at) == asked[...]).astype(F32).astype(BF16)
-        total[at : at + 64] = dot_nn(hot, grads)
+    chunk = filled // 4
+    for at in range(0, filled, chunk):
+        hot = ((iota((chunk, n_dest * cap), 0) + at) == asked[...]).astype(F32).astype(BF16)
+        total[at : at + chunk] = dot_nn(hot, grads)
     mine = me[0]
     odd = me[1]
     column = iota((n_dest * 4, 128), 1)
@@ -1345,29 +1386,24 @@
 
 
 def update_slots(tab, half, rest, grads, places, scale, arrays, outs, held, in_sems, out_sems):
-    slots = held.shape[1]
     first_scale = -RATE / (1.0 - BETA_ONE**STEP)
     second_scale = 1.0 / (1.0 - BETA_TWO**STEP)
     rows = (pl.ds(pl.multiple_of(half * HALF, HALF), HALF), slice(None))
     columns = (slice(None), pl.ds(pl.multiple_of(half * 128, 128), 128))
     whole = (slice(None), slice(None))
-
-    def each(i, action):
-        kind = tab[i, TAB_KIND]
-
-        def other():
-            pl.when(kind == KIND_DENSE)(lambda: action(KIND_DENSE, columns))
-            if rest:
-                pl.when(kind != KIND_DENSE)(lambda: action(KIND_PLACE, whole))
-
-        lax.cond(kind == KIND_TABLE, lambda: action(KIND_TABLE, rows), other)
-
-    def loop(act):
-        def body(i, c):
-            each(i, partial(act, i))
-            return c
-
-        lax.fori_loop(0, slots, body, 0)
+    ends = [tab[k, TAB_ENDS] for k in range(4)]
+    spans = [(KIND_TABLE, 0, ends[0], rows), (KIND_DENSE, ends[0], ends[1], columns)]
+    if rest:
+        spans += [(KIND_PLACE, ends[1], ends[2], whole), (0, ends[2], ends[3], whole)]
+
+    def loop(action):
+        for case, start, stop, region in spans:
+
+            def body(j, c):
+                action(tab[j, TAB_SORTED], case, region)
+                return c
+
+            lax.fori_loop(start, stop, body, 0)
 
     def in_copies(i, region):
         return [
@@ -1404,12 +1440,9 @@
         elif case == KIND_DENSE:
             g = grads[i].astype(F32)
             step(i, region, jnp.concatenate([g[:, :128], g[:, 128:]], 0))
-        else:
-
-            @pl.when(tab[i, TAB_KIND] > 0)
-            def _():
-                spot = pl.multiple_of((tab[i, TAB_KIND] - KIND_PLACE) * UNIT, UNIT)
-                step(i, region, places[pl.ds(spot, UNIT), :])
+        elif case == KIND_PLACE:
+            spot = pl.multiple_of((tab[i, TAB_KIND] - KIND_PLACE) * UNIT, UNIT)
+            step(i, region, places[pl.ds(spot, UNIT), :])
 
         for copy in out_copies(i, region):
             copy.start()
@@ -1531,7 +1564,7 @@
     n_blk = lax.axis_size("blk")
     everyone = ("blk", "rep")
     cap = 48 if n_blk <= 16 else 16
-    take_cap = 40 if n_blk <= 16 else 16
+    take_cap = 80 if n_blk <= 16 else 32
     me = jnp.stack([lax.axis_index("blk"), lax.axis_index("rep")]).astype(I32)
 
     def exchange(a, axes):
@@ -1543,9 +1576,9 @@
     )
     message = exchange(message, everyone)
     first = along_z(collect(tab, me, message), n_blk)
-    rows, message = fetch(message, weights, cap, take_cap)
+    rows, message = fetch(me, message, weights, cap, take_cap)
     rows, first = lax.optimization_barrier((rows, first))
-    rows = exchange(rows, everyone)
+    rows = exchange(rows, "blk")
     gathered = spread(first, n_blk)
     emb, low, normed, scale, probs, state, matrices = forward(
         tab, me, query_lengths, passage_lengths, positive, rows, where_row, vectors, gathered, n_blk

time: 164 us -> 158 us (0.963)
  Pallas kernels: 38.5 us -> 36.2 us
    ppermute x1, waiting for transfers between devices: 11 us -> 5.37 us  [spread(): arrays = [first, lax.ppermute(first, 'rep', [(0, 1), (1, 0)])]]
    ppermute x9, waiting for transfers between devices: 7.61 us -> 11.7 us  [across(): return lax.ppermute(values, 'blk', pairs)]
  transfers between devices with their start and end apart: 14 -> 14, of which waited for: 6 -> 7; matrix products, arithmetic and copies ran while one was open for 1% -> 1% of each run, Pallas kernels for 6% -> 6%
where the time goes in v4:
time: 158 us; the launch traced here: 157 us
  waiting for transfers between devices  66.2 us (42%)
  Pallas kernels  36.2 us (23%)
  blocking collectives  30.8 us (19%)
  starting transfers between devices  20.8 us (13%)
    all_to_all x3, waiting for transfers between devices, exchange(): return lax.all_to_all(a, axes, 0, 0, tiled=True)  47.9 us
    all_to_all x2, blocking collectives, exchange(): return lax.all_to_all(a, axes, 0, 0, tiled=True)  30.8 us
    ppermute x9, waiting for transfers between devices, across(): return lax.ppermute(values, 'blk', pairs)  11.7 us
    all_to_all x3, starting transfers between devices, exchange(): return lax.all_to_all(a, axes, 0, 0, tiled=True)  9.72 us
    ppermute x9, starting transfers between devices, across(): return lax.ppermute(values, 'blk', pairs)  8.34 us
    pallas_call x1, Pallas kernels, backward(): pl.pallas_call(partial(backward_kernel, cap), out_shape=(jax.ShapeDtypeSt...  6.01 us
    pallas_call x1, Pallas kernels, forward(): pl.pallas_call(forward_kernel, out_shape=(jax.ShapeDtypeStruct((n_blk * 8...  5.42 us
    ppermute x1, waiting for transfers between devices, spread(): arrays = [first, lax.ppermute(first, 'rep', [(0, 1), (1, 0)])]  5.37 us
  transfers between devices with their start and end apart: 14, of which 7 were waited for; matrix products, arithmetic and copies ran while one was open for 1% of the time, Pallas kernels for 6%

profile of v4, /device:TPU:0, one launch (start us, length us, event | category | flops | bytes accessed | tf_op | source)
XLA Modules:
  0.0 157.2 jit_solution(785095486984771310)
XLA Ops:
  0.7 0.1 pad_add_fusion.me
  0.8 4.0 %request.1 = (bf16[32,40,128]{2,1,0:T(8,128)(2,1)S(1)}, s32[2,1280]{1,0:T(2,128)S(1)}, s32[32,128]{1,0:T(8,128)S(1)}) custom-call(s32[269]{0:T(512)} %owner_line.1, s32[2]{0:T(128)S(1)} %pad_add_fusion.me, s32[1,2]{1,0:T(1,128)} %positive.3, s32[1,2]{1,0:T(1,128)} %query_lengths.3, s32[1,2]{1,0:T(1,128)} %passage_lengths.3, s32[269]{0:T(512)} %owner_line.1, ...), custom_call_target="tpu_custom_call" | custom-call | tf_op jit(solution)/shard_map/request/pallas_call | solution.py:804
  4.8 18.8 %all_to_all.74.message = bf16[32,40,128]{2,1,0:T(8,128)(2,1)S(1)} all-to-all(bf16[32,40,128]{2,1,0:T(8,128)(2,1)S(1)} %get-tuple-element.314), channel_id=1, replica_groups=mesh['blk'=16,'rep'=2] {'blk','rep'}, dimensions={0} | all-to-all | bytes 655360 | tf_op jit(solution)/shard_map/all_to_all | solution.py:1571
  23.6 1.4 collect.1
  25.0 0.1 collective-permute-start
  25.2 1.3 collective-permute-start.1
  26.5 2.8 %collective-permute-start.2 = (bf16[15,16,128]{2,1,0:T(8,128)(2,1)S(1)}, bf16[15,16,128]{2,1,0:T(8,128)(2,1)S(1)}, u32[]{:S(2)}, u32[]{:S(2)}) collective-permute-start(bf16[15,16,128]{2,1,0:T(8,128)(2,1)S(1)} %collect.1), channel_id=1, source_target_pairs={{0,24},{2,26},{4,28},{6,30},{8,0},{10,2},{12,4},{14,6},{16,8},{18,... | collective-permute-start | bytes 184328 | tf_op jit(solution)/shard_map/ppermute | solution.py:552
  29.3 4.8 %fetch.1 = (bf16[1280,256]{1,0:T(8,128)(2,1)}, s32[32,128]{1,0:T(8,128)S(1)}) custom-call(s32[2]{0:T(128)S(1)} %pad_add_fusion.me, bf16[32,40,128]{2,1,0:T(8,128)(2,1)S(1)} %all_to_all.74.message, f32[17,128,256]{2,1,0:T(8,128)} %weight.3), custom_call_target="tpu_custom_call" | custom-call | tf_op jit(solution)/shard_map/fetch/pallas_call | solution.py:884
  34.2 3.6 %all-to-all-start.9 = ((bf16[16,80,256]{2,1,0:T(8,128)(2,1)}), bf16[16,80,256]{2,1,0:T(8,128)(2,1)S(1)}, u32[]{:S(2)}, u32[]{:S(2)}) async-start(bf16[16,80,256]{2,1,0:T(8,128)(2,1)} %bitcast.138), calls=%async_computation.9 | async-start | bytes 1310720 | tf_op jit(solution)/shard_map/all_to_all | solution.py:1571
  37.8 0.9 collective-permute-start.3
  38.7 1.9 %collective-permute-start.4 = (bf16[4,15,16,128]{3,2,1,0:T(8,128)(2,1)S(1)}, bf16[4,15,16,128]{3,2,1,0:T(8,128)(2,1)S(1)}, u32[]{:S(2)}, u32[]{:S(2)}) collective-permute-start(bf16[4,15,16,128]{3,2,1,0:T(8,128)(2,1)S(1)} %pad_maximum_fusion.7.g0), channel_id=1, source_target_pairs={{0,4},{2,6},{4,0},{6,2},{8,12},{10,14},{12,8},{14,10},{16,20},{18,... | collective-permute-start | bytes 737288 | tf_op jit(solution)/shard_map/ppermute | solution.py:552
  40.6 5.4 %collective-permute-done.3.g1 = bf16[4,15,16,128]{3,2,1,0:T(8,128)(2,1)S(1)} collective-permute-done((bf16[4,15,16,128]{3,2,1,0:T(8,128)(2,1)S(1)}, bf16[4,15,16,128]{3,2,1,0:T(8,128)(2,1)S(1)}, u32[]{:S(2)}, u32[]{:S(2)}) %collective-permute-start.3) | collective-permute-done | bytes 245792 | tf_op jit(solution)/shard_map/ppermute | solution.py:562
  46.0 1.7 %collective-permute-start.5 = (bf16[4,15,16,128]{3,2,1,0:T(8,128)(2,1)S(1)}, bf16[4,15,16,128]{3,2,1,0:T(8,128)(2,1)S(1)}, u32[]{:S(2)}, u32[]{:S(2)}) collective-permute-start(bf16[4,15,16,128]{3,2,1,0:T(8,128)(2,1)S(1)} %collective-permute-done.3.g1), channel_id=1, source_target_pairs={{0,4},{2,6},{4,0},{6,2},{8,12},{10,14},{12,8},{14,10},{16,20},{18,... | collective-permute-start | bytes 737288 | tf_op jit(solution)/shard_map/ppermute | solution.py:552
  47.6 0.5 collective-permute-start.7
  48.1 3.7 %collective-permute-done.4.g2 = bf16[4,15,16,128]{3,2,1,0:T(8,128)(2,1)S(1)} collective-permute-done((bf16[4,15,16,128]{3,2,1,0:T(8,128)(2,1)S(1)}, bf16[4,15,16,128]{3,2,1,0:T(8,128)(2,1)S(1)}, u32[]{:S(2)}, u32[]{:S(2)}) %collective-permute-start.4) | collective-permute-done | bytes 245792 | tf_op jit(solution)/shard_map/ppermute | solution.py:552
  51.9 6.5 %collective-permute-done.5.g3 = bf16[4,15,16,128]{3,2,1,0:T(8,128)(2,1)S(1)} collective-permute-done((bf16[4,15,16,128]{3,2,1,0:T(8,128)(2,1)S(1)}, bf16[4,15,16,128]{3,2,1,0:T(8,128)(2,1)S(1)}, u32[]{:S(2)}, u32[]{:S(2)}) %collective-permute-start.5) | collective-permute-done | bytes 245792 | tf_op jit(solution)/shard_map/ppermute | solution.py:552
  58.4 1.5 collective-permute-done.9.g7
  60.0 5.4 %forward.1 = (bf16[128,384]{1,0:T(8,128)(2,1)S(1)}, bf16[1280,256]{1,0:T(8,128)(2,1)S(1)}, f32[1280,256]{1,0:T(8,128)S(1)}, f32[1280,128]{1,0:T(8,128)S(1)}, f32...) custom-call(s32[32,128]{1,0:T(8,128)S(1)} %get-tuple-element.316.tab, ...), custom_call_target="tpu_custom_call" | custom-call | tf_op jit(solution)/shard_map/forward/pallas_call | solution.py:1005
  65.4 11.9 %all_to_all.75 = bf16[16,8,384]{2,1,0:T(8,128)(2,1)S(1)} all-to-all(bf16[16,8,384]{2,1,0:T(8,128)(2,1)S(1)} %bitcast.453), channel_id=1, replica_groups=mesh['blk'=16,'rep'=2] {'blk'}, dimensions={0} | all-to-all | bytes 196608 | tf_op jit(solution)/shard_map/all_to_all | solution.py:1571
  77.3 6.0 %backward.1 = (bf16[32,200,128]{2,1,0:T(8,128)(2,1)}, f32[1,1]{1,0:T(1,128)}, f32[1,1]{1,0:T(1,128)}) custom-call(s32[32,128]{1,0:T(8,128)S(1)} %get-tuple-element.316.tab, s32[2]{0:T(128)S(1)} %pad_add_fusion.me, s32[6]{0:T(128)S(1)} %copy-done.145, f32[6]{0:T(128)S(1)} %copy-done.147, bf16[128,384]{1,0:T(8,128)(2,1)S(1)} %bitcast.450, ...), custom_call_target="tpu_custom_call" | custom-call | tf_op jit(solution)/shard_map/backward/pallas_call | solution.py:1267
  83.4 2.7 %all-to-all-start.11 = ((bf16[32,200,128]{2,1,0:T(8,128)(2,1)}), bf16[32,200,128]{2,1,0:T(8,128)(2,1)S(1)}, u32[]{:S(2)}, u32[]{:S(2)}) async-start(bf16[32,200,128]{2,1,0:T(8,128)(2,1)} %get-tuple-element.329), calls=%async_computation.11 | async-start | bytes 3276800 | tf_op jit(solution)/shard_map/all_to_all | solution.py:1571
  86.1 0.1 reshape.1268.asked
  86.2 38.8 %all-to-all-done.11.payload = bf16[32,200,128]{2,1,0:T(8,128)(2,1)S(1)} async-done(((bf16[32,200,128]{2,1,0:T(8,128)(2,1)}), bf16[32,200,128]{2,1,0:T(8,128)(2,1)S(1)}, u32[]{:S(2)}, u32[]{:S(2)}) %all-to-all-start.11) | async-done | bytes 1638432 | tf_op jit(solution)/shard_map/all_to_all | solution.py:1571
  124.9 4.6 %reduce.47 = (bf16[17,64,256]{2,1,0:T(8,128)(2,1)S(1)}, bf16[32,40,128]{2,1,0:T(8,128)(2,1)}) custom-call(s32[32,128]{1,0:T(8,128)S(1)} %get-tuple-element.316.tab, s32[2]{0:T(128)S(1)} %pad_add_fusion.me, f32[1,1]{1,0:T(1,128)} %get-tuple-element.328.loss, s32[1,1536]{1,0:T(1,128)S(1)} %reshape.1268.asked, bf16[32,200,128]{2,1,0:T(8,128)(2,1)S(1)} %all-to-all-done.11.payload), custom_call_target="tpu_custom_call" | custom-call | tf_op jit(solution)/shard_map/reduce/pallas_call | solution.py:1369
  129.6 3.4 %all-to-all-start.12 = ((bf16[32,40,128]{2,1,0:T(8,128)(2,1)}), bf16[32,40,128]{2,1,0:T(8,128)(2,1)S(1)}, u32[]{:S(2)}, u32[]{:S(2)}) async-start(bf16[32,40,128]{2,1,0:T(8,128)(2,1)} %get-tuple-element.330), calls=%async_computation.12 | async-start | bytes 655360 | tf_op jit(solution)/shard_map/all_to_all | solution.py:1571
  133.0 1.8 %collective-permute-start.10 = (bf16[17,64,256]{2,1,0:T(8,128)(2,1)S(1)}, bf16[17,64,256]{2,1,0:T(8,128)(2,1)S(1)}, u32[]{:S(2)}, u32[]{:S(2)}) collective-permute-start(bf16[17,64,256]{2,1,0:T(8,128)(2,1)S(1)} %get-tuple-element.331.own), channel_id=1, source_target_pairs={{0,1},{1,0},{2,3},{3,2},{4,5},{5,4},{6,7},{7,6},{8,9},{9,8},{10,11... | collective-permute-start | bytes 1671176 | tf_op jit(solution)/shard_map/ppermute | solution.py:1594
  134.8 0.8 slice_reduce_fusion
  135.6 9.1 %all-to-all-done.12.news = bf16[32,40,128]{2,1,0:T(8,128)(2,1)S(1)} async-done(((bf16[32,40,128]{2,1,0:T(8,128)(2,1)}), bf16[32,40,128]{2,1,0:T(8,128)(2,1)S(1)}, u32[]{:S(2)}, u32[]{:S(2)}) %all-to-all-start.12) | async-done | bytes 327712 | tf_op jit(solution)/shard_map/all_to_all | solution.py:1571
  144.7 5.3 %update.1 = (f32[17,128,256]{2,1,0:T(8,128)}, f32[17,128,256]{2,1,0:T(8,128)}, f32[17,128,256]{2,1,0:T(8,128)}, f32[16,256]{1,0:T(8,128)}, f32[16,256]{1,0:T(8,1...) custom-call(s32[32,128]{1,0:T(8,128)S(1)} %get-tuple-element.316.tab, ...), custom_call_target="tpu_custom_call" | custom-call | tf_op jit(solution)/shard_map/update/pallas_call | solution.py:1533
  150.1 1.2 collective-permute-done.10.other
  151.3 4.7 %finish.1 = (f32[17,128,256]{2,1,0:T(8,128)}, f32[17,128,256]{2,1,0:T(8,128)}, f32[17,128,256]{2,1,0:T(8,128)}) custom-call(s32[32,128]{1,0:T(8,128)S(1)} %get-tuple-element.316.tab, s32[2]{0:T(128)S(1)} %pad_add_fusion.me, f32[128,256]{1,0:T(8,128)S(1)} %get-tuple-element.332.factor, ...), custom_call_target="tpu_custom_call", output_to_operand_aliasing={{0}: (7, {}), {1}: (8, {}), {2}: (9, {})} | custom-call | tf_op jit(solution)/shard_map/finish/pallas_call | solution.py:1546
  156.0 1.0 while.66
  (41 shorter events, 0.1 us)
Async XLA Ops:
  0.6 59.3 %copy-start.159 = (s32[1,2]{1,0:T(1,128)S(1)}, s32[1,2]{1,0:T(1,128)}, u32[]{:S(2)}) copy-start(s32[1,2]{1,0:T(1,128)} %query_lengths.3) | copy-start | bytes 28
  0.7 59.3 %copy-start.154 = (s32[1,2]{1,0:T(1,128)S(1)}, s32[1,2]{1,0:T(1,128)}, u32[]{:S(2)}) copy-start(s32[1,2]{1,0:T(1,128)} %passage_lengths.3) | copy-start | bytes 28
  0.7 59.3 %copy-start.156 = (s32[1,2]{1,0:T(1,128)S(1)}, s32[1,2]{1,0:T(1,128)}, u32[]{:S(2)}) copy-start(s32[1,2]{1,0:T(1,128)} %positive.3) | copy-start | bytes 28
  0.7 59.3 %copy-start.49 = (f32[16,256]{1,0:T(8,128)S(1)}, f32[16,256]{1,0:T(8,128)}, u32[]{:S(2)}) copy-start(f32[16,256]{1,0:T(8,128)} %vectors.5) | copy-start | bytes 49156
  4.8 72.5 %copy-start.145 = (s32[6]{0:T(128)S(1)}, s32[6]{0:T(128)}, u32[]{:S(2)}) copy-start(s32[6]{0:T(128)} %prefix_lengths.1) | copy-start | bytes 76
  4.8 72.5 %copy-start.147 = (f32[6]{0:T(128)S(1)}, f32[6]{0:T(128)}, u32[]{:S(2)}) copy-start(f32[6]{0:T(128)} %prefix_weights.1) | copy-start | bytes 76
  25.0 9.1 %collective-permute-start = (bf16[15,16,128]{2,1,0:T(8,128)(2,1)S(1)}, bf16[15,16,128]{2,1,0:T(8,128)(2,1)S(1)}, u32[]{:S(2)}, u32[]{:S(2)}) collective-permute-start(bf16[15,16,128]{2,1,0:T(8,128)(2,1)S(1)} %collect.1), channel_id=1, source_target_pairs={{0,8},{2,10},{4,12},{6,14},{8,16},{10,18},{12,20},{14,22},{16,24},... | collective-permute-start | bytes 184328 | tf_op jit(solution)/shard_map/ppermute | solution.py:552
  25.2 8.9 %collective-permute-start.1 = (bf16[15,16,128]{2,1,0:T(8,128)(2,1)S(1)}, bf16[15,16,128]{2,1,0:T(8,128)(2,1)S(1)}, u32[]{:S(2)}, u32[]{:S(2)}) collective-permute-start(bf16[15,16,128]{2,1,0:T(8,128)(2,1)S(1)} %collect.1), channel_id=1, source_target_pairs={{0,16},{2,18},{4,20},{6,22},{8,24},{10,26},{12,28},{14,30},{16,0},... | collective-permute-start | bytes 184328 | tf_op jit(solution)/shard_map/ppermute | solution.py:552
  26.5 7.6 %collective-permute-start.2 = (bf16[15,16,128]{2,1,0:T(8,128)(2,1)S(1)}, bf16[15,16,128]{2,1,0:T(8,128)(2,1)S(1)}, u32[]{:S(2)}, u32[]{:S(2)}) collective-permute-start(bf16[15,16,128]{2,1,0:T(8,128)(2,1)S(1)} %collect.1), channel_id=1, source_target_pairs={{0,24},{2,26},{4,28},{6,30},{8,0},{10,2},{12,4},{14,6},{16,8},{18,... | collective-permute-start | bytes 184328 | tf_op jit(solution)/shard_map/ppermute | solution.py:552
  34.2 25.7 %copy-start.64 = (bf16[4,15,16,128]{3,2,1,0:T(8,128)(2,1)}, bf16[4,15,16,128]{3,2,1,0:T(8,128)(2,1)S(1)}, u32[]{:S(2)}) copy-start(bf16[4,15,16,128]{3,2,1,0:T(8,128)(2,1)S(1)} %pad_maximum_fusion.7.g0) | copy-start | bytes 737284
  34.2 25.7 %all-to-all-start.9 = ((bf16[16,80,256]{2,1,0:T(8,128)(2,1)}), bf16[16,80,256]{2,1,0:T(8,128)(2,1)S(1)}, u32[]{:S(2)}, u32[]{:S(2)}) async-start(bf16[16,80,256]{2,1,0:T(8,128)(2,1)} %bitcast.138), calls=%async_computation.9 | async-start | bytes 1310720 | tf_op jit(solution)/shard_map/all_to_all | solution.py:1571
  37.8 8.2 %collective-permute-start.3 = (bf16[4,15,16,128]{3,2,1,0:T(8,128)(2,1)S(1)}, bf16[4,15,16,128]{3,2,1,0:T(8,128)(2,1)S(1)}, u32[]{:S(2)}, u32[]{:S(2)}) collective-permute-start(bf16[4,15,16,128]{3,2,1,0:T(8,128)(2,1)S(1)} %pad_maximum_fusion.7.g0), channel_id=1, source_target_pairs={{0,1},{1,0},{2,3},{3,2},{4,5},{5,4},{6,7},{7,6},{8,9},{9,8},{10,11... | collective-permute-start | bytes 737288 | tf_op jit(solution)/shard_map/ppermute | solution.py:562
  38.7 13.1 %collective-permute-start.4 = (bf16[4,15,16,128]{3,2,1,0:T(8,128)(2,1)S(1)}, bf16[4,15,16,128]{3,2,1,0:T(8,128)(2,1)S(1)}, u32[]{:S(2)}, u32[]{:S(2)}) collective-permute-start(bf16[4,15,16,128]{3,2,1,0:T(8,128)(2,1)S(1)} %pad_maximum_fusion.7.g0), channel_id=1, source_target_pairs={{0,4},{2,6},{4,0},{6,2},{8,12},{10,14},{12,8},{14,10},{16,20},{18,... | collective-permute-start | bytes 737288 | tf_op jit(solution)/shard_map/ppermute | solution.py:552
  46.0 13.9 %copy-start.104 = (bf16[4,15,16,128]{3,2,1,0:T(8,128)(2,1)}, bf16[4,15,16,128]{3,2,1,0:T(8,128)(2,1)S(1)}, u32[]{:S(2)}) copy-start(bf16[4,15,16,128]{3,2,1,0:T(8,128)(2,1)S(1)} %collective-permute-done.3.g1) | copy-start | bytes 737284
  46.0 12.4 %collective-permute-start.5 = (bf16[4,15,16,128]{3,2,1,0:T(8,128)(2,1)S(1)}, bf16[4,15,16,128]{3,2,1,0:T(8,128)(2,1)S(1)}, u32[]{:S(2)}, u32[]{:S(2)}) collective-permute-start(bf16[4,15,16,128]{3,2,1,0:T(8,128)(2,1)S(1)} %collective-permute-done.3.g1), channel_id=1, source_target_pairs={{0,4},{2,6},{4,0},{6,2},{8,12},{10,14},{12,8},{14,10},{16,20},{18,... | collective-permute-start | bytes 737288 | tf_op jit(solution)/shard_map/ppermute | solution.py:552
  47.6 10.8 %collective-permute-start.6 = (bf16[4,15,16,128]{3,2,1,0:T(8,128)(2,1)S(1)}, bf16[4,15,16,128]{3,2,1,0:T(8,128)(2,1)S(1)}, u32[]{:S(2)}, u32[]{:S(2)}) collective-permute-start(bf16[4,15,16,128]{3,2,1,0:T(8,128)(2,1)S(1)} %pad_maximum_fusion.7.g0), channel_id=1, source_target_pairs={{0,2},{2,0},{4,6},{6,4},{8,10},{10,8},{12,14},{14,12},{16,18},{18,... | collective-permute-start | bytes 737288 | tf_op jit(solution)/shard_map/ppermute | solution.py:552
  47.6 10.8 %collective-permute-start.7 = (bf16[4,15,16,128]{3,2,1,0:T(8,128)(2,1)S(1)}, bf16[4,15,16,128]{3,2,1,0:T(8,128)(2,1)S(1)}, u32[]{:S(2)}, u32[]{:S(2)}) collective-permute-start(bf16[4,15,16,128]{3,2,1,0:T(8,128)(2,1)S(1)} %collective-permute-done.3.g1), channel_id=1, source_target_pairs={{0,2},{2,0},{4,6},{6,4},{8,10},{10,8},{12,14},{14,12},{16,18},{18,... | collective-permute-start | bytes 737288 | tf_op jit(solution)/shard_map/ppermute | solution.py:552
  51.9 8.0 %copy-start.105 = (bf16[4,15,16,128]{3,2,1,0:T(8,128)(2,1)}, bf16[4,15,16,128]{3,2,1,0:T(8,128)(2,1)S(1)}, u32[]{:S(2)}) copy-start(bf16[4,15,16,128]{3,2,1,0:T(8,128)(2,1)S(1)} %collective-permute-done.4.g2) | copy-start | bytes 737284
  51.9 6.5 %collective-permute-start.8 = (bf16[4,15,16,128]{3,2,1,0:T(8,128)(2,1)S(1)}, bf16[4,15,16,128]{3,2,1,0:T(8,128)(2,1)S(1)}, u32[]{:S(2)}, u32[]{:S(2)}) collective-permute-start(bf16[4,15,16,128]{3,2,1,0:T(8,128)(2,1)S(1)} %collective-permute-done.4.g2), channel_id=1, source_target_pairs={{0,2},{2,0},{4,6},{6,4},{8,10},{10,8},{12,14},{14,12},{16,18},{18,... | collective-permute-start | bytes 737288 | tf_op jit(solution)/shard_map/ppermute | solution.py:552
  58.4 1.5 copy-start.106
  58.4 1.5 collective-permute-start.9
  77.3 67.4 %copy-start.83 = (f32[16,256]{1,0:T(8,128)S(1)}, f32[16,256]{1,0:T(8,128)}, u32[]{:S(2)}) copy-start(f32[16,256]{1,0:T(8,128)} %vector_first.1) | copy-start | bytes 49156
  77.3 67.4 %copy-start.85 = (f32[16,256]{1,0:T(8,128)S(1)}, f32[16,256]{1,0:T(8,128)}, u32[]{:S(2)}) copy-start(f32[16,256]{1,0:T(8,128)} %vector_second.1) | copy-start | bytes 49156
  83.4 41.6 %all-to-all-start.11 = ((bf16[32,200,128]{2,1,0:T(8,128)(2,1)}), bf16[32,200,128]{2,1,0:T(8,128)(2,1)S(1)}, u32[]{:S(2)}, u32[]{:S(2)}) async-start(bf16[32,200,128]{2,1,0:T(8,128)(2,1)} %get-tuple-element.329), calls=%async_computation.11 | async-start | bytes 3276800 | tf_op jit(solution)/shard_map/all_to_all | solution.py:1571
  129.6 15.1 %all-to-all-start.12 = ((bf16[32,40,128]{2,1,0:T(8,128)(2,1)}), bf16[32,40,128]{2,1,0:T(8,128)(2,1)S(1)}, u32[]{:S(2)}, u32[]{:S(2)}) async-start(bf16[32,40,128]{2,1,0:T(8,128)(2,1)} %get-tuple-element.330), calls=%async_computation.12 | async-start | bytes 655360 | tf_op jit(solution)/shard_map/all_to_all | solution.py:1571
  133.0 18.3 %collective-permute-start.10 = (bf16[17,64,256]{2,1,0:T(8,128)(2,1)S(1)}, bf16[17,64,256]{2,1,0:T(8,128)(2,1)S(1)}, u32[]{:S(2)}, u32[]{:S(2)}) collective-permute-start(bf16[17,64,256]{2,1,0:T(8,128)(2,1)S(1)} %get-tuple-element.331.own), channel_id=1, source_target_pairs={{0,1},{1,0},{2,3},{3,2},{4,5},{5,4},{6,7},{7,6},{8,9},{9,8},{10,11... | collective-permute-start | bytes 1671176 | tf_op jit(solution)/shard_map/ppermute | solution.py:1594
  151.3 4.7 %copy-start.62 = (s32[1,2,512]{2,1,0:T(2,128)S(1)}, s32[1,2,512]{2,1,0:T(2,128)}, u32[]{:S(2)}) copy-start(s32[1,2,512]{2,1,0:T(2,128)} %param.35) | copy-start | bytes 12292
  151.3 4.7 %copy-start.81 = (s32[269]{0:T(512)S(1)}, s32[269]{0:T(512)}, u32[]{:S(2)}) copy-start(s32[269]{0:T(512)} %owner_line.1) | copy-start | bytes 3232
  151.3 4.7 %copy-start.149 = (s32[1,2,128]{2,1,0:T(2,128)S(1)}, s32[1,2,128]{2,1,0:T(2,128)}, u32[]{:S(2)}) copy-start(s32[1,2,128]{2,1,0:T(2,128)} %param.34) | copy-start | bytes 3076

commit v5 on v4

--- a/solution.py
+++ b/solution.py
@@ -473,7 +473,9 @@
 AT_UP = AT_O + D
 AT_DOWN = AT_UP + FF
 
-TAB_OWNER, TAB_RANK, TAB_SLOT, TAB_UNIT, TAB_KIND, TAB_ORDER, TAB_SORTED, TAB_ENDS = range(8)
+TAB_OWNER, TAB_RANK, TAB_SLOT, TAB_UNIT, TAB_KIND, TAB_ORDER, TAB_SORTED, TAB_ENDS, TAB_SOURCE = range(
+    9
+)
 PIECE = 16
 PIECES = 16
 DENSE_CAP = 8
@@ -600,7 +602,7 @@
 
 def request_kernel(
     slots, n_blk, cap, take_cap, owners, me, positive, query_lengths, passage_lengths, owner_line,
-    query_ids, passage_ids, weights, message, where_row, tab, ids, owner_row, loaded, sems,
+    query_ids, passage_ids, weights, message, where_row, tab, ids, owner_row, asked, loaded, sems,
 ):
     n_rep = 2
     n_dest = n_blk * n_rep
@@ -670,6 +672,14 @@
         wide = jnp.concatenate([column, jnp.full((96, 1), 5, I32)], 0)
         return jnp.broadcast_to(wide, (128, 128)).T[:1]
 
+    capped = jnp.minimum(rank, DENSE_CAP - 1)
+    source = (2 * owner_column + capped // 2 % 2) * 2 + capped // 4
+    order = jnp.minimum(order, DENSE - 1)
+    by_order = jnp.sum(
+        jnp.where((to_row(order) == block_column) & (block_row < DENSE), to_row(source), 0),
+        1,
+        keepdims=True,
+    )
     sort_row = to_row(sort)
     ahead = (sort_row < sort) | ((sort_row == sort) & (block_row < block_column))
     place_row = to_row(jnp.sum(ahead.astype(I32), 1, keepdims=True))
@@ -695,8 +705,12 @@
                         kind,
                         jnp.where(
                             entry == TAB_ORDER,
-                            jnp.minimum(order, DENSE - 1),
-                            jnp.where(entry == TAB_SORTED, sorted_slot, ends),
+                            order,
+                            jnp.where(
+                                entry == TAB_SORTED,
+                                sorted_slot,
+                                jnp.where(entry == TAB_ENDS, ends, by_order),
+                            ),
                         ),
                     ),
                 ),
@@ -769,12 +783,12 @@
         positive[0, 0],
         jnp.where(column_of == 1, positive[0, 1], jnp.where(column_of == 2, flag, 0)),
     ).astype(F32)
-    row8 = iota((8, 128), 0)
-    for d in range(n_dest):
-        asked = jnp.where(row8 == 0, take_high[d : d + 1], marks)
-        for i, part in ((1, take_low), (3, sent_high), (4, sent_low)):
-            asked = jnp.where(row8 == i, part[d : d + 1], asked)
-        message[d, AT_ASKED:] = asked.astype(BF16)
+    asked[...] = jnp.zeros(asked.shape, F32)
+    for i, part in enumerate(
+        (take_high, take_low, jnp.broadcast_to(marks, (n_dest, 128)), sent_high, sent_low)
+    ):
+        asked[pl.ds(i, n_dest, stride=8), :] = part
+    message[:, AT_ASKED:, :] = asked[: 8 * n_dest].reshape(n_dest, 8, 128).astype(BF16)
     for spot in range(HELD):
         present = spot // 2 * 4 + 2 * me[1] + spot % 2 < have
 
@@ -813,6 +827,7 @@
         scratch_shapes=[
             pltpu.VMEM((1, TOKENS), I32),
             pltpu.VMEM((1, -(-n_units // 128) * 128), I32),
+            pltpu.VMEM((8 * n_dest + 8, 128), F32),
             pltpu.VMEM((HELD, UNIT, D), F32),
             pltpu.SemaphoreType.DMA((HELD,)),
         ],
@@ -822,15 +837,10 @@
 
 
 def collect_kernel(tab, me, message, mine_out):
-    for b in range(DENSE):
-        order = tab[b, TAB_ORDER]
-        rank = tab[b, TAB_RANK]
-
-        @pl.when(order % 2 == me[1])
-        def _():
-            spot = pl.multiple_of(rank // 4 * PIECE, PIECE)
-            sender = 2 * tab[b, TAB_OWNER] + rank // 2 % 2
-            mine_out[order // 2] = message[sender, pl.ds(spot, PIECE), :]
+    for k in range(CLASS):
+        source = tab[2 * k + me[1], TAB_SOURCE]
+        spot = pl.multiple_of(source % 2 * PIECE, PIECE)
+        mine_out[k] = message[source // 2, pl.ds(spot, PIECE), :]
 
 
 def collect(tab, me, message):
@@ -844,24 +854,25 @@
     )(tab, me, message)
 
 
-def fetch_kernel(slots, cap, take_cap, me, message, weights, rows_out, asked_out, wanted, held, table, sem):
+def fetch_kernel(slots, cap, take_cap, me, message, weights, rows_out, asked_out, lists, wanted, held, table, sem):
     n_dest = message.shape[0]
     copy = pltpu.make_async_copy(weights, held, sem)
     copy.start()
-    column_of = iota((1, 128), 1)
+    n_blk = n_dest // 2
+    lists[: 8 * n_dest] = message[:, AT_ASKED:, :].astype(F32).reshape(8 * n_dest, 128)
+    mine = 8 * me[1]
     wanted[...] = jnp.zeros(wanted.shape, I32)
-    for s in range(n_dest):
-        part = message[s, AT_ASKED:].astype(F32)
-        want = (part[0:1] * 32.0 + part[1:2] - 1.0).astype(I32)
-        if s % 2 == 0:
-            even = want
-        else:
-            wanted[s // 2 : s // 2 + 1] = jnp.where(me[1] == 0, even, want)
-        marks = part[2:3]
-        row = jnp.where(column_of < cap, part[3:4] * 32.0 + part[4:5] - 1.0, 0.0)
-        for i in range(3):
-            row = jnp.where(column_of == 124 + i, marks[:, i : i + 1], row)
-        asked_out[s : s + 1] = row.astype(I32)
+    wanted[:n_blk] = (
+        lists[pl.ds(mine, n_blk, stride=16), :] * 32.0
+        + lists[pl.ds(mine + 1, n_blk, stride=16), :]
+        - 1.0
+    ).astype(I32)
+    every = [lists[pl.ds(i, n_dest, stride=8), :] for i in (2, 3, 4)]
+    column_of = iota((n_dest, 128), 1)
+    row = jnp.where(column_of < cap, every[1] * 32.0 + every[2] - 1.0, 0.0)
+    for i in range(3):
+        row = jnp.where(column_of == 124 + i, every[0][:, i : i + 1], row)
+    asked_out[...] = row.astype(I32)
     wide = table.shape[0]
     columns = wanted[...].T
     copy.wait()
@@ -890,6 +901,7 @@
         in_specs=[smem, vmem, in_hbm],
         out_specs=(vmem, vmem),
         scratch_shapes=[
+            pltpu.VMEM((8 * n_dest + 16, 128), F32),
             pltpu.VMEM((-(-n_dest // 256) * 128, 128), I32),
             pltpu.VMEM(weights.shape, F32),
             pltpu.VMEM((slots * UNIT, D), BF16),
@@ -1274,7 +1286,7 @@
         in_specs=[smem] * 4 + [vmem] * 10,
         out_specs=(vmem, smem, smem),
         scratch_shapes=[
-            pltpu.VMEM((emb.shape[0] * 3, 128), F32),
+            pltpu.VMEM((emb.shape[0] * 3 + 8, 128), F32),
             pltpu.VMEM((emb.shape[0], D), F32),
             pltpu.VMEM((TOKENS, D), F32),
             pltpu.VMEM((n_dest * L_ROWS, 128), F32),
@@ -1377,21 +1389,25 @@
         scratch_shapes=[
             pltpu.VMEM((slots * HALF, D), F32),
             pltpu.VMEM((n_dest * cap, D), BF16),
-            pltpu.VMEM((n_dest * L_ROWS, 128), F32),
-            pltpu.VMEM((n_dest * 32, 128), F32),
+            pltpu.VMEM(((n_dest + 1) * L_ROWS, 128), F32),
+            pltpu.VMEM(((n_dest + 1) * 32, 128), F32),
         ],
         compiler_params=params(n_dest // 2, 16),
         name="reduce",
     )(tab, me, loss, asked, payload)
 
 
-def update_slots(tab, half, rest, grads, places, scale, arrays, outs, held, in_sems, out_sems):
+def update_slots(
+    tab, half, rest, grads, places, scale, arrays, outs, held, in_sems, out_sems, wanted=None
+):
     first_scale = -RATE / (1.0 - BETA_ONE**STEP)
     second_scale = 1.0 / (1.0 - BETA_TWO**STEP)
     rows = (pl.ds(pl.multiple_of(half * HALF, HALF), HALF), slice(None))
     columns = (slice(None), pl.ds(pl.multiple_of(half * 128, 128), 128))
     whole = (slice(None), slice(None))
     ends = [tab[k, TAB_ENDS] for k in range(4)]
+    if wanted is not None:
+        ends = [jnp.where(wanted, end, 0) for end in ends]
     spans = [(KIND_TABLE, 0, ends[0], rows), (KIND_DENSE, ends[0], ends[1], columns)]
     if rest:
         spans += [(KIND_PLACE, ends[1], ends[2], whole), (0, ends[2], ends[3], whole)]
@@ -1506,12 +1522,12 @@
 
 
 def finish_kernel(
-    tab, me, factor, other, weight, first, second, weight_in, first_in, second_in, weight_out,
+    full, tab, me, factor, other, weight, first, second, weight_in, first_in, second_in, weight_out,
     first_out, second_out, held, in_sems, out_sems,
 ):
     steps = update_slots(
         tab, 1 - me[1], False, other, None, factor, (weight, first, second),
-        (weight_out, first_out, second_out), held, in_sems, out_sems,
+        (weight_out, first_out, second_out), held, in_sems, out_sems, full[0] == 0,
     )
     next(steps)
     next(steps)
@@ -1541,18 +1557,18 @@
     )(tab, me, news, own, *stay(weights, first, second), vectors, vector_first, vector_second)
 
 
-def finish(tab, me, factor, other, weights, first, second, started, n_blk):
+def finish(full, tab, me, factor, other, weights, first, second, started, n_blk):
     big = pltpu.HBM(weights.shape, F32)
     return pl.pallas_call(
         finish_kernel,
         out_shape=(big, big, big),
-        in_specs=[smem, smem, vmem, vmem] + [in_hbm] * 6,
+        in_specs=[smem, smem, smem, vmem, vmem] + [in_hbm] * 6,
         out_specs=(in_hbm, in_hbm, in_hbm),
         scratch_shapes=update_scratch(weights.shape),
-        input_output_aliases={7: 0, 8: 1, 9: 2},
+        input_output_aliases={8: 0, 9: 1, 10: 2},
         compiler_params=params(n_blk, 14),
         name="finish",
-    )(tab, me, factor, other, *stay(weights, first, second, *started))
+    )(full, tab, me, factor, other, *stay(weights, first, second, *started))
 
 
 def quick(
@@ -1597,9 +1613,7 @@
         tab, me, news, own, weights, first_moments, second_moments, vectors, vector_first,
         vector_second,
     )
-    outs[:3] = finish(
-        tab, me, factor, other, weights, first_moments, second_moments, outs[:3], n_blk
-    )
+    outs = (*outs, loss_sum.reshape(()), count.reshape(()), norm.reshape(()))
 
     def general(carry):
         return 0, local(
@@ -1608,8 +1622,13 @@
             vector_second,
         )
 
-    outs = (*outs, loss_sum.reshape(()), count.reshape(()), norm.reshape(()))
-    return lax.while_loop(lambda c: c[0] > 0, general, (jnp.max(message[:, 126]), outs))[1]
+    full = jnp.max(message[:, 126])
+    outs = lax.while_loop(lambda c: c[0] > 0, general, (full, outs))[1]
+    finished = finish(
+        full.reshape(1), tab, me, factor, other, weights, first_moments, second_moments, outs[:3],
+        n_blk,
+    )
+    return (*finished, *outs[3:])
 
 
 def solution(mesh):

time: 158 us -> 157 us (level)
  transfers between devices with their start and end apart: 14 -> 14, of which waited for: 7 -> 7; matrix products, arithmetic and copies ran while one was open for 1% -> 1% of each run, Pallas kernels for 6% -> 7%
where the time goes in v5:
time: 157 us; the launch traced here: 156 us
  waiting for transfers between devices  65 us (41%)
  Pallas kernels  36.1 us (23%)
  blocking collectives  30.8 us (20%)
  starting transfers between devices  21.5 us (14%)
  between operations  1.78 us (1%)
    all_to_all x3, waiting for transfers between devices, exchange(): return lax.all_to_all(a, axes, 0, 0, tiled=True)  47 us
    all_to_all x2, blocking collectives, exchange(): return lax.all_to_all(a, axes, 0, 0, tiled=True)  30.8 us
    ppermute x9, waiting for transfers between devices, across(): return lax.ppermute(values, 'blk', pairs)  11.7 us
    all_to_all x3, starting transfers between devices, exchange(): return lax.all_to_all(a, axes, 0, 0, tiled=True)  10.4 us
    ppermute x9, starting transfers between devices, across(): return lax.ppermute(values, 'blk', pairs)  8.34 us
    pallas_call x1, Pallas kernels, backward(): pl.pallas_call(partial(backward_kernel, cap), out_shape=(jax.ShapeDtypeSt...  6.1 us
    pallas_call x1, Pallas kernels, update(): pl.pallas_call(update_kernel, out_shape=(big, big, big, small, small, sma...  5.69 us
    pallas_call x1, Pallas kernels, forward(): pl.pallas_call(forward_kernel, out_shape=(jax.ShapeDtypeStruct((n_blk * 8...  5.45 us
  transfers between devices with their start and end apart: 14, of which 7 were waited for; matrix products, arithmetic and copies ran while one was open for 1% of the time, Pallas kernels for 7%

profile of v5, /device:TPU:0, one launch (start us, length us, event | category | flops | bytes accessed | tf_op | source)
XLA Modules:
  0.0 156.2 jit_solution(9093269112823528817)
XLA Ops:
  0.6 0.0 copy-start.133
  0.7 0.1 pad_add_fusion.me
  0.8 4.1 %request.1 = (bf16[32,40,128]{2,1,0:T(8,128)(2,1)S(1)}, s32[2,1280]{1,0:T(2,128)S(1)}, s32[32,128]{1,0:T(8,128)S(1)}) custom-call(s32[269]{0:T(512)} %owner_line.1, s32[2]{0:T(128)S(1)} %pad_add_fusion.me, s32[1,2]{1,0:T(1,128)} %positive.3, s32[1,2]{1,0:T(1,128)} %query_lengths.3, s32[1,2]{1,0:T(1,128)} %passage_lengths.3, s32[269]{0:T(512)} %owner_line.1, ...), custom_call_target="tpu_custom_call" | custom-call | tf_op jit(solution)/shard_map/request/pallas_call | solution.py:818
  4.9 18.8 %all_to_all.74.message = bf16[32,40,128]{2,1,0:T(8,128)(2,1)S(1)} all-to-all(bf16[32,40,128]{2,1,0:T(8,128)(2,1)S(1)} %get-tuple-element.314), channel_id=1, replica_groups=mesh['blk'=16,'rep'=2] {'blk','rep'}, dimensions={0} | all-to-all | bytes 655360 | tf_op jit(solution)/shard_map/all_to_all | solution.py:1587
  23.7 0.9 collect.1
  24.6 0.1 collective-permute-start
  24.8 1.3 collective-permute-start.1
  26.1 2.8 %collective-permute-start.2 = (bf16[15,16,128]{2,1,0:T(8,128)(2,1)S(1)}, bf16[15,16,128]{2,1,0:T(8,128)(2,1)S(1)}, u32[]{:S(2)}, u32[]{:S(2)}) collective-permute-start(bf16[15,16,128]{2,1,0:T(8,128)(2,1)S(1)} %collect.1), channel_id=1, source_target_pairs={{0,24},{2,26},{4,28},{6,30},{8,0},{10,2},{12,4},{14,6},{16,8},{18,... | collective-permute-start | bytes 184328 | tf_op jit(solution)/shard_map/ppermute | solution.py:554
  28.9 4.8 %fetch.1 = (bf16[1280,256]{1,0:T(8,128)(2,1)}, s32[32,128]{1,0:T(8,128)S(1)}) custom-call(s32[2]{0:T(128)S(1)} %pad_add_fusion.me, bf16[32,40,128]{2,1,0:T(8,128)(2,1)S(1)} %all_to_all.74.message, f32[17,128,256]{2,1,0:T(8,128)} %weight.3), custom_call_target="tpu_custom_call" | custom-call | tf_op jit(solution)/shard_map/fetch/pallas_call | solution.py:895
  33.8 3.6 %all-to-all-start.9 = ((bf16[16,80,256]{2,1,0:T(8,128)(2,1)}), bf16[16,80,256]{2,1,0:T(8,128)(2,1)S(1)}, u32[]{:S(2)}, u32[]{:S(2)}) async-start(bf16[16,80,256]{2,1,0:T(8,128)(2,1)} %bitcast.139), calls=%async_computation.9 | async-start | bytes 1310720 | tf_op jit(solution)/shard_map/all_to_all | solution.py:1587
  37.4 0.9 collective-permute-start.3
  38.3 1.9 %collective-permute-start.4 = (bf16[4,15,16,128]{3,2,1,0:T(8,128)(2,1)S(1)}, bf16[4,15,16,128]{3,2,1,0:T(8,128)(2,1)S(1)}, u32[]{:S(2)}, u32[]{:S(2)}) collective-permute-start(bf16[4,15,16,128]{3,2,1,0:T(8,128)(2,1)S(1)} %pad_maximum_fusion.7.g0), channel_id=1, source_target_pairs={{0,4},{2,6},{4,0},{6,2},{8,12},{10,14},{12,8},{14,10},{16,20},{18,... | collective-permute-start | bytes 737288 | tf_op jit(solution)/shard_map/ppermute | solution.py:554
  40.2 5.4 %collective-permute-done.3.g1 = bf16[4,15,16,128]{3,2,1,0:T(8,128)(2,1)S(1)} collective-permute-done((bf16[4,15,16,128]{3,2,1,0:T(8,128)(2,1)S(1)}, bf16[4,15,16,128]{3,2,1,0:T(8,128)(2,1)S(1)}, u32[]{:S(2)}, u32[]{:S(2)}) %collective-permute-start.3) | collective-permute-done | bytes 245792 | tf_op jit(solution)/shard_map/ppermute | solution.py:564
  45.6 1.7 %collective-permute-start.5 = (bf16[4,15,16,128]{3,2,1,0:T(8,128)(2,1)S(1)}, bf16[4,15,16,128]{3,2,1,0:T(8,128)(2,1)S(1)}, u32[]{:S(2)}, u32[]{:S(2)}) collective-permute-start(bf16[4,15,16,128]{3,2,1,0:T(8,128)(2,1)S(1)} %collective-permute-done.3.g1), channel_id=1, source_target_pairs={{0,4},{2,6},{4,0},{6,2},{8,12},{10,14},{12,8},{14,10},{16,20},{18,... | collective-permute-start | bytes 737288 | tf_op jit(solution)/shard_map/ppermute | solution.py:554
  47.2 0.5 collective-permute-start.7
  47.7 3.7 %collective-permute-done.4.g2 = bf16[4,15,16,128]{3,2,1,0:T(8,128)(2,1)S(1)} collective-permute-done((bf16[4,15,16,128]{3,2,1,0:T(8,128)(2,1)S(1)}, bf16[4,15,16,128]{3,2,1,0:T(8,128)(2,1)S(1)}, u32[]{:S(2)}, u32[]{:S(2)}) %collective-permute-start.4) | collective-permute-done | bytes 245792 | tf_op jit(solution)/shard_map/ppermute | solution.py:554
  51.5 6.5 %collective-permute-done.5.g3 = bf16[4,15,16,128]{3,2,1,0:T(8,128)(2,1)S(1)} collective-permute-done((bf16[4,15,16,128]{3,2,1,0:T(8,128)(2,1)S(1)}, bf16[4,15,16,128]{3,2,1,0:T(8,128)(2,1)S(1)}, u32[]{:S(2)}, u32[]{:S(2)}) %collective-permute-start.5) | collective-permute-done | bytes 245792 | tf_op jit(solution)/shard_map/ppermute | solution.py:554
  58.0 1.5 collective-permute-done.9.g7
  59.6 5.4 %forward.1 = (bf16[128,384]{1,0:T(8,128)(2,1)S(1)}, bf16[1280,256]{1,0:T(8,128)(2,1)S(1)}, f32[1280,256]{1,0:T(8,128)S(1)}, f32[1280,128]{1,0:T(8,128)S(1)}, f32...) custom-call(s32[32,128]{1,0:T(8,128)S(1)} %get-tuple-element.316.tab, ...), custom_call_target="tpu_custom_call" | custom-call | tf_op jit(solution)/shard_map/forward/pallas_call | solution.py:1017
  65.0 11.9 %all_to_all.75 = bf16[16,8,384]{2,1,0:T(8,128)(2,1)S(1)} all-to-all(bf16[16,8,384]{2,1,0:T(8,128)(2,1)S(1)} %bitcast.454), channel_id=1, replica_groups=mesh['blk'=16,'rep'=2] {'blk'}, dimensions={0} | all-to-all | bytes 196608 | tf_op jit(solution)/shard_map/all_to_all | solution.py:1587
  77.0 6.1 %backward.1 = (bf16[32,200,128]{2,1,0:T(8,128)(2,1)}, f32[1,1]{1,0:T(1,128)}, f32[1,1]{1,0:T(1,128)}) custom-call(s32[32,128]{1,0:T(8,128)S(1)} %get-tuple-element.316.tab, s32[2]{0:T(128)S(1)} %pad_add_fusion.me, s32[6]{0:T(128)S(1)} %copy-done.120, f32[6]{0:T(128)S(1)} %copy-done.122, bf16[128,384]{1,0:T(8,128)(2,1)S(1)} %bitcast.451, ...), custom_call_target="tpu_custom_call" | custom-call | tf_op jit(solution)/shard_map/backward/pallas_call | solution.py:1279
  83.1 2.9 %all-to-all-start.11 = ((bf16[32,200,128]{2,1,0:T(8,128)(2,1)}), bf16[32,200,128]{2,1,0:T(8,128)(2,1)S(1)}, u32[]{:S(2)}, u32[]{:S(2)}) async-start(bf16[32,200,128]{2,1,0:T(8,128)(2,1)} %get-tuple-element.329), calls=%async_computation.11 | async-start | bytes 3276800 | tf_op jit(solution)/shard_map/all_to_all | solution.py:1587
  86.0 0.1 reshape.1272.asked
  86.0 38.6 %all-to-all-done.11.payload = bf16[32,200,128]{2,1,0:T(8,128)(2,1)S(1)} async-done(((bf16[32,200,128]{2,1,0:T(8,128)(2,1)}), bf16[32,200,128]{2,1,0:T(8,128)(2,1)S(1)}, u32[]{:S(2)}, u32[]{:S(2)}) %all-to-all-start.11) | async-done | bytes 1638432 | tf_op jit(solution)/shard_map/all_to_all | solution.py:1587
  124.6 3.9 %reduce.47 = (bf16[17,64,256]{2,1,0:T(8,128)(2,1)S(1)}, bf16[32,40,128]{2,1,0:T(8,128)(2,1)}) custom-call(s32[32,128]{1,0:T(8,128)S(1)} %get-tuple-element.316.tab, s32[2]{0:T(128)S(1)} %pad_add_fusion.me, f32[1,1]{1,0:T(1,128)} %get-tuple-element.328.loss, s32[1,1536]{1,0:T(1,128)S(1)} %reshape.1272.asked, bf16[32,200,128]{2,1,0:T(8,128)(2,1)S(1)} %all-to-all-done.11.payload), custom_call_target="tpu_custom_call" | custom-call | tf_op jit(solution)/shard_map/reduce/pallas_call | solution.py:1381
  128.6 3.9 %all-to-all-start.12 = ((bf16[32,40,128]{2,1,0:T(8,128)(2,1)}), bf16[32,40,128]{2,1,0:T(8,128)(2,1)S(1)}, u32[]{:S(2)}, u32[]{:S(2)}) async-start(bf16[32,40,128]{2,1,0:T(8,128)(2,1)} %get-tuple-element.330), calls=%async_computation.12 | async-start | bytes 655360 | tf_op jit(solution)/shard_map/all_to_all | solution.py:1587
  132.5 1.8 %collective-permute-start.10 = (bf16[17,64,256]{2,1,0:T(8,128)(2,1)S(1)}, bf16[17,64,256]{2,1,0:T(8,128)(2,1)S(1)}, u32[]{:S(2)}, u32[]{:S(2)}) collective-permute-start(bf16[17,64,256]{2,1,0:T(8,128)(2,1)S(1)} %get-tuple-element.331.own), channel_id=1, source_target_pairs={{0,1},{1,0},{2,3},{3,2},{4,5},{5,4},{6,7},{7,6},{8,9},{9,8},{10,11... | collective-permute-start | bytes 1671176 | tf_op jit(solution)/shard_map/ppermute | solution.py:1610
  134.4 0.8 slice_reduce_fusion
  135.9 8.4 %all-to-all-done.12.news = bf16[32,40,128]{2,1,0:T(8,128)(2,1)S(1)} async-done(((bf16[32,40,128]{2,1,0:T(8,128)(2,1)}), bf16[32,40,128]{2,1,0:T(8,128)(2,1)S(1)}, u32[]{:S(2)}, u32[]{:S(2)}) %all-to-all-start.12) | async-done | bytes 327712 | tf_op jit(solution)/shard_map/all_to_all | solution.py:1587
  144.3 5.7 %update.1 = (f32[17,128,256]{2,1,0:T(8,128)}, f32[17,128,256]{2,1,0:T(8,128)}, f32[17,128,256]{2,1,0:T(8,128)}, f32[16,256]{1,0:T(8,128)}, f32[16,256]{1,0:T(8,1...) custom-call(s32[32,128]{1,0:T(8,128)S(1)} %get-tuple-element.316.tab, ...), custom_call_target="tpu_custom_call" | custom-call | tf_op jit(solution)/shard_map/update/pallas_call | solution.py:1549
  150.0 0.9 collective-permute-done.10.other
  150.9 5.2 %finish.1 = (f32[17,128,256]{2,1,0:T(8,128)}, f32[17,128,256]{2,1,0:T(8,128)}, f32[17,128,256]{2,1,0:T(8,128)}) custom-call(s32[1]{0:T(128)} %bitcast.134.full, s32[32,128]{1,0:T(8,128)S(1)} %get-tuple-element.316.tab, s32[2]{0:T(128)S(1)} %pad_add_fusion.me, ...), custom_call_target="tpu_custom_call", output_to_operand_aliasing={{0}: (8, {}), {1}: (9, {}), {2}: (10, {})} | custom-call | tf_op jit(solution)/shard_map/finish/pallas_call | solution.py:1562
  (37 shorter events, 0.1 us)
Async XLA Ops:
  0.6 58.9 %copy-start.133 = (s32[1,2]{1,0:T(1,128)S(1)}, s32[1,2]{1,0:T(1,128)}, u32[]{:S(2)}) copy-start(s32[1,2]{1,0:T(1,128)} %query_lengths.3) | copy-start | bytes 28
  0.7 58.9 %copy-start.128 = (s32[1,2]{1,0:T(1,128)S(1)}, s32[1,2]{1,0:T(1,128)}, u32[]{:S(2)}) copy-start(s32[1,2]{1,0:T(1,128)} %passage_lengths.3) | copy-start | bytes 28
  0.7 58.9 %copy-start.130 = (s32[1,2]{1,0:T(1,128)S(1)}, s32[1,2]{1,0:T(1,128)}, u32[]{:S(2)}) copy-start(s32[1,2]{1,0:T(1,128)} %positive.3) | copy-start | bytes 28
  4.9 72.1 %copy-start.120 = (s32[6]{0:T(128)S(1)}, s32[6]{0:T(128)}, u32[]{:S(2)}) copy-start(s32[6]{0:T(128)} %prefix_lengths.1) | copy-start | bytes 76
  4.9 72.1 %copy-start.122 = (f32[6]{0:T(128)S(1)}, f32[6]{0:T(128)}, u32[]{:S(2)}) copy-start(f32[6]{0:T(128)} %prefix_weights.1) | copy-start | bytes 76
  24.6 9.1 %collective-permute-start = (bf16[15,16,128]{2,1,0:T(8,128)(2,1)S(1)}, bf16[15,16,128]{2,1,0:T(8,128)(2,1)S(1)}, u32[]{:S(2)}, u32[]{:S(2)}) collective-permute-start(bf16[15,16,128]{2,1,0:T(8,128)(2,1)S(1)} %collect.1), channel_id=1, source_target_pairs={{0,8},{2,10},{4,12},{6,14},{8,16},{10,18},{12,20},{14,22},{16,24},... | collective-permute-start | bytes 184328 | tf_op jit(solution)/shard_map/ppermute | solution.py:554
  24.8 8.9 %collective-permute-start.1 = (bf16[15,16,128]{2,1,0:T(8,128)(2,1)S(1)}, bf16[15,16,128]{2,1,0:T(8,128)(2,1)S(1)}, u32[]{:S(2)}, u32[]{:S(2)}) collective-permute-start(bf16[15,16,128]{2,1,0:T(8,128)(2,1)S(1)} %collect.1), channel_id=1, source_target_pairs={{0,16},{2,18},{4,20},{6,22},{8,24},{10,26},{12,28},{14,30},{16,0},... | collective-permute-start | bytes 184328 | tf_op jit(solution)/shard_map/ppermute | solution.py:554
  26.1 7.6 %collective-permute-start.2 = (bf16[15,16,128]{2,1,0:T(8,128)(2,1)S(1)}, bf16[15,16,128]{2,1,0:T(8,128)(2,1)S(1)}, u32[]{:S(2)}, u32[]{:S(2)}) collective-permute-start(bf16[15,16,128]{2,1,0:T(8,128)(2,1)S(1)} %collect.1), channel_id=1, source_target_pairs={{0,24},{2,26},{4,28},{6,30},{8,0},{10,2},{12,4},{14,6},{16,8},{18,... | collective-permute-start | bytes 184328 | tf_op jit(solution)/shard_map/ppermute | solution.py:554
  33.8 25.7 %copy-start.48 = (bf16[4,15,16,128]{3,2,1,0:T(8,128)(2,1)}, bf16[4,15,16,128]{3,2,1,0:T(8,128)(2,1)S(1)}, u32[]{:S(2)}) copy-start(bf16[4,15,16,128]{3,2,1,0:T(8,128)(2,1)S(1)} %pad_maximum_fusion.7.g0) | copy-start | bytes 737284
  33.8 25.7 %all-to-all-start.9 = ((bf16[16,80,256]{2,1,0:T(8,128)(2,1)}), bf16[16,80,256]{2,1,0:T(8,128)(2,1)S(1)}, u32[]{:S(2)}, u32[]{:S(2)}) async-start(bf16[16,80,256]{2,1,0:T(8,128)(2,1)} %bitcast.139), calls=%async_computation.9 | async-start | bytes 1310720 | tf_op jit(solution)/shard_map/all_to_all | solution.py:1587
  37.4 8.2 %collective-permute-start.3 = (bf16[4,15,16,128]{3,2,1,0:T(8,128)(2,1)S(1)}, bf16[4,15,16,128]{3,2,1,0:T(8,128)(2,1)S(1)}, u32[]{:S(2)}, u32[]{:S(2)}) collective-permute-start(bf16[4,15,16,128]{3,2,1,0:T(8,128)(2,1)S(1)} %pad_maximum_fusion.7.g0), channel_id=1, source_target_pairs={{0,1},{1,0},{2,3},{3,2},{4,5},{5,4},{6,7},{7,6},{8,9},{9,8},{10,11... | collective-permute-start | bytes 737288 | tf_op jit(solution)/shard_map/ppermute | solution.py:564
  38.3 13.1 %collective-permute-start.4 = (bf16[4,15,16,128]{3,2,1,0:T(8,128)(2,1)S(1)}, bf16[4,15,16,128]{3,2,1,0:T(8,128)(2,1)S(1)}, u32[]{:S(2)}, u32[]{:S(2)}) collective-permute-start(bf16[4,15,16,128]{3,2,1,0:T(8,128)(2,1)S(1)} %pad_maximum_fusion.7.g0), channel_id=1, source_target_pairs={{0,4},{2,6},{4,0},{6,2},{8,12},{10,14},{12,8},{14,10},{16,20},{18,... | collective-permute-start | bytes 737288 | tf_op jit(solution)/shard_map/ppermute | solution.py:554
  45.6 13.9 %copy-start.83 = (bf16[4,15,16,128]{3,2,1,0:T(8,128)(2,1)}, bf16[4,15,16,128]{3,2,1,0:T(8,128)(2,1)S(1)}, u32[]{:S(2)}) copy-start(bf16[4,15,16,128]{3,2,1,0:T(8,128)(2,1)S(1)} %collective-permute-done.3.g1) | copy-start | bytes 737284
  45.6 12.4 %collective-permute-start.5 = (bf16[4,15,16,128]{3,2,1,0:T(8,128)(2,1)S(1)}, bf16[4,15,16,128]{3,2,1,0:T(8,128)(2,1)S(1)}, u32[]{:S(2)}, u32[]{:S(2)}) collective-permute-start(bf16[4,15,16,128]{3,2,1,0:T(8,128)(2,1)S(1)} %collective-permute-done.3.g1), channel_id=1, source_target_pairs={{0,4},{2,6},{4,0},{6,2},{8,12},{10,14},{12,8},{14,10},{16,20},{18,... | collective-permute-start | bytes 737288 | tf_op jit(solution)/shard_map/ppermute | solution.py:554
  47.2 10.8 %collective-permute-start.6 = (bf16[4,15,16,128]{3,2,1,0:T(8,128)(2,1)S(1)}, bf16[4,15,16,128]{3,2,1,0:T(8,128)(2,1)S(1)}, u32[]{:S(2)}, u32[]{:S(2)}) collective-permute-start(bf16[4,15,16,128]{3,2,1,0:T(8,128)(2,1)S(1)} %pad_maximum_fusion.7.g0), channel_id=1, source_target_pairs={{0,2},{2,0},{4,6},{6,4},{8,10},{10,8},{12,14},{14,12},{16,18},{18,... | collective-permute-start | bytes 737288 | tf_op jit(solution)/shard_map/ppermute | solution.py:554
  47.2 10.8 %collective-permute-start.7 = (bf16[4,15,16,128]{3,2,1,0:T(8,128)(2,1)S(1)}, bf16[4,15,16,128]{3,2,1,0:T(8,128)(2,1)S(1)}, u32[]{:S(2)}, u32[]{:S(2)}) collective-permute-start(bf16[4,15,16,128]{3,2,1,0:T(8,128)(2,1)S(1)} %collective-permute-done.3.g1), channel_id=1, source_target_pairs={{0,2},{2,0},{4,6},{6,4},{8,10},{10,8},{12,14},{14,12},{16,18},{18,... | collective-permute-start | bytes 737288 | tf_op jit(solution)/shard_map/ppermute | solution.py:554
  51.5 8.0 %copy-start.84 = (bf16[4,15,16,128]{3,2,1,0:T(8,128)(2,1)}, bf16[4,15,16,128]{3,2,1,0:T(8,128)(2,1)S(1)}, u32[]{:S(2)}) copy-start(bf16[4,15,16,128]{3,2,1,0:T(8,128)(2,1)S(1)} %collective-permute-done.4.g2) | copy-start | bytes 737284
  51.5 6.5 %collective-permute-start.8 = (bf16[4,15,16,128]{3,2,1,0:T(8,128)(2,1)S(1)}, bf16[4,15,16,128]{3,2,1,0:T(8,128)(2,1)S(1)}, u32[]{:S(2)}, u32[]{:S(2)}) collective-permute-start(bf16[4,15,16,128]{3,2,1,0:T(8,128)(2,1)S(1)} %collective-permute-done.4.g2), channel_id=1, source_target_pairs={{0,2},{2,0},{4,6},{6,4},{8,10},{10,8},{12,14},{14,12},{16,18},{18,... | collective-permute-start | bytes 737288 | tf_op jit(solution)/shard_map/ppermute | solution.py:554
  58.0 1.5 copy-start.85
  58.0 1.5 collective-permute-start.9
  76.9 67.3 %copy-start.65 = (f32[16,256]{1,0:T(8,128)S(1)}, f32[16,256]{1,0:T(8,128)}, u32[]{:S(2)}) copy-start(f32[16,256]{1,0:T(8,128)} %vector_first.1) | copy-start | bytes 49156
  77.0 67.3 %copy-start.67 = (f32[16,256]{1,0:T(8,128)S(1)}, f32[16,256]{1,0:T(8,128)}, u32[]{:S(2)}) copy-start(f32[16,256]{1,0:T(8,128)} %vector_second.1) | copy-start | bytes 49156
  83.1 41.6 %all-to-all-start.11 = ((bf16[32,200,128]{2,1,0:T(8,128)(2,1)}), bf16[32,200,128]{2,1,0:T(8,128)(2,1)S(1)}, u32[]{:S(2)}, u32[]{:S(2)}) async-start(bf16[32,200,128]{2,1,0:T(8,128)(2,1)} %get-tuple-element.329), calls=%async_computation.11 | async-start | bytes 3276800 | tf_op jit(solution)/shard_map/all_to_all | solution.py:1587
  128.6 22.3 %copy-start.63 = (s32[269]{0:T(512)S(1)}, s32[269]{0:T(512)}, u32[]{:S(2)}) copy-start(s32[269]{0:T(512)} %owner_line.1) | copy-start | bytes 3232
  128.6 22.3 %copy-start.124 = (s32[1,2,128]{2,1,0:T(2,128)S(1)}, s32[1,2,128]{2,1,0:T(2,128)}, u32[]{:S(2)}) copy-start(s32[1,2,128]{2,1,0:T(2,128)} %param.34) | copy-start | bytes 3076
  128.6 15.7 %all-to-all-start.12 = ((bf16[32,40,128]{2,1,0:T(8,128)(2,1)}), bf16[32,40,128]{2,1,0:T(8,128)(2,1)S(1)}, u32[]{:S(2)}, u32[]{:S(2)}) async-start(bf16[32,40,128]{2,1,0:T(8,128)(2,1)} %get-tuple-element.330), calls=%async_computation.12 | async-start | bytes 655360 | tf_op jit(solution)/shard_map/all_to_all | solution.py:1587
  132.5 18.3 %collective-permute-start.10 = (bf16[17,64,256]{2,1,0:T(8,128)(2,1)S(1)}, bf16[17,64,256]{2,1,0:T(8,128)(2,1)S(1)}, u32[]{:S(2)}, u32[]{:S(2)}) collective-permute-start(bf16[17,64,256]{2,1,0:T(8,128)(2,1)S(1)} %get-tuple-element.331.own), channel_id=1, source_target_pairs={{0,1},{1,0},{2,3},{3,2},{4,5},{5,4},{6,7},{7,6},{8,9},{9,8},{10,11... | collective-permute-start | bytes 1671176 | tf_op jit(solution)/shard_map/ppermute | solution.py:1610

commit v6 on v5

--- a/solution.py
+++ b/solution.py
@@ -1398,16 +1398,15 @@
 
 
 def update_slots(
-    tab, half, rest, grads, places, scale, arrays, outs, held, in_sems, out_sems, wanted=None
+    tab, half, rest, grads, places, scale, arrays, outs, held, in_sems, out_sems, ready=None
 ):
+    old = held if ready is None else ready
     first_scale = -RATE / (1.0 - BETA_ONE**STEP)
     second_scale = 1.0 / (1.0 - BETA_TWO**STEP)
     rows = (pl.ds(pl.multiple_of(half * HALF, HALF), HALF), slice(None))
     columns = (slice(None), pl.ds(pl.multiple_of(half * 128, 128), 128))
     whole = (slice(None), slice(None))
     ends = [tab[k, TAB_ENDS] for k in range(4)]
-    if wanted is not None:
-        ends = [jnp.where(wanted, end, 0) for end in ends]
     spans = [(KIND_TABLE, 0, ends[0], rows), (KIND_DENSE, ends[0], ends[1], columns)]
     if rest:
         spans += [(KIND_PLACE, ends[1], ends[2], whole), (0, ends[2], ends[3], whole)]
@@ -1439,18 +1438,19 @@
 
     def step(i, region, g):
         g = g * scale[: g.shape[0], : g.shape[1]]
-        m1 = BETA_ONE * held[(1, i) + region] + (1.0 - BETA_ONE) * g
-        m2 = BETA_TWO * held[(2, i) + region] + (1.0 - BETA_TWO) * (g * g)
+        m1 = BETA_ONE * old[(1, i) + region] + (1.0 - BETA_ONE) * g
+        m2 = BETA_TWO * old[(2, i) + region] + (1.0 - BETA_TWO) * (g * g)
         root = jnp.sqrt(m2 * second_scale) + EPSILON
         held[(0, i) + region] = (
-            held[(0, i) + region] * (1.0 - RATE * DECAY) + (m1 * first_scale) / root
+            old[(0, i) + region] * (1.0 - RATE * DECAY) + (m1 * first_scale) / root
         )
         held[(1, i) + region] = m1
         held[(2, i) + region] = m2
 
     def act(i, case, region):
-        for copy in in_copies(i, region):
-            copy.wait()
+        if ready is None:
+            for copy in in_copies(i, region):
+                copy.wait()
         if case == KIND_TABLE:
             step(i, region, grads[i].astype(F32))
         elif case == KIND_DENSE:
@@ -1467,17 +1467,36 @@
         for copy in out_copies(i, region):
             copy.wait()
 
-    loop(start)
+    if ready is None:
+        loop(start)
     yield
     loop(act)
     loop(finish)
     yield
 
 
+def ahead_copies(tab, half, arrays, ready, sems, wait):
+    rows = (pl.ds(pl.multiple_of(half * HALF, HALF), HALF), slice(None))
+    columns = (slice(None), pl.ds(pl.multiple_of(half * 128, 128), 128))
+    ends = [tab[k, TAB_ENDS] for k in range(2)]
+    for start, stop, region in ((0, ends[0], rows), (ends[0], ends[1], columns)):
+
+        def body(j, c):
+            i = tab[j, TAB_SORTED]
+            for k, a in enumerate(arrays):
+                copy = pltpu.make_async_copy(
+                    a.at[(i,) + region], ready.at[(k, i) + region], sems.at[k, i]
+                )
+                copy.wait() if wait else copy.start()
+            return c
+
+        lax.fori_loop(start, stop, body, 0)
+
+
 def update_kernel(
     tab, me, news, own, weight, first, second, vectors, vector_first, vector_second,
     weight_out, first_out, second_out, vectors_out, vector_first_out, vector_second_out, loss_out,
-    norm_out, factor_out, places, held, in_sems, out_sems,
+    norm_out, factor_out, ready, places, held, in_sems, out_sems, ready_sems,
 ):
     n_dest = news.shape[0]
     pr = place_rows(n_dest)
@@ -1488,6 +1507,7 @@
         (weight_out, first_out, second_out), held, in_sems, out_sems,
     )
     next(steps)
+    ahead_copies(tab, 1 - me[1], (weight, first, second), ready, ready_sems, False)
     extras = []
     for d in range(n_dest):
         part = news[d].astype(F32)
@@ -1519,15 +1539,16 @@
     vector_second_out[...] = m2
     factor_out[...] = jnp.broadcast_to(jnp.concatenate([factor, factor], 1), (UNIT, D))
     next(steps)
+    ahead_copies(tab, 1 - me[1], (weight, first, second), ready, ready_sems, True)
 
 
 def finish_kernel(
-    full, tab, me, factor, other, weight, first, second, weight_in, first_in, second_in, weight_out,
+    tab, me, factor, other, ready, weight_in, first_in, second_in, weight_out,
     first_out, second_out, held, in_sems, out_sems,
 ):
     steps = update_slots(
-        tab, 1 - me[1], False, other, None, factor, (weight, first, second),
-        (weight_out, first_out, second_out), held, in_sems, out_sems, full[0] == 0,
+        tab, 1 - me[1], False, other, None, factor, (),
+        (weight_out, first_out, second_out), held, in_sems, out_sems, ready=ready,
     )
     next(steps)
     next(steps)
@@ -1548,27 +1569,35 @@
     one = jax.ShapeDtypeStruct((1, 1), F32)
     return pl.pallas_call(
         update_kernel,
-        out_shape=(big, big, big, small, small, small, one, one, jax.ShapeDtypeStruct((UNIT, D), F32)),
+        out_shape=(big, big, big, small, small, small, one, one, jax.ShapeDtypeStruct((UNIT, D), F32),
+            pltpu.VMEM((3,) + weights.shape, F32),
+        ),
         in_specs=[smem, smem] + [vmem] * 2 + [in_hbm] * 3 + [vmem] * 3,
-        out_specs=(in_hbm, in_hbm, in_hbm, vmem, vmem, vmem, smem, smem, vmem),
-        scratch_shapes=[pltpu.VMEM((PLEN, D), F32)] + update_scratch(weights.shape),
+        out_specs=(in_hbm, in_hbm, in_hbm, vmem, vmem, vmem, smem, smem, vmem, vmem),
+        scratch_shapes=[pltpu.VMEM((PLEN, D), F32)]
+        + update_scratch(weights.shape)
+        + [pltpu.SemaphoreType.DMA((3, weights.shape[0]))],
         compiler_params=params(n_dest // 2, 14),
         name="update",
     )(tab, me, news, own, *stay(weights, first, second), vectors, vector_first, vector_second)
 
 
-def finish(full, tab, me, factor, other, weights, first, second, started, n_blk):
-    big = pltpu.HBM(weights.shape, F32)
+def finish(tab, me, factor, other, ready, started, n_blk):
+    shape = started[0].shape
+    big = pltpu.HBM(shape, F32)
     return pl.pallas_call(
         finish_kernel,
         out_shape=(big, big, big),
-        in_specs=[smem, smem, smem, vmem, vmem] + [in_hbm] * 6,
+        in_specs=[smem, smem, vmem, vmem, vmem] + [in_hbm] * 3,
         out_specs=(in_hbm, in_hbm, in_hbm),
-        scratch_shapes=update_scratch(weights.shape),
-        input_output_aliases={8: 0, 9: 1, 10: 2},
+        scratch_shapes=update_scratch(shape),
+        input_output_aliases={5: 0, 6: 1, 7: 2},
         compiler_params=params(n_blk, 14),
         name="finish",
-    )(full, tab, me, factor, other, *stay(weights, first, second, *started))
+    )(
+        tab, me, factor, other, pltpu.with_memory_space_constraint(ready, pltpu.VMEM),
+        *stay(*started),
+    )
 
 
 def quick(
@@ -1609,7 +1638,7 @@
     own, news = reduce(tab, me, loss, asked, payload, slots, cap)
     other = lax.ppermute(own, "rep", [(0, 1), (1, 0)])
     news = exchange(news, everyone)
-    *outs, loss_sum, norm, factor = update(
+    *outs, loss_sum, norm, factor, ready = update(
         tab, me, news, own, weights, first_moments, second_moments, vectors, vector_first,
         vector_second,
     )
@@ -1623,12 +1652,8 @@
         )
 
     full = jnp.max(message[:, 126])
-    outs = lax.while_loop(lambda c: c[0] > 0, general, (full, outs))[1]
-    finished = finish(
-        full.reshape(1), tab, me, factor, other, weights, first_moments, second_moments, outs[:3],
-        n_blk,
-    )
-    return (*finished, *outs[3:])
+    outs = (*finish(tab, me, factor, other, ready, outs[:3], n_blk), *outs[3:])
+    return lax.while_loop(lambda c: c[0] > 0, general, (full, outs))[1]
 
 
 def solution(mesh):

time: 157 us -> 156 us (level)
    pallas_call x1, Pallas kernels: 5.18 us -> 3.55 us  [finish(): pl.pallas_call(finish_kernel, out_shape=(big, big, big), in_specs=[smem,...]
  transfers between devices with their start and end apart: 14 -> 14, of which waited for: 7 -> 6; matrix products, arithmetic and copies ran while one was open for 1% -> 1% of each run, Pallas kernels for 7% -> 8%
where the time goes in v6:
time: 156 us
  waiting for transfers between devices  64.8 us (42%)
  Pallas kernels  35.8 us (23%)
  blocking collectives  30.8 us (20%)
  starting transfers between devices  21.4 us (14%)
    all_to_all x3, waiting for transfers between devices, exchange(): return lax.all_to_all(a, axes, 0, 0, tiled=True)  47.7 us
    all_to_all x2, blocking collectives, exchange(): return lax.all_to_all(a, axes, 0, 0, tiled=True)  30.8 us
    ppermute x9, waiting for transfers between devices, across(): return lax.ppermute(values, 'blk', pairs)  11.7 us
    all_to_all x3, starting transfers between devices, exchange(): return lax.all_to_all(a, axes, 0, 0, tiled=True)  10.3 us
    ppermute x9, starting transfers between devices, across(): return lax.ppermute(values, 'blk', pairs)  8.34 us
    pallas_call x1, Pallas kernels, update(): pl.pallas_call(update_kernel, out_shape=(big, big, big, small, small, sma...  6.99 us
    pallas_call x1, Pallas kernels, backward(): pl.pallas_call(partial(backward_kernel, cap), out_shape=(jax.ShapeDtypeSt...  6 us
    pallas_call x1, Pallas kernels, forward(): pl.pallas_call(forward_kernel, out_shape=(jax.ShapeDtypeStruct((n_blk * 8...  5.42 us
  transfers between devices with their start and end apart: 14, of which 6 were waited for; matrix products, arithmetic and copies ran while one was open for 1% of the time, Pallas kernels for 8%

profile of v6, /device:TPU:0, one launch (start us, length us, event | category | flops | bytes accessed | tf_op | source)
XLA Modules:
  0.0 155.8 jit_solution(17193308181408435080)
XLA Ops:
  0.6 0.0 copy-start.153
  0.7 0.1 pad_add_fusion.me
  0.8 4.1 %request.1 = (bf16[32,40,128]{2,1,0:T(8,128)(2,1)S(1)}, s32[2,1280]{1,0:T(2,128)S(1)}, s32[32,128]{1,0:T(8,128)S(1)}) custom-call(s32[269]{0:T(512)} %owner_line.1, s32[2]{0:T(128)S(1)} %pad_add_fusion.me, s32[1,2]{1,0:T(1,128)} %positive.3, s32[1,2]{1,0:T(1,128)} %query_lengths.3, s32[1,2]{1,0:T(1,128)} %passage_lengths.3, s32[269]{0:T(512)} %owner_line.1, ...), custom_call_target="tpu_custom_call" | custom-call | tf_op jit(solution)/shard_map/request/pallas_call | solution.py:818
  4.9 18.8 %all_to_all.74.message = bf16[32,40,128]{2,1,0:T(8,128)(2,1)S(1)} all-to-all(bf16[32,40,128]{2,1,0:T(8,128)(2,1)S(1)} %get-tuple-element.315), channel_id=1, replica_groups=mesh['blk'=16,'rep'=2] {'blk','rep'}, dimensions={0} | all-to-all | bytes 655360 | tf_op jit(solution)/shard_map/all_to_all | solution.py:1616
  23.7 0.9 collect.1
  24.7 0.1 collective-permute-start
  24.8 1.3 collective-permute-start.1
  26.1 2.8 %collective-permute-start.2 = (bf16[15,16,128]{2,1,0:T(8,128)(2,1)S(1)}, bf16[15,16,128]{2,1,0:T(8,128)(2,1)S(1)}, u32[]{:S(2)}, u32[]{:S(2)}) collective-permute-start(bf16[15,16,128]{2,1,0:T(8,128)(2,1)S(1)} %collect.1), channel_id=1, source_target_pairs={{0,24},{2,26},{4,28},{6,30},{8,0},{10,2},{12,4},{14,6},{16,8},{18,... | collective-permute-start | bytes 184328 | tf_op jit(solution)/shard_map/ppermute | solution.py:554
  28.9 4.8 %fetch.1 = (bf16[1280,256]{1,0:T(8,128)(2,1)}, s32[32,128]{1,0:T(8,128)S(1)}) custom-call(s32[2]{0:T(128)S(1)} %pad_add_fusion.me, bf16[32,40,128]{2,1,0:T(8,128)(2,1)S(1)} %all_to_all.74.message, f32[17,128,256]{2,1,0:T(8,128)} %weight.1), custom_call_target="tpu_custom_call" | custom-call | tf_op jit(solution)/shard_map/fetch/pallas_call | solution.py:895
  33.8 3.6 %all-to-all-start.9 = ((bf16[16,80,256]{2,1,0:T(8,128)(2,1)}), bf16[16,80,256]{2,1,0:T(8,128)(2,1)S(1)}, u32[]{:S(2)}, u32[]{:S(2)}) async-start(bf16[16,80,256]{2,1,0:T(8,128)(2,1)} %bitcast.138), calls=%async_computation.9 | async-start | bytes 1310720 | tf_op jit(solution)/shard_map/all_to_all | solution.py:1616
  37.4 0.9 collective-permute-start.3
  38.3 1.9 %collective-permute-start.4 = (bf16[4,15,16,128]{3,2,1,0:T(8,128)(2,1)S(1)}, bf16[4,15,16,128]{3,2,1,0:T(8,128)(2,1)S(1)}, u32[]{:S(2)}, u32[]{:S(2)}) collective-permute-start(bf16[4,15,16,128]{3,2,1,0:T(8,128)(2,1)S(1)} %pad_maximum_fusion.7.g0), channel_id=1, source_target_pairs={{0,4},{2,6},{4,0},{6,2},{8,12},{10,14},{12,8},{14,10},{16,20},{18,... | collective-permute-start | bytes 737288 | tf_op jit(solution)/shard_map/ppermute | solution.py:554
  40.2 5.4 %collective-permute-done.3.g1 = bf16[4,15,16,128]{3,2,1,0:T(8,128)(2,1)S(1)} collective-permute-done((bf16[4,15,16,128]{3,2,1,0:T(8,128)(2,1)S(1)}, bf16[4,15,16,128]{3,2,1,0:T(8,128)(2,1)S(1)}, u32[]{:S(2)}, u32[]{:S(2)}) %collective-permute-start.3) | collective-permute-done | bytes 245792 | tf_op jit(solution)/shard_map/ppermute | solution.py:564
  45.6 1.7 %collective-permute-start.5 = (bf16[4,15,16,128]{3,2,1,0:T(8,128)(2,1)S(1)}, bf16[4,15,16,128]{3,2,1,0:T(8,128)(2,1)S(1)}, u32[]{:S(2)}, u32[]{:S(2)}) collective-permute-start(bf16[4,15,16,128]{3,2,1,0:T(8,128)(2,1)S(1)} %collective-permute-done.3.g1), channel_id=1, source_target_pairs={{0,4},{2,6},{4,0},{6,2},{8,12},{10,14},{12,8},{14,10},{16,20},{18,... | collective-permute-start | bytes 737288 | tf_op jit(solution)/shard_map/ppermute | solution.py:554
  47.3 0.5 collective-permute-start.7
  47.8 3.7 %collective-permute-done.4.g2 = bf16[4,15,16,128]{3,2,1,0:T(8,128)(2,1)S(1)} collective-permute-done((bf16[4,15,16,128]{3,2,1,0:T(8,128)(2,1)S(1)}, bf16[4,15,16,128]{3,2,1,0:T(8,128)(2,1)S(1)}, u32[]{:S(2)}, u32[]{:S(2)}) %collective-permute-start.4) | collective-permute-done | bytes 245792 | tf_op jit(solution)/shard_map/ppermute | solution.py:554
  51.5 6.5 %collective-permute-done.5.g3 = bf16[4,15,16,128]{3,2,1,0:T(8,128)(2,1)S(1)} collective-permute-done((bf16[4,15,16,128]{3,2,1,0:T(8,128)(2,1)S(1)}, bf16[4,15,16,128]{3,2,1,0:T(8,128)(2,1)S(1)}, u32[]{:S(2)}, u32[]{:S(2)}) %collective-permute-start.5) | collective-permute-done | bytes 245792 | tf_op jit(solution)/shard_map/ppermute | solution.py:554
  58.0 1.5 collective-permute-done.9.g7
  59.6 5.4 %forward.1 = (bf16[128,384]{1,0:T(8,128)(2,1)S(1)}, bf16[1280,256]{1,0:T(8,128)(2,1)S(1)}, f32[1280,256]{1,0:T(8,128)S(1)}, f32[1280,128]{1,0:T(8,128)S(1)}, f32...) custom-call(s32[32,128]{1,0:T(8,128)S(1)} %get-tuple-element.317.tab, ...), custom_call_target="tpu_custom_call" | custom-call | tf_op jit(solution)/shard_map/forward/pallas_call | solution.py:1017
  65.0 11.9 %all_to_all.75 = bf16[16,8,384]{2,1,0:T(8,128)(2,1)S(1)} all-to-all(bf16[16,8,384]{2,1,0:T(8,128)(2,1)S(1)} %bitcast.453), channel_id=1, replica_groups=mesh['blk'=16,'rep'=2] {'blk'}, dimensions={0} | all-to-all | bytes 196608 | tf_op jit(solution)/shard_map/all_to_all | solution.py:1616
  77.0 6.0 %backward.1 = (bf16[32,200,128]{2,1,0:T(8,128)(2,1)}, f32[1,1]{1,0:T(1,128)}, f32[1,1]{1,0:T(1,128)}) custom-call(s32[32,128]{1,0:T(8,128)S(1)} %get-tuple-element.317.tab, s32[2]{0:T(128)S(1)} %pad_add_fusion.me, s32[6]{0:T(128)S(1)} %copy-done.141, f32[6]{0:T(128)S(1)} %copy-done.143, bf16[128,384]{1,0:T(8,128)(2,1)S(1)} %bitcast.450, ...), custom_call_target="tpu_custom_call" | custom-call | tf_op jit(solution)/shard_map/backward/pallas_call | solution.py:1279
  83.0 2.9 %all-to-all-start.11 = ((bf16[32,200,128]{2,1,0:T(8,128)(2,1)}), bf16[32,200,128]{2,1,0:T(8,128)(2,1)S(1)}, u32[]{:S(2)}, u32[]{:S(2)}) async-start(bf16[32,200,128]{2,1,0:T(8,128)(2,1)} %get-tuple-element.330), calls=%async_computation.11 | async-start | bytes 3276800 | tf_op jit(solution)/shard_map/all_to_all | solution.py:1616
  85.9 0.1 reshape.1268.asked
  86.0 38.6 %all-to-all-done.11.payload = bf16[32,200,128]{2,1,0:T(8,128)(2,1)S(1)} async-done(((bf16[32,200,128]{2,1,0:T(8,128)(2,1)}), bf16[32,200,128]{2,1,0:T(8,128)(2,1)S(1)}, u32[]{:S(2)}, u32[]{:S(2)}) %all-to-all-start.11) | async-done | bytes 1638432 | tf_op jit(solution)/shard_map/all_to_all | solution.py:1616
  124.5 4.1 %reduce.47 = (bf16[17,64,256]{2,1,0:T(8,128)(2,1)S(1)}, bf16[32,40,128]{2,1,0:T(8,128)(2,1)}) custom-call(s32[32,128]{1,0:T(8,128)S(1)} %get-tuple-element.317.tab, s32[2]{0:T(128)S(1)} %pad_add_fusion.me, f32[1,1]{1,0:T(1,128)} %get-tuple-element.329.loss, s32[1,1536]{1,0:T(1,128)S(1)} %reshape.1268.asked, bf16[32,200,128]{2,1,0:T(8,128)(2,1)S(1)} %all-to-all-done.11.payload), custom_call_target="tpu_custom_call" | custom-call | tf_op jit(solution)/shard_map/reduce/pallas_call | solution.py:1381
  128.6 3.8 %all-to-all-start.12 = ((bf16[32,40,128]{2,1,0:T(8,128)(2,1)}), bf16[32,40,128]{2,1,0:T(8,128)(2,1)S(1)}, u32[]{:S(2)}, u32[]{:S(2)}) async-start(bf16[32,40,128]{2,1,0:T(8,128)(2,1)} %get-tuple-element.331), calls=%async_computation.12 | async-start | bytes 655360 | tf_op jit(solution)/shard_map/all_to_all | solution.py:1616
  132.4 1.8 %collective-permute-start.10 = (bf16[17,64,256]{2,1,0:T(8,128)(2,1)S(1)}, bf16[17,64,256]{2,1,0:T(8,128)(2,1)S(1)}, u32[]{:S(2)}, u32[]{:S(2)}) collective-permute-start(bf16[17,64,256]{2,1,0:T(8,128)(2,1)S(1)} %get-tuple-element.332.own), channel_id=1, source_target_pairs={{0,1},{1,0},{2,3},{3,2},{4,5},{5,4},{6,7},{7,6},{8,9},{9,8},{10,11... | collective-permute-start | bytes 1671176 | tf_op jit(solution)/shard_map/ppermute | solution.py:1639
  134.2 0.8 slice_reduce_fusion
  135.0 9.1 %all-to-all-done.12.news = bf16[32,40,128]{2,1,0:T(8,128)(2,1)S(1)} async-done(((bf16[32,40,128]{2,1,0:T(8,128)(2,1)}), bf16[32,40,128]{2,1,0:T(8,128)(2,1)S(1)}, u32[]{:S(2)}, u32[]{:S(2)}) %all-to-all-start.12) | async-done | bytes 327712 | tf_op jit(solution)/shard_map/all_to_all | solution.py:1616
  144.2 7.0 %update.1 = (f32[17,128,256]{2,1,0:T(8,128)}, f32[17,128,256]{2,1,0:T(8,128)}, f32[17,128,256]{2,1,0:T(8,128)}, f32[16,256]{1,0:T(8,128)}, f32[16,256]{1,0:T(8,1...) custom-call(s32[32,128]{1,0:T(8,128)S(1)} %get-tuple-element.317.tab, ...), custom_call_target="tpu_custom_call" | custom-call | tf_op jit(solution)/shard_map/update/pallas_call | solution.py:1570
  151.2 3.5 %finish.1 = (f32[17,128,256]{2,1,0:T(8,128)}, f32[17,128,256]{2,1,0:T(8,128)}, f32[17,128,256]{2,1,0:T(8,128)}) custom-call(s32[32,128]{1,0:T(8,128)S(1)} %get-tuple-element.317.tab, s32[2]{0:T(128)S(1)} %pad_add_fusion.me, f32[128,256]{1,0:T(8,128)S(1)} %get-tuple-element.333.factor, ...), custom_call_target="tpu_custom_call", output_to_operand_aliasing={{0}: (5, {}), {1}: (6, {}), {2}: (7, {})} | custom-call | tf_op jit(solution)/shard_map/finish/pallas_call | solution.py:1588
  154.7 0.9 while.66
  (35 shorter events, 0.1 us)
Async XLA Ops:
  0.6 58.9 %copy-start.153 = (s32[1,2]{1,0:T(1,128)S(1)}, s32[1,2]{1,0:T(1,128)}, u32[]{:S(2)}) copy-start(s32[1,2]{1,0:T(1,128)} %query_lengths.3) | copy-start | bytes 28
  0.7 58.9 %copy-start.148 = (s32[1,2]{1,0:T(1,128)S(1)}, s32[1,2]{1,0:T(1,128)}, u32[]{:S(2)}) copy-start(s32[1,2]{1,0:T(1,128)} %passage_lengths.3) | copy-start | bytes 28
  0.7 58.9 %copy-start.150 = (s32[1,2]{1,0:T(1,128)S(1)}, s32[1,2]{1,0:T(1,128)}, u32[]{:S(2)}) copy-start(s32[1,2]{1,0:T(1,128)} %positive.3) | copy-start | bytes 28
  0.7 58.9 %copy-start.49 = (f32[16,256]{1,0:T(8,128)S(1)}, f32[16,256]{1,0:T(8,128)}, u32[]{:S(2)}) copy-start(f32[16,256]{1,0:T(8,128)} %vectors.5) | copy-start | bytes 49156
  4.9 72.1 %copy-start.141 = (s32[6]{0:T(128)S(1)}, s32[6]{0:T(128)}, u32[]{:S(2)}) copy-start(s32[6]{0:T(128)} %prefix_lengths.1) | copy-start | bytes 76
  4.9 72.1 %copy-start.143 = (f32[6]{0:T(128)S(1)}, f32[6]{0:T(128)}, u32[]{:S(2)}) copy-start(f32[6]{0:T(128)} %prefix_weights.1) | copy-start | bytes 76
  24.7 9.1 %collective-permute-start = (bf16[15,16,128]{2,1,0:T(8,128)(2,1)S(1)}, bf16[15,16,128]{2,1,0:T(8,128)(2,1)S(1)}, u32[]{:S(2)}, u32[]{:S(2)}) collective-permute-start(bf16[15,16,128]{2,1,0:T(8,128)(2,1)S(1)} %collect.1), channel_id=1, source_target_pairs={{0,8},{2,10},{4,12},{6,14},{8,16},{10,18},{12,20},{14,22},{16,24},... | collective-permute-start | bytes 184328 | tf_op jit(solution)/shard_map/ppermute | solution.py:554
  24.8 8.9 %collective-permute-start.1 = (bf16[15,16,128]{2,1,0:T(8,128)(2,1)S(1)}, bf16[15,16,128]{2,1,0:T(8,128)(2,1)S(1)}, u32[]{:S(2)}, u32[]{:S(2)}) collective-permute-start(bf16[15,16,128]{2,1,0:T(8,128)(2,1)S(1)} %collect.1), channel_id=1, source_target_pairs={{0,16},{2,18},{4,20},{6,22},{8,24},{10,26},{12,28},{14,30},{16,0},... | collective-permute-start | bytes 184328 | tf_op jit(solution)/shard_map/ppermute | solution.py:554
  26.1 7.6 %collective-permute-start.2 = (bf16[15,16,128]{2,1,0:T(8,128)(2,1)S(1)}, bf16[15,16,128]{2,1,0:T(8,128)(2,1)S(1)}, u32[]{:S(2)}, u32[]{:S(2)}) collective-permute-start(bf16[15,16,128]{2,1,0:T(8,128)(2,1)S(1)} %collect.1), channel_id=1, source_target_pairs={{0,24},{2,26},{4,28},{6,30},{8,0},{10,2},{12,4},{14,6},{16,8},{18,... | collective-permute-start | bytes 184328 | tf_op jit(solution)/shard_map/ppermute | solution.py:554
  33.8 25.7 %copy-start.62 = (bf16[4,15,16,128]{3,2,1,0:T(8,128)(2,1)}, bf16[4,15,16,128]{3,2,1,0:T(8,128)(2,1)S(1)}, u32[]{:S(2)}) copy-start(bf16[4,15,16,128]{3,2,1,0:T(8,128)(2,1)S(1)} %pad_maximum_fusion.7.g0) | copy-start | bytes 737284
  33.8 25.7 %all-to-all-start.9 = ((bf16[16,80,256]{2,1,0:T(8,128)(2,1)}), bf16[16,80,256]{2,1,0:T(8,128)(2,1)S(1)}, u32[]{:S(2)}, u32[]{:S(2)}) async-start(bf16[16,80,256]{2,1,0:T(8,128)(2,1)} %bitcast.138), calls=%async_computation.9 | async-start | bytes 1310720 | tf_op jit(solution)/shard_map/all_to_all | solution.py:1616
  37.4 8.2 %collective-permute-start.3 = (bf16[4,15,16,128]{3,2,1,0:T(8,128)(2,1)S(1)}, bf16[4,15,16,128]{3,2,1,0:T(8,128)(2,1)S(1)}, u32[]{:S(2)}, u32[]{:S(2)}) collective-permute-start(bf16[4,15,16,128]{3,2,1,0:T(8,128)(2,1)S(1)} %pad_maximum_fusion.7.g0), channel_id=1, source_target_pairs={{0,1},{1,0},{2,3},{3,2},{4,5},{5,4},{6,7},{7,6},{8,9},{9,8},{10,11... | collective-permute-start | bytes 737288 | tf_op jit(solution)/shard_map/ppermute | solution.py:564
  38.3 13.1 %collective-permute-start.4 = (bf16[4,15,16,128]{3,2,1,0:T(8,128)(2,1)S(1)}, bf16[4,15,16,128]{3,2,1,0:T(8,128)(2,1)S(1)}, u32[]{:S(2)}, u32[]{:S(2)}) collective-permute-start(bf16[4,15,16,128]{3,2,1,0:T(8,128)(2,1)S(1)} %pad_maximum_fusion.7.g0), channel_id=1, source_target_pairs={{0,4},{2,6},{4,0},{6,2},{8,12},{10,14},{12,8},{14,10},{16,20},{18,... | collective-permute-start | bytes 737288 | tf_op jit(solution)/shard_map/ppermute | solution.py:554
  45.6 13.9 %copy-start.100 = (bf16[4,15,16,128]{3,2,1,0:T(8,128)(2,1)}, bf16[4,15,16,128]{3,2,1,0:T(8,128)(2,1)S(1)}, u32[]{:S(2)}) copy-start(bf16[4,15,16,128]{3,2,1,0:T(8,128)(2,1)S(1)} %collective-permute-done.3.g1) | copy-start | bytes 737284
  45.6 12.4 %collective-permute-start.5 = (bf16[4,15,16,128]{3,2,1,0:T(8,128)(2,1)S(1)}, bf16[4,15,16,128]{3,2,1,0:T(8,128)(2,1)S(1)}, u32[]{:S(2)}, u32[]{:S(2)}) collective-permute-start(bf16[4,15,16,128]{3,2,1,0:T(8,128)(2,1)S(1)} %collective-permute-done.3.g1), channel_id=1, source_target_pairs={{0,4},{2,6},{4,0},{6,2},{8,12},{10,14},{12,8},{14,10},{16,20},{18,... | collective-permute-start | bytes 737288 | tf_op jit(solution)/shard_map/ppermute | solution.py:554
  47.3 10.8 %collective-permute-start.6 = (bf16[4,15,16,128]{3,2,1,0:T(8,128)(2,1)S(1)}, bf16[4,15,16,128]{3,2,1,0:T(8,128)(2,1)S(1)}, u32[]{:S(2)}, u32[]{:S(2)}) collective-permute-start(bf16[4,15,16,128]{3,2,1,0:T(8,128)(2,1)S(1)} %pad_maximum_fusion.7.g0), channel_id=1, source_target_pairs={{0,2},{2,0},{4,6},{6,4},{8,10},{10,8},{12,14},{14,12},{16,18},{18,... | collective-permute-start | bytes 737288 | tf_op jit(solution)/shard_map/ppermute | solution.py:554
  47.3 10.8 %collective-permute-start.7 = (bf16[4,15,16,128]{3,2,1,0:T(8,128)(2,1)S(1)}, bf16[4,15,16,128]{3,2,1,0:T(8,128)(2,1)S(1)}, u32[]{:S(2)}, u32[]{:S(2)}) collective-permute-start(bf16[4,15,16,128]{3,2,1,0:T(8,128)(2,1)S(1)} %collective-permute-done.3.g1), channel_id=1, source_target_pairs={{0,2},{2,0},{4,6},{6,4},{8,10},{10,8},{12,14},{14,12},{16,18},{18,... | collective-permute-start | bytes 737288 | tf_op jit(solution)/shard_map/ppermute | solution.py:554
  51.5 8.0 %copy-start.101 = (bf16[4,15,16,128]{3,2,1,0:T(8,128)(2,1)}, bf16[4,15,16,128]{3,2,1,0:T(8,128)(2,1)S(1)}, u32[]{:S(2)}) copy-start(bf16[4,15,16,128]{3,2,1,0:T(8,128)(2,1)S(1)} %collective-permute-done.4.g2) | copy-start | bytes 737284
  51.5 6.5 %collective-permute-start.8 = (bf16[4,15,16,128]{3,2,1,0:T(8,128)(2,1)S(1)}, bf16[4,15,16,128]{3,2,1,0:T(8,128)(2,1)S(1)}, u32[]{:S(2)}, u32[]{:S(2)}) collective-permute-start(bf16[4,15,16,128]{3,2,1,0:T(8,128)(2,1)S(1)} %collective-permute-done.4.g2), channel_id=1, source_target_pairs={{0,2},{2,0},{4,6},{6,4},{8,10},{10,8},{12,14},{14,12},{16,18},{18,... | collective-permute-start | bytes 737288 | tf_op jit(solution)/shard_map/ppermute | solution.py:554
  58.0 1.5 copy-start.102
  58.0 1.5 collective-permute-start.9
  76.9 67.2 %copy-start.79 = (f32[16,256]{1,0:T(8,128)S(1)}, f32[16,256]{1,0:T(8,128)}, u32[]{:S(2)}) copy-start(f32[16,256]{1,0:T(8,128)} %vector_first.1) | copy-start | bytes 49156
  76.9 67.2 %copy-start.81 = (f32[16,256]{1,0:T(8,128)S(1)}, f32[16,256]{1,0:T(8,128)}, u32[]{:S(2)}) copy-start(f32[16,256]{1,0:T(8,128)} %vector_second.1) | copy-start | bytes 49156
  83.0 41.6 %all-to-all-start.11 = ((bf16[32,200,128]{2,1,0:T(8,128)(2,1)}), bf16[32,200,128]{2,1,0:T(8,128)(2,1)S(1)}, u32[]{:S(2)}, u32[]{:S(2)}) async-start(bf16[32,200,128]{2,1,0:T(8,128)(2,1)} %get-tuple-element.330), calls=%async_computation.11 | async-start | bytes 3276800 | tf_op jit(solution)/shard_map/all_to_all | solution.py:1616
  128.6 15.5 %all-to-all-start.12 = ((bf16[32,40,128]{2,1,0:T(8,128)(2,1)}), bf16[32,40,128]{2,1,0:T(8,128)(2,1)S(1)}, u32[]{:S(2)}, u32[]{:S(2)}) async-start(bf16[32,40,128]{2,1,0:T(8,128)(2,1)} %get-tuple-element.331), calls=%async_computation.12 | async-start | bytes 655360 | tf_op jit(solution)/shard_map/all_to_all | solution.py:1616
  132.4 18.7 %collective-permute-start.10 = (bf16[17,64,256]{2,1,0:T(8,128)(2,1)S(1)}, bf16[17,64,256]{2,1,0:T(8,128)(2,1)S(1)}, u32[]{:S(2)}, u32[]{:S(2)}) collective-permute-start(bf16[17,64,256]{2,1,0:T(8,128)(2,1)S(1)} %get-tuple-element.332.own), channel_id=1, source_target_pairs={{0,1},{1,0},{2,3},{3,2},{4,5},{5,4},{6,7},{7,6},{8,9},{9,8},{10,11... | collective-permute-start | bytes 1671176 | tf_op jit(solution)/shard_map/ppermute | solution.py:1639
